TPU v7x, 256 devices: a whole 4x4x8 slice. The times are simulated.
256 devices in a mesh: row: 128 (over z_lo, y, x, core), pair: 2 (over z_hi).
Axes of the slice: x: 4, y: 4, z: 8 (z_hi: 2, z_lo: 4; z = z_hi * 4 + z_lo), core: 2. Of those that a mesh axis runs over, the one named last changes fastest.
Arguments:
- slab: float32 [524288, 512], P('row', 'pair'), may hold values from -260 to 260, as said below
- block_ids: int32 [4], P('pair'), may hold values from 0 to 3, each once
Outputs:
- new_slab: float32 [524288, 512], P('row', 'pair')
- col_norms: float32 [512], P('pair')
- new_ids: int32 [4], P('pair')
Inputs may be any that keep to these rules, and one draw needn't show every extreme that they name: `slab`: finite values; within each pair the columns have distinct scales.
All inputs are finite; a program needn't handle non-finite values.
Results may differ from a plain program's by a relative error of at most 0.0003.
Values sent between devices are 32-bit elements; how exact they have to be, the bound alone decides.
No kernel may reach another device: no remote copies, remote signals or barrier semaphores. Data moves between devices by JAX's collectives and lax.ppermute only.
A program may use at most 64 MiB of HBM per device.

v0:
```python
import jax
import jax.numpy as jnp
import numpy as np
from jax import lax
from jax.sharding import PartitionSpec as P

ROUNDS = 48


def passed_along(array, axis, by):
    length = lax.axis_size(axis)
    return lax.ppermute(array, axis, [(i, (i + by) % length) for i in range(length)])


def cyclic_tables(width, count):
    partner = np.zeros((count, width), np.int32)
    first_flag = np.zeros((count, width), np.int32)
    for step in range(count):
        for k in range(width // 2):
            if k == 0:
                first, second = (step, width - 1)
            else:
                first, second = ((step + k) % (width - 1), (step - k) % (width - 1))
            partner[step, first] = second
            partner[step, second] = first
            first_flag[step, first] = 1
    return (jnp.asarray(partner), jnp.asarray(first_flag))


def jacobi_rounds(gram, count):
    width = gram.shape[0]
    partner_tab, first_tab = cyclic_tables(width, count)
    columns = lax.broadcasted_iota(jnp.int32, (width, width), 1)
    rows_iota = lax.broadcasted_iota(jnp.int32, (width, width), 0)
    on_diag = rows_iota == columns

    def one_round(step, state):
        mat, rot = state
        partner = partner_tab[step]
        is_first = first_tab[step] > 0
        pick = partner[:, None] == columns
        picked = jnp.where(pick, mat, jnp.zeros_like(mat))
        diag = jnp.diagonal(mat)
        row_part = jnp.sum(picked, axis=1)
        col_part = jnp.sum(picked, axis=0)
        other = jnp.sum(jnp.where(pick, diag[None, :], jnp.zeros_like(mat)), axis=1)
        gpq = jnp.where(is_first, row_part, col_part)
        gpp = jnp.where(is_first, diag, other)
        gqq = jnp.where(is_first, other, diag)
        diff = gqq - gpp
        sgn = jnp.where(diff >= 0, 1.0, -1.0).astype(mat.dtype)
        den = jnp.abs(diff) + jnp.sqrt(diff * diff + 4.0 * gpq * gpq)
        tang = jnp.where(den > 0, 2.0 * gpq * sgn / jnp.where(den > 0, den, 1.0), 0.0)
        cosv = 1.0 / jnp.sqrt(1.0 + tang * tang)
        sinv = tang * cosv
        offset = jnp.where(is_first, -sinv, sinv)
        rotation = jnp.where(
            on_diag, cosv[None, :], jnp.where(pick, offset[None, :], jnp.zeros_like(mat))
        )
        left = jnp.dot(
            rotation.T, mat, precision=lax.Precision.HIGHEST, preferred_element_type=mat.dtype
        )
        mat = jnp.dot(
            left, rotation, precision=lax.Precision.HIGHEST, preferred_element_type=mat.dtype
        )
        rot = jnp.dot(
            rot, rotation, precision=lax.Precision.HIGHEST, preferred_element_type=mat.dtype
        )
        return (mat, rot)

    start = (gram, jnp.eye(width, dtype=gram.dtype))
    return lax.fori_loop(0, count, one_round, start)


def per_device(slab, block_ids):
    rows_here, width = slab.shape
    block = width // 2
    local_gram = lax.dot_general(
        slab,
        slab,
        (((0,), (0,)), ((), ())),
        precision=lax.Precision.HIGHEST,
        preferred_element_type=jnp.float32,
    )
    gram = lax.psum(local_gram, "row")
    gram, rot = jacobi_rounds(gram, ROUNDS)
    second_leaves = block_ids[1] > block_ids[0]
    rot_leave = jnp.where(second_leaves, rot[:, block:], rot[:, :block])
    rot_stay = jnp.where(second_leaves, rot[:, :block], rot[:, block:])
    diag = jnp.diagonal(gram)
    leave_diag = jnp.where(second_leaves, diag[block:], diag[:block])
    leave_label = (
        jnp.where(second_leaves, block_ids[1], block_ids[0]).astype(jnp.float32).reshape(1)
    )
    stay_label = jnp.where(second_leaves, block_ids[0], block_ids[1])
    leaving = jnp.dot(
        slab, rot_leave, precision=lax.Precision.HIGHEST, preferred_element_type=jnp.float32
    )
    arrived, arrived_label, arrived_diag = passed_along(
        (leaving, leave_label, leave_diag), "pair", 1
    )
    staying = jnp.dot(
        slab, rot_stay, precision=lax.Precision.HIGHEST, preferred_element_type=jnp.float32
    )
    total_rows = rows_here * lax.axis_size("row")
    stay_sums, arrived_sums = lax.psum(
        (jnp.sum(staying * staying, axis=0), jnp.sum(arrived * arrived, axis=0)), "row"
    )
    col_norms = jnp.sqrt(jnp.concatenate([stay_sums, arrived_sums]) / total_rows)
    new_slab = jnp.concatenate([staying, arrived], axis=1)
    new_ids = jnp.stack([stay_label, arrived_label[0].astype(jnp.int32)])
    return (new_slab, col_norms, new_ids)


def solution(mesh):
    placed = (P("row", "pair"), P("pair"))
    return jax.shard_map(
        per_device,
        mesh=mesh,
        in_specs=placed,
        out_specs=(P("row", "pair"), P("pair"), P("pair")),
        check_vma=False,
    )
```

profile of v0, /device:TPU:1, one launch (start us, length us, event | category | flops | bytes accessed | tf_op | source)
XLA Modules:
  0.0 2062.7 jit_solution(2535742047432997580)
XLA Ops:
  7.2 10.9 fusion.45
  20.1 1173.0 %all-reduce.3.cloned.1.call-done = f32[256,256]{1,0:T(8,128)} async-done(((f32[256,256]{1,0:T(8,128)}), f32[256,256]{1,0:T(8,128)}) %all-reduce.3.cloned.1.call-update) | async-done | bytes 262160 | tf_op jit(solution)/shard_map/psum | solution.py:85
  1193.2 453.3 %while.17 = (s32[]{:T(128)}, f32[256,256]{1,0:T(8,128)}, f32[256,256]{0,1:T(8,128)S(1)}, s32[]{:T(128)}, s32[48,256]{1,0:T(8,128)}, /*index=5*/s32[48,256]{1,0:T(8,128)}) while((s32[]{:T(128)}, f32[256,256]{1,0:T(8,128)}, f32[256,256]{0,1:T(8,128)S(1)}, s32[]{:T(128)}, s32[48,256]{1,0:T(8,128)}, ...), condition=%wide.region_5.6_spmd.clone.clone, body=%wide.region_1.5_spmd.sunk.clone.clone.sunk | while | flops 605166592 | bytes 2391129 | solution.py:72
  1203.3 2.6 gather_fusion
  1212.8 2.6 gather_fusion
  1222.2 2.6 gather_fusion
  1231.7 2.6 gather_fusion
  1241.1 2.6 gather_fusion
  1250.6 2.6 gather_fusion
  1260.0 2.6 gather_fusion
  1278.9 2.6 gather_fusion
  1297.8 2.6 gather_fusion
  1316.7 2.6 gather_fusion
  1345.0 2.6 gather_fusion
  1363.9 2.6 gather_fusion
  1382.8 2.6 gather_fusion
  1401.7 2.6 gather_fusion
  1411.1 2.6 gather_fusion
  1646.5 7.8 convolution_bitcast_fusion.1
  1654.3 5.2 collective-permute-start
  1660.7 43.3 %collective-permute-start.1 = (f32[1]{0:T(128)}, f32[1]{0:T(128)}, u32[]{:S(2)}, u32[]{:S(2)}) collective-permute-start(f32[1]{0:T(128)} %bitcast.5), channel_id=1, source_target_pairs={{0,1},{1,0},{2,3},{3,2},{4,5},{5,4},{6,7},{7,6},{8,9},{9,8},{10,11... | collective-permute-start | bytes 20 | tf_op jit(solution)/shard_map/ppermute | solution.py:12
  1706.6 6.6 multiply_reduce_fusion.1
  1715.4 5.6 copy.8
  1721.2 334.1 %all-reduce = (f32[128]{0:T(128)S(1)}, f32[128]{0:T(128)S(1)}) all-reduce(f32[128]{0:T(128)S(1)} %multiply_reduce_fusion, f32[128]{0:T(128)S(1)} %get-tuple-element.178), channel_id=1, replica_groups=mesh['row'=128,'pair'=2] {'row'}, use_global_device_ids=true, to_apply=%region_9.10 | all-reduce | flops 256 | bytes 2048 | tf_op jit(solution)/shard_map/psum | solution.py:106
  (477 shorter events, 416.9 us)
Async XLA Ops:
  7.2 11.0 copy-start
  7.2 1186.0 %all-reduce.3.cloned.1.call-start = ((), (), s32[]{:S(2)}) async-start(), calls=%async_computation | async-start | bytes 524288 | tf_op jit(solution)/shard_map/psum | solution.py:85
  1654.3 58.9 %collective-permute-start = (f32[4096,128]{0,1:T(8,128)}, f32[4096,128]{0,1:T(8,128)S(1)}, u32[]{:S(2)}, u32[]{:S(2)}) collective-permute-start(f32[4096,128]{0,1:T(8,128)} %convolution_bitcast_fusion.1), channel_id=1, source_target_pairs={{0,1},{1,0},{2,3},{3,2},{4,5},{5,4},{6,7},{7,6},{8,9},{9,8},{10,11... | collective-permute-start | bytes 6291464 | tf_op jit(solution)/shard_map/ppermute | solution.py:12
  1660.7 44.6 %collective-permute-start.1 = (f32[1]{0:T(128)}, f32[1]{0:T(128)}, u32[]{:S(2)}, u32[]{:S(2)}) collective-permute-start(f32[1]{0:T(128)} %bitcast.5), channel_id=1, source_target_pairs={{0,1},{1,0},{2,3},{3,2},{4,5},{5,4},{6,7},{7,6},{8,9},{9,8},{10,11... | collective-permute-start | bytes 20 | tf_op jit(solution)/shard_map/ppermute | solution.py:12
Sparse Core Ops, SparseCore 0:
  18.3 1174.8 all-reduce.2
where the time goes:
time: 2070 us; the launch traced here: 2060 us
  waiting for transfers between devices  1170 us (57%)
  blocking collectives  334 us (16%)
  matrix products  192 us (9%)
  local copies, waits for them, and re-layouts  164 us (8%)
  other arithmetic  130 us (6%)
  starting transfers between devices  48.5 us (2%)
    psum x1, waiting for transfers between devices, per_device(): gram = lax.psum(local_gram, 'row')  1170 us
    psum x1, blocking collectives, per_device(): lax.psum((jnp.sum(staying * staying, axis=0), jnp.sum(arrived * arrived,...  334 us
    gather x48, local copies, waits for them, and re-layouts, one_round(): diag = jnp.diagonal(mat)  123 us
    dot_general x48, matrix products, one_round(): jnp.dot(rotation.T, mat, precision=lax.Precision.HIGHEST, preferred_eleme...  77.7 us
    reduce_sum x48, other arithmetic, one_round(): col_part = jnp.sum(picked, axis=0)  57 us
    dot_general x48, matrix products, one_round(): jnp.dot(left, rotation, precision=lax.Precision.HIGHEST, preferred_elemen...  56.6 us
    ppermute x2, starting transfers between devices, passed_along(): lax.ppermute(array, axis, [(i, (i + by) % length) for i in range(length)])  48.5 us
  transfers between devices with their start and end apart: 3, of which 1 were waited for; matrix products, arithmetic and copies ran while one was open for 0% of the time, Pallas kernels for 0%

commit v1 on v0

v1 whole, which is shorter than its diff:
```python
import functools

import jax
import jax.numpy as jnp
from jax import lax
from jax.experimental import pallas as pl
from jax.experimental.pallas import tpu as pltpu
from jax.sharding import PartitionSpec as P

ROUNDS = 48
BLOCK = 128
WIDTH = 256
F32 = jnp.float32
BF16 = jnp.bfloat16
HIGHEST = lax.Precision.HIGHEST
VMEM_LIMIT = 32 * 1024 * 1024


def product(a, b):
    return jnp.dot(a, b, preferred_element_type=F32)


def product_over_rows(a, b):
    return lax.dot_general(a, b, (((0,), (0,)), ((), ())), preferred_element_type=F32)


def gram_kernel(x_ref, out_ref, even, odd):
    step = pl.program_id(0)

    @pl.when(step == 0)
    def _():
        even[...] = jnp.zeros_like(even)
        odd[...] = jnp.zeros_like(odd)

    x = x_ref[...]
    high = x.astype(BF16)
    rest = x - high.astype(F32)
    mid = rest.astype(BF16)
    low = (rest - mid.astype(F32)).astype(BF16)
    even[...] += product_over_rows(high, high) + product_over_rows(mid, mid)
    odd[...] += product_over_rows(high, mid) + product_over_rows(high, low)

    @pl.when(step == pl.num_programs(0) - 1)
    def _():
        gram = even[...] + odd[...] + odd[...].T
        out_ref[0:128, :] = gram[0:128, 0:128]
        out_ref[128:256, :] = gram[0:128, 128:256]
        out_ref[256:384, :] = gram[128:256, 128:256]


def local_gram(slab, rows=1024):
    return pl.pallas_call(
        gram_kernel,
        grid=(slab.shape[0] // rows,),
        in_specs=[pl.BlockSpec((rows, WIDTH), lambda i: (i, 0))],
        out_specs=pl.BlockSpec((3 * BLOCK, BLOCK), lambda i: (0, 0)),
        out_shape=jax.ShapeDtypeStruct((3 * BLOCK, BLOCK), F32),
        scratch_shapes=[pltpu.VMEM((WIDTH, WIDTH), F32), pltpu.VMEM((WIDTH, WIDTH), F32)],
        compiler_params=pltpu.CompilerParams(vmem_limit_bytes=VMEM_LIMIT),
    )(slab)


def exchanged(array, mask):
    return lax.ppermute(array, "row", [(i, i ^ mask) for i in range(128)])


def row_part(array, index, rows):
    return lax.dynamic_slice_in_dim(array, index * rows, rows, 0)


def summed_over_four(mine, shift):
    got = [exchanged(mine, d << shift) for d in (1, 2, 3)]
    return (mine + got[1]) + (got[0] + got[2])


def summed_over_rows(part):
    me = lax.axis_index("row")
    core, x = me & 1, (me >> 1) & 3
    half = part.shape[0] // 2
    quarter = half // 4
    total = row_part(part, core, half) + exchanged(row_part(part, 1 - core, half), 1)
    got = [exchanged(row_part(total, x ^ d, quarter), d << 1) for d in (1, 2, 3)]
    total = (row_part(total, x, quarter) + got[1]) + (got[0] + got[2])
    total = summed_over_four(total, 3)
    total = summed_over_four(total, 5)
    parts = jnp.stack([total] + [exchanged(total, d << 1) for d in (1, 2, 3)])
    total = jnp.concatenate([lax.dynamic_index_in_dim(parts, x ^ j, 0, False) for j in range(4)])
    other = exchanged(total, 1)
    return jnp.where(
        core == 0, jnp.concatenate([total, other]), jnp.concatenate([other, total])
    )


def angles(g, d_top, d_bot):
    diff = d_bot - d_top
    sgn = jnp.where(diff >= 0, 1.0, -1.0)
    den = jnp.abs(diff) + jnp.sqrt(diff * diff + 4.0 * g * g)
    tang = jnp.where(den > 0, 2.0 * g * sgn / jnp.where(den > 0, den, 1.0), 0.0)
    cosv = 1.0 / jnp.sqrt(1.0 + tang * tang)
    return tang, cosv, tang * cosv

def jacobi_kernel(rounds, swap_ref, gram_ref, leave_ref, stay_ref, diag_ref, vt, vb, wt, wb):
    half = 128
    lane = lax.broadcasted_iota(jnp.int32, (8, half), 1)
    first, last = lane == 0, lane == half - 1
    row = lax.broadcasted_iota(jnp.int32, (2 * half, half), 0)
    col = lax.broadcasted_iota(jnp.int32, (2 * half, half), 1)
    vt[...] = (row == col).astype(F32)
    vb[...] = (row == 255 - col).astype(F32)
    a, b, c = gram_ref[0:128, :], gram_ref[128:256, :], gram_ref[256:384, :]
    rev = (row[:half] == half - 1 - col[:half]).astype(F32)
    wt[0:128, :] = a
    wt[128:256, :] = b.T
    wb[0:128, :] = jnp.dot(b, rev, precision=HIGHEST, preferred_element_type=F32)
    wb[128:256, :] = jnp.dot(c, rev, precision=HIGHEST, preferred_element_type=F32)
    eye = row[:half] == col[:half]
    d_top = jnp.sum(jnp.where(eye, wt[0:128, :], 0.0), axis=0, keepdims=True)
    anti = row[:half] == half - 1 - col[:half]
    d_bot = jnp.sum(jnp.where(anti, wb[128:256, :], 0.0), axis=0, keepdims=True)
    g = (jnp.sum(jnp.where(eye, wb[0:128, :], 0.0), axis=0, keepdims=True))
    d_top, d_bot, g = (jnp.broadcast_to(v, (8, half)) for v in (d_top, d_bot, g))

    def shifted(top, bot):
        new_top = jnp.where(last, bot, pltpu.roll(top, half - 1, 1))
        new_bot = jnp.where(first, bot, pltpu.roll(jnp.where(first, top, bot), 1, 1))
        return new_top, new_bot

    def one_round(_, state):
        g, d_top, d_bot = state
        t, c, s = angles(g, d_top, d_bot)
        d_top, d_bot = shifted(d_top - t * g, d_bot + t * g)
        acc = [jnp.zeros((8, half), F32) for _ in range(4)]
        for k in range(32):
            sl = pl.ds(8 * k, 8)
            a, b = vt[sl, :], vb[sl, :]
            nvt, nvb = shifted(c * a - s * b, s * a + c * b)
            vt[sl, :] = nvt
            vb[sl, :] = nvb
            a, b = wt[sl, :], wb[sl, :]
            nwt, nwb = shifted(c * a - s * b, s * a + c * b)
            wt[sl, :] = nwt
            wb[sl, :] = nwb
            acc[k % 4] = acc[k % 4] + nvt * nwb
        g = jnp.sum((acc[0] + acc[1]) + (acc[2] + acc[3]), axis=0, keepdims=True)
        return jnp.broadcast_to(g, (8, half)), d_top, d_bot

    g, d_top, d_bot = lax.fori_loop(0, rounds, one_round, (g, d_top, d_bot))
    swap = swap_ref[0]
    r = lax.broadcasted_iota(jnp.int32, (half, 2 * half), 0)
    j = lax.broadcasted_iota(jnp.int32, (half, 2 * half), 1)
    idx = jnp.where(swap > 0, jnp.where(j >= half, j - half, j + half), j)
    p_top = (r + rounds == idx).astype(F32)
    back = rounds - idx
    back = jnp.where(idx == 2 * half - 1, 0, jnp.where(back <= 0, back + 255, back))
    p_bot = ((r == back) & ((idx < rounds) | (idx >= rounds + half))).astype(F32)
    dot = functools.partial(jnp.dot, precision=HIGHEST, preferred_element_type=F32)
    rot = dot(vt[...], p_top) + dot(vb[...], p_bot)
    high = rot.astype(BF16)
    low = (rot - high.astype(F32)).astype(BF16)
    stay_ref[:, 0:128] = high[:, 0:128]
    stay_ref[:, 128:256] = low[:, 0:128]
    leave_ref[:, 0:128] = high[:, 128:256]
    leave_ref[:, 128:256] = low[:, 128:256]
    diag_ref[...] = dot(d_top, p_top) + dot(d_bot, p_bot)

def jacobi(gram, swap):
    in_vmem = pl.BlockSpec(memory_space=pltpu.VMEM)
    return pl.pallas_call(
        functools.partial(jacobi_kernel, ROUNDS),
        in_specs=[pl.BlockSpec(memory_space=pltpu.SMEM), in_vmem],
        out_specs=(in_vmem, in_vmem, in_vmem),
        out_shape=(
            jax.ShapeDtypeStruct((WIDTH, WIDTH), BF16),
            jax.ShapeDtypeStruct((WIDTH, WIDTH), BF16),
            jax.ShapeDtypeStruct((8, WIDTH), F32),
        ),
        scratch_shapes=[pltpu.VMEM((WIDTH, BLOCK), F32)] * 4,
        compiler_params=pltpu.CompilerParams(vmem_limit_bytes=VMEM_LIMIT),
    )(swap, gram)


def rotate_kernel(x_ref, rot_ref, out_ref):
    x = x_ref[...]
    high = x.astype(BF16)
    low = (x - high.astype(F32)).astype(BF16)
    both = product(high, rot_ref[...])
    out_ref[...] = (both[:, 0:128] + both[:, 128:256]) + product(low, rot_ref[:, 0:128])


def rotated(slab, rot, columns, rows=1024):
    count = slab.shape[0]
    return pl.pallas_call(
        rotate_kernel,
        grid=(count // rows,),
        in_specs=[
            pl.BlockSpec((rows, WIDTH), lambda i: (i, 0)),
            pl.BlockSpec((WIDTH, WIDTH), lambda i: (0, 0)),
        ],
        out_specs=pl.BlockSpec((rows, BLOCK), lambda i: (i, 0)),
        out_shape=jax.ShapeDtypeStruct((count, columns), F32),
        compiler_params=pltpu.CompilerParams(vmem_limit_bytes=VMEM_LIMIT),
        cost_estimate=pl.CostEstimate(
            flops=6 * count * WIDTH * BLOCK, bytes_accessed=6 * count * WIDTH, transcendentals=0
        ),
    )(slab, rot)


def passed_along(array):
    return lax.ppermute(array, "pair", [(0, 1), (1, 0)])


def per_device(slab, block_ids):
    swap = (block_ids[1] <= block_ids[0]).astype(jnp.int32)
    stay_label = jnp.where(swap > 0, block_ids[1], block_ids[0])
    leave_label = jnp.where(swap > 0, block_ids[0], block_ids[1])
    gram = summed_over_rows(local_gram(slab))
    rot_leave, rot_stay, diag = jacobi(gram, swap.reshape(1))
    diag = diag[0]
    note = jnp.concatenate([diag[BLOCK:], jnp.full((BLOCK,), leave_label.astype(F32))])
    note = passed_along(note)
    leaving, note = lax.optimization_barrier((rotated(slab, rot_leave, BLOCK), note))
    arrived = passed_along(leaving)
    new_slab = rotated(slab, rot_stay, WIDTH)
    new_slab = lax.dynamic_update_slice(new_slab, arrived, (0, BLOCK))
    total_rows = slab.shape[0] * lax.axis_size("row")
    squares = jnp.concatenate([diag[:BLOCK], note[:BLOCK]])
    col_norms = jnp.sqrt(jnp.maximum(squares, 0.0) / total_rows)
    new_ids = jnp.stack([stay_label, note[BLOCK].astype(jnp.int32)])
    return (new_slab, col_norms, new_ids)


def solution(mesh):
    return jax.shard_map(
        per_device,
        mesh=mesh,
        in_specs=(P("row", "pair"), P("pair")),
        out_specs=(P("row", "pair"), P("pair"), P("pair")),
        check_vma=False,
    )
```

time: 2070 us -> 167 us (0.08)
  the two profiles are of different devices: /device:TPU:1 before, /device:TPU:56 now
where the time goes in v1:
time: 167 us; the launch traced here: 164 us
  waiting for transfers between devices  99.7 us (60%)
  starting transfers between devices  26.2 us (16%)
  Pallas kernels  20.6 us (12%)
  local copies, waits for them, and re-layouts  10.8 us (6%)
  between operations  5.45 us (3%)
    ppermute x2, waiting for transfers between devices, passed_along(): return lax.ppermute(array, 'pair', [(0, 1), (1, 0)])  84.5 us
    ppermute x14, starting transfers between devices, exchanged(): return lax.ppermute(array, 'row', [(i, i ^ mask) for i in range(128)])  18.2 us
    ppermute x14, waiting for transfers between devices, exchanged(): return lax.ppermute(array, 'row', [(i, i ^ mask) for i in range(128)])  15.2 us
    pallas_call x1, Pallas kernels, jacobi(): pl.pallas_call(functools.partial(jacobi_kernel, ROUNDS), in_specs=[pl.Blo...  12.6 us
    ppermute x2, starting transfers between devices, passed_along(): return lax.ppermute(array, 'pair', [(0, 1), (1, 0)])  8.02 us
    unnamed x16, local copies, waits for them, and re-layouts  6.64 us
    pallas_call x2, Pallas kernels, rotated(): pl.pallas_call(rotate_kernel, grid=(count // rows,), in_specs=[pl.BlockSp...  4.79 us
  transfers between devices with their start and end apart: 16, of which 10 were waited for; matrix products, arithmetic and copies ran while one was open for 1% of the time, Pallas kernels for 3%

profile of v1, /device:TPU:56, one launch (start us, length us, event | category | flops | bytes accessed | tf_op | source)
XLA Modules:
  0.0 164.2 jit_solution(12098805534009637746)
XLA Ops:
  0.7 2.2 %copy-done = f32[4096,256]{1,0:T(8,128)S(1)} copy-done((f32[4096,256]{1,0:T(8,128)S(1)}, f32[4096,256]{1,0:T(8,128)}, u32[]{:S(2)}) %copy-start) | copy-done | bytes 4194328
  2.8 3.2 %shard_map.49 = f32[384,128]{1,0:T(8,128)S(1)} custom-call(f32[4096,256]{1,0:T(8,128)S(1)} %copy-done), custom_call_target="tpu_custom_call" | custom-call | tf_op jit(solution)/shard_map/pallas_call | solution.py:52
  6.2 1.3 collective-permute-done
  7.5 3.1 %collective-permute-start.1 = (f32[48,128]{1,0:T(8,128)S(1)}, f32[48,128]{1,0:T(8,128)S(1)}, u32[]{:S(2)}, u32[]{:S(2)}) collective-permute-start(f32[48,128]{1,0:T(8,128)S(1)} %get-tuple-element.23), channel_id=1, source_target_pairs={{0,8},{2,10},{4,12},{6,14},{8,0},{10,2},{12,4},{14,6},{16,24},{18,... | collective-permute-start | bytes 73736 | tf_op jit(solution)/shard_map/ppermute | solution.py:64
  11.8 1.2 collective-permute-done.1
  12.9 2.7 %collective-permute-done.3 = f32[48,128]{1,0:T(8,128)S(1)} collective-permute-done((f32[48,128]{1,0:T(8,128)S(1)}, f32[48,128]{1,0:T(8,128)S(1)}, u32[]{:S(2)}, u32[]{:S(2)}) %collective-permute-start.3) | collective-permute-done | bytes 24608 | tf_op jit(solution)/shard_map/ppermute | solution.py:64
  17.0 3.5 %collective-permute-start.4 = (f32[48,128]{1,0:T(8,128)S(1)}, f32[48,128]{1,0:T(8,128)S(1)}, u32[]{:S(2)}, u32[]{:S(2)}) collective-permute-start(f32[48,128]{1,0:T(8,128)S(1)} %add_add_fusion.2), channel_id=1, source_target_pairs={{0,32},{2,34},{4,36},{6,38},{8,40},{10,42},{12,44},{14,46},{16,48}... | collective-permute-start | bytes 73736 | tf_op jit(solution)/shard_map/ppermute | solution.py:64
  20.8 1.7 %collective-permute-done.4 = f32[48,128]{1,0:T(8,128)S(1)} collective-permute-done((f32[48,128]{1,0:T(8,128)S(1)}, f32[48,128]{1,0:T(8,128)S(1)}, u32[]{:S(2)}, u32[]{:S(2)}) %collective-permute-start.4) | collective-permute-done | bytes 24608 | tf_op jit(solution)/shard_map/ppermute | solution.py:64
  22.6 2.0 %collective-permute-start.9 = (f32[48,128]{1,0:T(8,128)S(1)}, f32[48,128]{1,0:T(8,128)S(1)}, u32[]{:S(2)}, u32[]{:S(2)}) collective-permute-start(f32[48,128]{1,0:T(8,128)S(1)} %add_add_fusion.1), channel_id=1, source_target_pairs={{0,192},{2,194},{4,196},{6,198},{8,200},{10,202},{12,204},{14,206}... | collective-permute-start | bytes 73736 | tf_op jit(solution)/shard_map/ppermute | solution.py:64
  24.5 2.8 %collective-permute-start.8 = (f32[48,128]{1,0:T(8,128)S(1)}, f32[48,128]{1,0:T(8,128)S(1)}, u32[]{:S(2)}, u32[]{:S(2)}) collective-permute-start(f32[48,128]{1,0:T(8,128)S(1)} %add_add_fusion.1), channel_id=1, source_target_pairs={{0,64},{2,66},{4,68},{6,70},{8,72},{10,74},{12,76},{14,78},{16,80}... | collective-permute-start | bytes 73736 | tf_op jit(solution)/shard_map/ppermute | solution.py:64
  27.4 2.1 %collective-permute-done.8 = f32[48,128]{1,0:T(8,128)S(1)} collective-permute-done((f32[48,128]{1,0:T(8,128)S(1)}, f32[48,128]{1,0:T(8,128)S(1)}, u32[]{:S(2)}, u32[]{:S(2)}) %collective-permute-start.8) | collective-permute-done | bytes 24608 | tf_op jit(solution)/shard_map/ppermute | solution.py:64
  29.4 2.7 %collective-permute-done.7 = f32[48,128]{1,0:T(8,128)S(1)} collective-permute-done((f32[48,128]{1,0:T(8,128)S(1)}, f32[48,128]{1,0:T(8,128)S(1)}, u32[]{:S(2)}, u32[]{:S(2)}) %collective-permute-start.7) | collective-permute-done | bytes 24608 | tf_op jit(solution)/shard_map/ppermute | solution.py:64
  32.1 2.1 %collective-permute-start.12 = (f32[48,128]{1,0:T(8,128)S(1)}, f32[48,128]{1,0:T(8,128)S(1)}, u32[]{:S(2)}, u32[]{:S(2)}) collective-permute-start(f32[48,128]{1,0:T(8,128)S(1)} %add_add_fusion), channel_id=1, source_target_pairs={{0,12},{2,14},{4,8},{6,10},{8,4},{10,6},{12,0},{14,2},{16,28},{18,... | collective-permute-start | bytes 73736 | tf_op jit(solution)/shard_map/ppermute | solution.py:64
  34.2 2.1 %collective-permute-start.10 = (f32[48,128]{1,0:T(8,128)S(1)}, f32[48,128]{1,0:T(8,128)S(1)}, u32[]{:S(2)}, u32[]{:S(2)}) collective-permute-start(f32[48,128]{1,0:T(8,128)S(1)} %add_add_fusion), channel_id=1, source_target_pairs={{0,4},{2,6},{4,0},{6,2},{8,12},{10,14},{12,8},{14,10},{16,20},{18,... | collective-permute-start | bytes 73736 | tf_op jit(solution)/shard_map/ppermute | solution.py:64
  37.2 2.3 %collective-permute-done.11 = f32[48,128]{1,0:T(8,128)S(1)} collective-permute-done((f32[48,128]{1,0:T(8,128)S(1)}, f32[48,128]{1,0:T(8,128)S(1)}, u32[]{:S(2)}, u32[]{:S(2)}) %collective-permute-start.11) | collective-permute-done | bytes 24608 | tf_op jit(solution)/shard_map/ppermute | solution.py:64
  43.1 12.6 %shard_map.50 = (bf16[256,256]{1,0:T(8,128)(2,1)S(1)}, bf16[256,256]{1,0:T(8,128)(2,1)S(1)}, f32[8,256]{1,0:T(8,128)S(1)}) custom-call(s32[1]{0:T(128)} %bitcast.2.swap_ref, f32[384,128]{1,0:T(8,128)S(1)} %broadcast_select_fusion.gram_ref), custom_call_target="tpu_custom_call" | custom-call | tf_op jit(solution)/shard_map/pallas_call | solution.py:168
  55.7 4.6 %collective-permute-start.14 = (f32[256]{0:T(256)S(1)}, f32[256]{0:T(256)S(1)}, u32[]{:S(2)}, u32[]{:S(2)}) collective-permute-start(f32[256]{0:T(256)S(1)} %concatenate.20), channel_id=1, source_target_pairs={{0,1},{1,0},{2,3},{3,2},{4,5},{5,4},{6,7},{7,6},{8,9},{9,8},{10,11... | collective-permute-start | bytes 3080 | tf_op jit(solution)/shard_map/ppermute | solution.py:209
  60.3 2.2 %copy-done.1 = f32[4096,256]{1,0:T(8,128)S(1)} copy-done((f32[4096,256]{1,0:T(8,128)S(1)}, f32[4096,256]{1,0:T(8,128)}, u32[]{:S(2)}) %copy-start.1) | copy-done | bytes 4194328
  62.5 1.8 %shard_map.52 = f32[4096,128]{1,0:T(8,128)S(1)} custom-call(f32[4096,256]{1,0:T(8,128)S(1)} %copy-done.1, bf16[256,256]{1,0:T(8,128)(2,1)S(1)} %get-tuple-element.9.rot_ref), custom_call_target="tpu_custom_call" | custom-call | flops 805306368 | bytes 6291456 | tf_op jit(solution)/shard_map/pallas_call | solution.py:192
  64.3 3.4 %collective-permute-start.15 = (f32[4096,128]{1,0:T(8,128)S(1)}, f32[4096,128]{1,0:T(8,128)}, u32[]{:S(2)}, u32[]{:S(2)}) collective-permute-start(f32[4096,128]{1,0:T(8,128)S(1)} %shard_map.52), channel_id=1, source_target_pairs={{0,1},{1,0},{2,3},{3,2},{4,5},{5,4},{6,7},{7,6},{8,9},{9,8},{10,11... | collective-permute-start | bytes 6291464 | tf_op jit(solution)/shard_map/ppermute | solution.py:209
  69.1 2.2 %copy-done.2 = f32[4096,256]{1,0:T(8,128)S(1)} copy-done((f32[4096,256]{1,0:T(8,128)S(1)}, f32[4096,256]{1,0:T(8,128)}, u32[]{:S(2)}) %copy-start.2) | copy-done | bytes 4194328
  71.3 3.0 %shard_map.51 = f32[4096,256]{1,0:T(8,128)} custom-call(f32[4096,256]{1,0:T(8,128)S(1)} %copy-done.2, bf16[256,256]{1,0:T(8,128)(2,1)S(1)} %get-tuple-element.8.rot_ref), custom_call_target="tpu_custom_call" | custom-call | flops 805306368 | bytes 6291456 | tf_op jit(solution)/shard_map/pallas_call | solution.py:192
  76.6 84.5 %collective-permute-done.15 = f32[4096,128]{1,0:T(8,128)} collective-permute-done((f32[4096,128]{1,0:T(8,128)S(1)}, f32[4096,128]{1,0:T(8,128)}, u32[]{:S(2)}, u32[]{:S(2)}) %collective-permute-start.15) | collective-permute-done | bytes 2097184 | tf_op jit(solution)/shard_map/ppermute | solution.py:209
  161.1 3.0 %constant_dynamic-update-slice_fusion.10 = f32[4096,256]{1,0:T(8,128)} fusion(f32[4096,256]{1,0:T(8,128)} %shard_map.51, f32[4096,128]{1,0:T(8,128)} %collective-permute-done.15), kind=kLoop, calls=%fused_computation.21 | loop fusion | bytes 4194304 | tf_op jit(solution)/shard_map/dynamic_update_slice | solution.py:224
  (46 shorter events, 6.4 us)
Async XLA Ops:
  0.6 39.1 %copy-start.3 = (s32[2]{0:T(128)S(1)}, s32[2]{0:T(128)}, u32[]{:S(2)}) copy-start(s32[2]{0:T(128)} %param.3) | copy-start | bytes 28
  0.6 2.2 %copy-start = (f32[4096,256]{1,0:T(8,128)S(1)}, f32[4096,256]{1,0:T(8,128)}, u32[]{:S(2)}) copy-start(f32[4096,256]{1,0:T(8,128)} %x_ref.5) | copy-start | bytes 12582916
  6.1 1.4 collective-permute-start
  7.5 5.4 %collective-permute-start.1 = (f32[48,128]{1,0:T(8,128)S(1)}, f32[48,128]{1,0:T(8,128)S(1)}, u32[]{:S(2)}, u32[]{:S(2)}) collective-permute-start(f32[48,128]{1,0:T(8,128)S(1)} %get-tuple-element.23), channel_id=1, source_target_pairs={{0,8},{2,10},{4,12},{6,14},{8,0},{10,2},{12,4},{14,6},{16,24},{18,... | collective-permute-start | bytes 73736 | tf_op jit(solution)/shard_map/ppermute | solution.py:64
  10.6 5.0 %collective-permute-start.3 = (f32[48,128]{1,0:T(8,128)S(1)}, f32[48,128]{1,0:T(8,128)S(1)}, u32[]{:S(2)}, u32[]{:S(2)}) collective-permute-start(f32[48,128]{1,0:T(8,128)S(1)} %get-tuple-element.24), channel_id=1, source_target_pairs={{0,12},{2,14},{4,8},{6,10},{8,4},{10,6},{12,0},{14,2},{16,28},{18,... | collective-permute-start | bytes 73736 | tf_op jit(solution)/shard_map/ppermute | solution.py:64
  11.8 3.9 %collective-permute-start.2 = (f32[48,128]{1,0:T(8,128)S(1)}, f32[48,128]{1,0:T(8,128)S(1)}, u32[]{:S(2)}, u32[]{:S(2)}) collective-permute-start(f32[48,128]{1,0:T(8,128)S(1)} %get-tuple-element.25), channel_id=1, source_target_pairs={{0,4},{2,6},{4,0},{6,2},{8,12},{10,14},{12,8},{14,10},{16,20},{18,... | collective-permute-start | bytes 73736 | tf_op jit(solution)/shard_map/ppermute | solution.py:64
  15.7 5.1 %collective-permute-start.6 = (f32[48,128]{1,0:T(8,128)S(1)}, f32[48,128]{1,0:T(8,128)S(1)}, u32[]{:S(2)}, u32[]{:S(2)}) collective-permute-start(f32[48,128]{1,0:T(8,128)S(1)} %add_add_fusion.2), channel_id=1, source_target_pairs={{0,48},{2,50},{4,52},{6,54},{8,56},{10,58},{12,60},{14,62},{16,32}... | collective-permute-start | bytes 73736 | tf_op jit(solution)/shard_map/ppermute | solution.py:64
  16.0 4.8 %collective-permute-start.5 = (f32[48,128]{1,0:T(8,128)S(1)}, f32[48,128]{1,0:T(8,128)S(1)}, u32[]{:S(2)}, u32[]{:S(2)}) collective-permute-start(f32[48,128]{1,0:T(8,128)S(1)} %add_add_fusion.2), channel_id=1, source_target_pairs={{0,16},{2,18},{4,20},{6,22},{8,24},{10,26},{12,28},{14,30},{16,0},... | collective-permute-start | bytes 73736 | tf_op jit(solution)/shard_map/ppermute | solution.py:64
  17.0 5.6 %collective-permute-start.4 = (f32[48,128]{1,0:T(8,128)S(1)}, f32[48,128]{1,0:T(8,128)S(1)}, u32[]{:S(2)}, u32[]{:S(2)}) collective-permute-start(f32[48,128]{1,0:T(8,128)S(1)} %add_add_fusion.2), channel_id=1, source_target_pairs={{0,32},{2,34},{4,36},{6,38},{8,40},{10,42},{12,44},{14,46},{16,48}... | collective-permute-start | bytes 73736 | tf_op jit(solution)/shard_map/ppermute | solution.py:64
  22.6 4.8 %collective-permute-start.9 = (f32[48,128]{1,0:T(8,128)S(1)}, f32[48,128]{1,0:T(8,128)S(1)}, u32[]{:S(2)}, u32[]{:S(2)}) collective-permute-start(f32[48,128]{1,0:T(8,128)S(1)} %add_add_fusion.1), channel_id=1, source_target_pairs={{0,192},{2,194},{4,196},{6,198},{8,200},{10,202},{12,204},{14,206}... | collective-permute-start | bytes 73736 | tf_op jit(solution)/shard_map/ppermute | solution.py:64
  24.5 4.9 %collective-permute-start.8 = (f32[48,128]{1,0:T(8,128)S(1)}, f32[48,128]{1,0:T(8,128)S(1)}, u32[]{:S(2)}, u32[]{:S(2)}) collective-permute-start(f32[48,128]{1,0:T(8,128)S(1)} %add_add_fusion.1), channel_id=1, source_target_pairs={{0,64},{2,66},{4,68},{6,70},{8,72},{10,74},{12,76},{14,78},{16,80}... | collective-permute-start | bytes 73736 | tf_op jit(solution)/shard_map/ppermute | solution.py:64
  27.4 4.7 %collective-permute-start.7 = (f32[48,128]{1,0:T(8,128)S(1)}, f32[48,128]{1,0:T(8,128)S(1)}, u32[]{:S(2)}, u32[]{:S(2)}) collective-permute-start(f32[48,128]{1,0:T(8,128)S(1)} %add_add_fusion.1), channel_id=1, source_target_pairs={{0,128},{2,130},{4,132},{6,134},{8,136},{10,138},{12,140},{14,142}... | collective-permute-start | bytes 73736 | tf_op jit(solution)/shard_map/ppermute | solution.py:64
  32.1 5.1 %collective-permute-start.12 = (f32[48,128]{1,0:T(8,128)S(1)}, f32[48,128]{1,0:T(8,128)S(1)}, u32[]{:S(2)}, u32[]{:S(2)}) collective-permute-start(f32[48,128]{1,0:T(8,128)S(1)} %add_add_fusion), channel_id=1, source_target_pairs={{0,12},{2,14},{4,8},{6,10},{8,4},{10,6},{12,0},{14,2},{16,28},{18,... | collective-permute-start | bytes 73736 | tf_op jit(solution)/shard_map/ppermute | solution.py:64
  34.2 5.3 %collective-permute-start.11 = (f32[48,128]{1,0:T(8,128)S(1)}, f32[48,128]{1,0:T(8,128)S(1)}, u32[]{:S(2)}, u32[]{:S(2)}) collective-permute-start(f32[48,128]{1,0:T(8,128)S(1)} %add_add_fusion), channel_id=1, source_target_pairs={{0,8},{2,10},{4,12},{6,14},{8,0},{10,2},{12,4},{14,6},{16,24},{18,... | collective-permute-start | bytes 73736 | tf_op jit(solution)/shard_map/ppermute | solution.py:64
  34.2 5.3 %collective-permute-start.10 = (f32[48,128]{1,0:T(8,128)S(1)}, f32[48,128]{1,0:T(8,128)S(1)}, u32[]{:S(2)}, u32[]{:S(2)}) collective-permute-start(f32[48,128]{1,0:T(8,128)S(1)} %add_add_fusion), channel_id=1, source_target_pairs={{0,4},{2,6},{4,0},{6,2},{8,12},{10,14},{12,8},{14,10},{16,20},{18,... | collective-permute-start | bytes 73736 | tf_op jit(solution)/shard_map/ppermute | solution.py:64
  39.7 3.3 %collective-permute-start.13 = (f32[192,128]{1,0:T(8,128)S(1)}, f32[192,128]{1,0:T(8,128)S(1)}, u32[]{:S(2)}, u32[]{:S(2)}) collective-permute-start(f32[192,128]{1,0:T(8,128)S(1)} %pad_maximum_fusion.1), channel_id=1, source_target_pairs={{0,2},{2,0},{4,6},{6,4},{8,10},{10,8},{12,14},{14,12},{16,18},{18,... | collective-permute-start | bytes 294920 | tf_op jit(solution)/shard_map/ppermute | solution.py:64
  55.7 8.6 %collective-permute-start.14 = (f32[256]{0:T(256)S(1)}, f32[256]{0:T(256)S(1)}, u32[]{:S(2)}, u32[]{:S(2)}) collective-permute-start(f32[256]{0:T(256)S(1)} %concatenate.20), channel_id=1, source_target_pairs={{0,1},{1,0},{2,3},{3,2},{4,5},{5,4},{6,7},{7,6},{8,9},{9,8},{10,11... | collective-permute-start | bytes 3080 | tf_op jit(solution)/shard_map/ppermute | solution.py:209
  60.3 2.2 %copy-start.1 = (f32[4096,256]{1,0:T(8,128)S(1)}, f32[4096,256]{1,0:T(8,128)}, u32[]{:S(2)}) copy-start(f32[4096,256]{1,0:T(8,128)} %x_ref.5) | copy-start | bytes 12582916
  64.3 96.8 %collective-permute-start.15 = (f32[4096,128]{1,0:T(8,128)S(1)}, f32[4096,128]{1,0:T(8,128)}, u32[]{:S(2)}, u32[]{:S(2)}) collective-permute-start(f32[4096,128]{1,0:T(8,128)S(1)} %shard_map.52), channel_id=1, source_target_pairs={{0,1},{1,0},{2,3},{3,2},{4,5},{5,4},{6,7},{7,6},{8,9},{9,8},{10,11... | collective-permute-start | bytes 6291464 | tf_op jit(solution)/shard_map/ppermute | solution.py:209
  69.1 2.2 %copy-start.2 = (f32[4096,256]{1,0:T(8,128)S(1)}, f32[4096,256]{1,0:T(8,128)}, u32[]{:S(2)}) copy-start(f32[4096,256]{1,0:T(8,128)} %x_ref.5) | copy-start | bytes 12582916

commit v2 on v1

v2 whole, which is shorter than its diff:
```python
import functools

import jax
import jax.numpy as jnp
from jax import lax
from jax.experimental import pallas as pl
from jax.experimental.pallas import tpu as pltpu
from jax.sharding import PartitionSpec as P

ROUNDS = 48
BLOCK = 128
WIDTH = 256
F32 = jnp.float32
BF16 = jnp.bfloat16
HIGHEST = lax.Precision.HIGHEST
VMEM_LIMIT = 32 * 1024 * 1024
ROWS = 4096
RAW = 640
CHUNKS = (1024, 1792, ROWS - RAW - 2816)
EXTRA = 80
STEP = 128
PACKED = 272
PARTS = 4


def product(a, b):
    return jnp.dot(a, b, preferred_element_type=F32)


def product_over_rows(a, b):
    return lax.dot_general(a, b, (((0,), (0,)), ((), ())), preferred_element_type=F32)


def gram_kernel(slab_ref, out_ref, x_ref, even, odd, sems):
    rows = ROWS // PARTS
    parts = [pl.ds(n * rows, rows) for n in range(PARTS)]
    copies = [
        pltpu.make_async_copy(slab_ref.at[part, :], x_ref.at[part, :], sems.at[n])
        for n, part in enumerate(parts)
    ]
    for copy in copies:
        copy.start()
    for n, part in enumerate(parts):
        copies[n].wait()
        x = x_ref[part, :]
        high = x.astype(BF16)
        rest = x - high.astype(F32)
        mid = rest.astype(BF16)
        low = (rest - mid.astype(F32)).astype(BF16)
        same = product_over_rows(high, high) + product_over_rows(mid, mid)
        cross = product_over_rows(high, mid) + product_over_rows(high, low)
        even[...] = same if n == 0 else even[...] + same
        odd[...] = cross if n == 0 else odd[...] + cross
    gram = even[...] + odd[...] + odd[...].T
    row = lax.broadcasted_iota(jnp.int32, (BLOCK, BLOCK), 0)
    col = lax.broadcasted_iota(jnp.int32, (BLOCK, BLOCK), 1)
    last = gram[128:256, 128:256]
    out_ref[0:128, :] = jnp.where(row <= col, gram[0:128, 0:128], last)
    out_ref[128:256, :] = gram[0:128, 128:256]
    diag = jnp.sum(jnp.where(row == col, last, 0.0), axis=0, keepdims=True)
    out_ref[256:272, :] = jnp.broadcast_to(diag, (16, BLOCK))


def local_gram(slab):
    return pl.pallas_call(
        gram_kernel,
        in_specs=[pl.BlockSpec(memory_space=pl.ANY)],
        out_specs=pl.BlockSpec(memory_space=pltpu.VMEM),
        out_shape=jax.ShapeDtypeStruct((PACKED, BLOCK), F32),
        scratch_shapes=[
            pltpu.VMEM((ROWS, WIDTH), F32),
            pltpu.VMEM((WIDTH, WIDTH), F32),
            pltpu.VMEM((WIDTH, WIDTH), F32),
            pltpu.SemaphoreType.DMA((PARTS,)),
        ],
        compiler_params=pltpu.CompilerParams(vmem_limit_bytes=VMEM_LIMIT),
    )(pltpu.with_memory_space_constraint(slab, pltpu.HBM))


def place():
    me = lax.axis_index("row")
    return me & 1, (me >> 1) & 3


def exchanged(array, mask):
    return lax.ppermute(array, "row", [(i, i ^ mask) for i in range(128)])


def passed_along(array):
    return lax.ppermute(array, "pair", [(0, 1), (1, 0)])


def with_three_others(mine, shift):
    return [mine] + [exchanged(mine, d << shift) for d in (1, 2, 3)]


def summed_over_four(mine, shift):
    parts = with_three_others(mine, shift)
    return (parts[0] + parts[2]) + (parts[1] + parts[3])


def summed_over_rows(part, core, raw):
    half = part.shape[0] // 2
    mine = lax.dynamic_slice_in_dim(part, core * half, half, 0)
    yours = lax.dynamic_slice_in_dim(part, (1 - core) * half, half, 0)
    total = summed_over_four(mine + exchanged(yours, 1), 5)
    raw, total = lax.optimization_barrier((raw, total))
    raw_arrived = passed_along(raw)
    total = summed_over_four(summed_over_four(total, 1), 3)
    return (total, exchanged(total, 1)), raw_arrived


def angles(g, d_top, d_bot):
    diff = d_bot - d_top
    sgn = jnp.where(diff >= 0, 1.0, -1.0)
    den = jnp.abs(diff) + jnp.sqrt(diff * diff + 4.0 * g * g)
    tang = jnp.where(den > 0, 2.0 * g * sgn / jnp.where(den > 0, den, 1.0), 0.0)
    cosv = 1.0 / jnp.sqrt(1.0 + tang * tang)
    return tang, cosv, tang * cosv

def rounds_kernel(
    ids_ref, mine_ref, other_ref, slab_ref, first_ref, second_ref, third_ref, stay_ref, diag_ref,
    packed, vt, vb, wt, wb, leave, x_ref, sem,
):
    rounds = ROUNDS
    fetch = pltpu.make_async_copy(slab_ref.at[pl.ds(RAW, ROWS - RAW), :], x_ref, sem)
    fetch.start()
    core, x = place()
    swap = (ids_ref[1] <= ids_ref[0]).astype(jnp.int32)
    for h, part in enumerate((mine_ref, other_ref)):
        start = pl.multiple_of((core ^ h) * (PACKED // 2), 8)
        packed[pl.ds(start, PACKED // 2), :] = part[...]
    half = 128
    lane = lax.broadcasted_iota(jnp.int32, (8, half), 1)
    first, last = lane == 0, lane == half - 1
    row = lax.broadcasted_iota(jnp.int32, (2 * half, half), 0)
    col = lax.broadcasted_iota(jnp.int32, (2 * half, half), 1)
    vt[...] = (row == col).astype(F32)
    vb[...] = (row == 255 - col).astype(F32)
    both, b = packed[0:128, :], packed[128:256, :]
    mirrored = both.T
    above, below = row[:half] < col[:half], row[:half] > col[:half]
    a = jnp.where(below, mirrored, both)
    c = jnp.where(below, both, jnp.where(above, mirrored, packed[256:257, :]))
    rev = (row[:half] == half - 1 - col[:half]).astype(F32)
    wt[0:128, :] = a
    wt[128:256, :] = b.T
    wb[0:128, :] = jnp.dot(b, rev, precision=HIGHEST, preferred_element_type=F32)
    wb[128:256, :] = jnp.dot(c, rev, precision=HIGHEST, preferred_element_type=F32)
    eye = row[:half] == col[:half]
    d_top = jnp.sum(jnp.where(eye, wt[0:128, :], 0.0), axis=0, keepdims=True)
    anti = row[:half] == half - 1 - col[:half]
    d_bot = jnp.sum(jnp.where(anti, wb[128:256, :], 0.0), axis=0, keepdims=True)
    g = (jnp.sum(jnp.where(eye, wb[0:128, :], 0.0), axis=0, keepdims=True))
    d_top, d_bot, g = (jnp.broadcast_to(v, (8, half)) for v in (d_top, d_bot, g))

    def shifted(top, bot):
        new_top = jnp.where(last, bot, pltpu.roll(top, half - 1, 1))
        new_bot = jnp.where(first, bot, pltpu.roll(jnp.where(first, top, bot), 1, 1))
        return new_top, new_bot

    def one_round(_, state):
        g, d_top, d_bot = state
        t, c, s = angles(g, d_top, d_bot)
        d_top, d_bot = shifted(d_top - t * g, d_bot + t * g)
        acc = [jnp.zeros((8, half), F32) for _ in range(4)]
        for k in range(32):
            sl = pl.ds(8 * k, 8)
            a, b = vt[sl, :], vb[sl, :]
            nvt, nvb = shifted(c * a - s * b, s * a + c * b)
            vt[sl, :] = nvt
            vb[sl, :] = nvb
            a, b = wt[sl, :], wb[sl, :]
            nwt, nwb = shifted(c * a - s * b, s * a + c * b)
            wt[sl, :] = nwt
            wb[sl, :] = nwb
            acc[k % 4] = acc[k % 4] + nvt * nwb
        g = jnp.sum((acc[0] + acc[1]) + (acc[2] + acc[3]), axis=0, keepdims=True)
        return jnp.broadcast_to(g, (8, half)), d_top, d_bot

    g, d_top, d_bot = lax.fori_loop(0, rounds, one_round, (g, d_top, d_bot))
    r = lax.broadcasted_iota(jnp.int32, (half, 2 * half), 0)
    j = lax.broadcasted_iota(jnp.int32, (half, 2 * half), 1)
    idx = jnp.where(swap > 0, jnp.where(j >= half, j - half, j + half), j)
    p_top = (r + rounds == idx).astype(F32)
    back = rounds - idx
    back = jnp.where(idx == 2 * half - 1, 0, jnp.where(back <= 0, back + 255, back))
    p_bot = ((r == back) & ((idx < rounds) | (idx >= rounds + half))).astype(F32)
    dot = functools.partial(jnp.dot, precision=HIGHEST, preferred_element_type=F32)
    rot = dot(vt[...], p_top) + dot(vb[...], p_bot)
    high = rot.astype(BF16)
    low = (rot - high.astype(F32)).astype(BF16)
    stay_ref[:, 0:128] = high[:, 0:128]
    stay_ref[:, 128:256] = low[:, 0:128]
    leave[:, 0:128] = high[:, 128:256]
    leave[:, 128:256] = low[:, 128:256]
    diag = dot(d_top, p_top) + dot(d_bot, p_bot)
    diag_ref[...] = diag
    wt[...] = rot[:, 128:256]
    first_ref[CHUNKS[0] : CHUNKS[0] + 64, :] = wt[pl.ds(pl.multiple_of(x * 64, 64), 64), :]
    first_ref[CHUNKS[0] + 64 : CHUNKS[0] + 72, :] = diag[:, 128:256]
    first_ref[CHUNKS[0] + 72 : CHUNKS[0] + 80, :] = jnp.full((8, half), jnp.maximum(ids_ref[0], ids_ref[1]).astype(F32))
    fetch.wait()
    for n, out_ref in enumerate((first_ref, second_ref, third_ref)):
        base = sum(CHUNKS[:n])

        def one_step(k, _, out_ref=out_ref, base=base):
            start = pl.multiple_of(k * STEP, STEP)
            out_ref[pl.ds(start, STEP), :] = rotation(x_ref[pl.ds(base + start, STEP), :], leave[...])
            return 0

        lax.fori_loop(0, CHUNKS[n] // STEP, one_step, 0, unroll=2)


def rotation(x, rot):
    high = x.astype(BF16)
    low = (x - high.astype(F32)).astype(BF16)
    both = product(high, rot)
    return (both[:, 0:128] + both[:, 128:256]) + product(low, rot[:, 0:128])


def rounds_and_leaving(parts, slab, block_ids):
    in_vmem = pl.BlockSpec(memory_space=pltpu.VMEM)
    return pl.pallas_call(
        rounds_kernel,
        in_specs=[
            pl.BlockSpec(memory_space=pltpu.SMEM),
            in_vmem,
            in_vmem,
            pl.BlockSpec(memory_space=pl.ANY),
        ],
        out_specs=(in_vmem,) * 5,
        out_shape=(
            jax.ShapeDtypeStruct((CHUNKS[0] + EXTRA, BLOCK), F32),
            jax.ShapeDtypeStruct((CHUNKS[1], BLOCK), F32),
            jax.ShapeDtypeStruct((CHUNKS[2], BLOCK), F32),
            jax.ShapeDtypeStruct((WIDTH, WIDTH), BF16),
            jax.ShapeDtypeStruct((8, WIDTH), F32),
        ),
        scratch_shapes=[pltpu.VMEM((PACKED, BLOCK), F32)]
        + [pltpu.VMEM((WIDTH, BLOCK), F32)] * 4
        + [
            pltpu.VMEM((WIDTH, WIDTH), BF16),
            pltpu.VMEM((ROWS - RAW, WIDTH), F32),
            pltpu.SemaphoreType.DMA,
        ],
        compiler_params=pltpu.CompilerParams(vmem_limit_bytes=VMEM_LIMIT),
        cost_estimate=pl.CostEstimate(flops=10**9, bytes_accessed=6 * 2**20, transcendentals=0),
    )(block_ids, *parts, pltpu.with_memory_space_constraint(slab, pltpu.HBM))


def cost(count):
    return pl.CostEstimate(
        flops=6 * count * WIDTH * BLOCK, bytes_accessed=6 * count * WIDTH, transcendentals=0
    )


def staying_kernel(x_ref, rot_ref, out_ref):
    out_ref[...] = rotation(x_ref[...], rot_ref[...])


def staying(slab, rot, rows=512):
    count = slab.shape[0]
    return pl.pallas_call(
        staying_kernel,
        grid=(count // rows,),
        in_specs=[
            pl.BlockSpec((rows, WIDTH), lambda i: (i, 0)),
            pl.BlockSpec((WIDTH, WIDTH), lambda i: (0, 0)),
        ],
        out_specs=pl.BlockSpec((rows, BLOCK), lambda i: (i, 0)),
        out_shape=pltpu.HBM((count, WIDTH), F32),
        compiler_params=pltpu.CompilerParams(vmem_limit_bytes=VMEM_LIMIT),
        cost_estimate=cost(count),
    )(pltpu.with_memory_space_constraint(slab, pltpu.HBM), rot)


def raw_kernel(x_ref, p0_ref, p1_ref, p2_ref, p3_ref, _, out_ref, full, rot):
    @pl.when(pl.program_id(0) == 0)
    def _():
        for d, piece in enumerate((p0_ref, p1_ref, p2_ref, p3_ref)):
            start = (place()[1] ^ d) * 64
            full[pl.ds(pl.multiple_of(start, 64), 64), :] = piece[...]
        high = full[...].astype(BF16)
        rot[:, 0:128] = high
        rot[:, 128:256] = (full[...] - high.astype(F32)).astype(BF16)

    out_ref[...] = rotation(x_ref[...], rot[...])


def rotated_raw(raw, pieces, result, rows=128):
    count = raw.shape[0]
    piece = pl.BlockSpec((64, BLOCK), lambda i: (0, 0))
    return pl.pallas_call(
        raw_kernel,
        grid=(count // rows,),
        in_specs=[
            pl.BlockSpec((rows, WIDTH), lambda i: (i, 0)),
            piece,
            piece,
            piece,
            piece,
            pl.BlockSpec(memory_space=pl.ANY),
        ],
        out_specs=pl.BlockSpec((rows, BLOCK), lambda i: (i, 1)),
        out_shape=pltpu.HBM(result.shape, F32),
        scratch_shapes=[pltpu.VMEM((WIDTH, BLOCK), F32), pltpu.VMEM((WIDTH, WIDTH), BF16)],
        input_output_aliases={5: 0},
        compiler_params=pltpu.CompilerParams(vmem_limit_bytes=VMEM_LIMIT),
        cost_estimate=cost(count),
    )(raw, *pieces, result)


def per_device(slab, block_ids):
    core, _ = place()
    parts, raw = summed_over_rows(local_gram(slab), core, slab[:RAW])
    *leaving, rot_stay, diag = rounds_and_leaving(parts, slab, block_ids)
    leaving[0], raw = lax.optimization_barrier((leaving[0], raw))
    arrived = [passed_along(chunk) for chunk in leaving]
    extra = arrived[0][CHUNKS[0] :]
    new_slab = staying(slab, rot_stay)
    new_slab = rotated_raw(raw, with_three_others(extra[:64], 1), new_slab)
    for n, chunk in enumerate(arrived):
        start = (RAW + sum(CHUNKS[:n]), BLOCK)
        new_slab = lax.dynamic_update_slice(new_slab, chunk[: CHUNKS[n]], start)
    total_rows = slab.shape[0] * lax.axis_size("row")
    squares = jnp.concatenate([diag[0, :BLOCK], extra[64]])
    col_norms = jnp.sqrt(jnp.maximum(squares, 0.0) / total_rows)
    new_ids = jnp.stack([jnp.min(block_ids), extra[72, 0].astype(jnp.int32)])
    return (new_slab, col_norms, new_ids)


def solution(mesh):
    return jax.shard_map(
        per_device,
        mesh=mesh,
        in_specs=(P("row", "pair"), P("pair")),
        out_specs=(P("row", "pair"), P("pair"), P("pair")),
        check_vma=False,
    )
```

time: 167 us -> 142 us (0.85)
  the two profiles are of different devices: /device:TPU:56 before, /device:TPU:8 now
where the time goes in v2:
time: 142 us; the launch traced here: 141 us
  waiting for transfers between devices  67.6 us (48%)
  starting transfers between devices  35.1 us (25%)
  Pallas kernels  30.3 us (21%)
  local copies, waits for them, and re-layouts  4.22 us (3%)
  other arithmetic  2.62 us (2%)
    ppermute x4, waiting for transfers between devices, passed_along(): return lax.ppermute(array, 'pair', [(0, 1), (1, 0)])  55.1 us
    ppermute x14, starting transfers between devices, exchanged(): return lax.ppermute(array, 'row', [(i, i ^ mask) for i in range(128)])  18 us
    ppermute x4, starting transfers between devices, passed_along(): return lax.ppermute(array, 'pair', [(0, 1), (1, 0)])  17.1 us
    pallas_call x1, Pallas kernels, rounds_and_leaving(): pl.pallas_call(rounds_kernel, in_specs=[pl.BlockSpec(memory_space=pltpu.S...  16.3 us
    ppermute x14, waiting for transfers between devices, exchanged(): return lax.ppermute(array, 'row', [(i, i ^ mask) for i in range(128)])  12.5 us
    pallas_call x1, Pallas kernels, staying(): pl.pallas_call(staying_kernel, grid=(count // rows,), in_specs=[pl.BlockS...  7.17 us
    pallas_call x1, Pallas kernels, local_gram(): pl.pallas_call(gram_kernel, in_specs=[pl.BlockSpec(memory_space=pl.ANY)],...  4.26 us
  transfers between devices with their start and end apart: 18, of which 10 were waited for; matrix products, arithmetic and copies ran while one was open for 4% of the time, Pallas kernels for 18%

profile of v2, /device:TPU:8, one launch (start us, length us, event | category | flops | bytes accessed | tf_op | source)
XLA Modules:
  0.0 141.3 jit_solution(4320730283355022403)
XLA Ops:
  0.6 4.3 %shard_map.49 = f32[272,128]{1,0:T(8,128)S(1)} custom-call(f32[4096,256]{1,0:T(8,128)} %x_ref.1), custom_call_target="tpu_custom_call" | custom-call | tf_op jit(solution)/shard_map/pallas_call | solution.py:65
  5.0 1.2 collective-permute-done
  6.3 4.7 %collective-permute-start.3 = (f32[136,128]{1,0:T(8,128)S(1)}, f32[136,128]{1,0:T(8,128)S(1)}, u32[]{:S(2)}, u32[]{:S(2)}) collective-permute-start(f32[136,128]{1,0:T(8,128)S(1)} %dynamic-slice_add_fusion), channel_id=1, source_target_pairs={{0,192},{2,194},{4,196},{6,198},{8,200},{10,202},{12,204},{14,206}... | collective-permute-start | bytes 208904 | tf_op jit(solution)/shard_map/ppermute | solution.py:86
  11.7 1.1 slice.22
  12.8 1.2 collective-permute-done.3
  14.0 2.2 %collective-permute-done.2 = f32[136,128]{1,0:T(8,128)S(1)} collective-permute-done((f32[136,128]{1,0:T(8,128)S(1)}, f32[136,128]{1,0:T(8,128)S(1)}, u32[]{:S(2)}, u32[]{:S(2)}) %collective-permute-start.2) | collective-permute-done | bytes 69664 | tf_op jit(solution)/shard_map/ppermute | solution.py:86
  17.0 2.8 %collective-permute-start.6 = (f32[136,128]{1,0:T(8,128)S(1)}, f32[136,128]{1,0:T(8,128)S(1)}, u32[]{:S(2)}, u32[]{:S(2)}) collective-permute-start(f32[136,128]{1,0:T(8,128)S(1)} %add_add_fusion.2), channel_id=1, source_target_pairs={{0,12},{2,14},{4,8},{6,10},{8,4},{10,6},{12,0},{14,2},{16,28},{18,... | collective-permute-start | bytes 208904 | tf_op jit(solution)/shard_map/ppermute | solution.py:86
  20.1 1.7 %collective-permute-start.4 = (f32[136,128]{1,0:T(8,128)S(1)}, f32[136,128]{1,0:T(8,128)S(1)}, u32[]{:S(2)}, u32[]{:S(2)}) collective-permute-start(f32[136,128]{1,0:T(8,128)S(1)} %add_add_fusion.2), channel_id=1, source_target_pairs={{0,8},{2,10},{4,12},{6,14},{8,0},{10,2},{12,4},{14,6},{16,24},{18,... | collective-permute-start | bytes 208904 | tf_op jit(solution)/shard_map/ppermute | solution.py:86
  21.8 5.8 %collective-permute-start.11 = (f32[640,256]{1,0:T(8,128)S(1)}, f32[640,256]{1,0:T(8,128)S(1)}, u32[]{:S(2)}, u32[]{:S(2)}) collective-permute-start(f32[640,256]{1,0:T(8,128)S(1)} %slice.22), channel_id=1, source_target_pairs={{0,1},{1,0},{2,3},{3,2},{4,5},{5,4},{6,7},{7,6},{8,9},{9,8},{10,11... | collective-permute-start | bytes 1966088 | tf_op jit(solution)/shard_map/ppermute | solution.py:90
  27.7 1.7 %collective-permute-start.9 = (f32[136,128]{1,0:T(8,128)S(1)}, f32[136,128]{1,0:T(8,128)S(1)}, u32[]{:S(2)}, u32[]{:S(2)}) collective-permute-start(f32[136,128]{1,0:T(8,128)S(1)} %add_add_fusion.1), channel_id=1, source_target_pairs={{0,48},{2,50},{4,52},{6,54},{8,56},{10,58},{12,60},{14,62},{16,32}... | collective-permute-start | bytes 208904 | tf_op jit(solution)/shard_map/ppermute | solution.py:86
  29.3 1.9 %collective-permute-start.8 = (f32[136,128]{1,0:T(8,128)S(1)}, f32[136,128]{1,0:T(8,128)S(1)}, u32[]{:S(2)}, u32[]{:S(2)}) collective-permute-start(f32[136,128]{1,0:T(8,128)S(1)} %add_add_fusion.1), channel_id=1, source_target_pairs={{0,16},{2,18},{4,20},{6,22},{8,24},{10,26},{12,28},{14,30},{16,0},... | collective-permute-start | bytes 208904 | tf_op jit(solution)/shard_map/ppermute | solution.py:86
  32.1 1.6 %collective-permute-done.8 = f32[136,128]{1,0:T(8,128)S(1)} collective-permute-done((f32[136,128]{1,0:T(8,128)S(1)}, f32[136,128]{1,0:T(8,128)S(1)}, u32[]{:S(2)}, u32[]{:S(2)}) %collective-permute-start.8) | collective-permute-done | bytes 69664 | tf_op jit(solution)/shard_map/ppermute | solution.py:86
  33.6 3.4 %collective-permute-done.7 = f32[136,128]{1,0:T(8,128)S(1)} collective-permute-done((f32[136,128]{1,0:T(8,128)S(1)}, f32[136,128]{1,0:T(8,128)S(1)}, u32[]{:S(2)}, u32[]{:S(2)}) %collective-permute-start.7) | collective-permute-done | bytes 69664 | tf_op jit(solution)/shard_map/ppermute | solution.py:86
  37.2 1.2 collective-permute-done.10.other_ref
  38.4 16.3 %shard_map.50 = (f32[1104,128]{1,0:T(8,128)S(1)}, f32[1792,128]{1,0:T(8,128)S(1)}, f32[640,128]{1,0:T(8,128)S(1)}, bf16[256,256]{1,0:T(8,128)(2,1)S(1)}, f32[8,256]{1,0:T(8,128)S(1)}) custom-call(s32[2]{0:T(128)S(1)} %copy-done, f32[136,128]{1,0:T(8,128)S(1)} %add_add_fusion.mine_ref, f32[136,128]{1,0:T(8,128)S(1)} %collective-permute-done.10.other_ref, ...), custom_call_target="tpu_custom_call" | custom-call | flops 1000000000 | bytes 6291456 | tf_op jit(solution)/shard_map/pallas_call | solution.py:224
  54.8 5.3 %collective-permute-start.12 = (f32[1104,128]{1,0:T(8,128)S(1)}, f32[1104,128]{1,0:T(8,128)S(1)}, u32[]{:S(2)}, u32[]{:S(2)}) collective-permute-start(f32[1104,128]{1,0:T(8,128)S(1)} %get-tuple-element.16), channel_id=1, source_target_pairs={{0,1},{1,0},{2,3},{3,2},{4,5},{5,4},{6,7},{7,6},{8,9},{9,8},{10,11... | collective-permute-start | bytes 1695752 | tf_op jit(solution)/shard_map/ppermute | solution.py:90
  61.5 5.3 %collective-permute-start.16 = (f32[1792,128]{1,0:T(8,128)S(1)}, f32[1792,128]{1,0:T(8,128)S(1)}, u32[]{:S(2)}, u32[]{:S(2)}) collective-permute-start(f32[1792,128]{1,0:T(8,128)S(1)} %get-tuple-element.18), channel_id=1, source_target_pairs={{0,1},{1,0},{2,3},{3,2},{4,5},{5,4},{6,7},{7,6},{8,9},{9,8},{10,11... | collective-permute-start | bytes 2752520 | tf_op jit(solution)/shard_map/ppermute | solution.py:90
  66.7 7.2 %shard_map.51._ = f32[4096,256]{1,0:T(8,128)} custom-call(f32[4096,256]{1,0:T(8,128)} %x_ref.1, bf16[256,256]{1,0:T(8,128)(2,1)S(1)} %get-tuple-element.17.rot_ref), custom_call_target="tpu_custom_call" | custom-call | flops 805306368 | bytes 6291456 | tf_op jit(solution)/shard_map/pallas_call | solution.py:264
  73.9 19.8 %collective-permute-done.12 = f32[1104,128]{1,0:T(8,128)S(1)} collective-permute-done((f32[1104,128]{1,0:T(8,128)S(1)}, f32[1104,128]{1,0:T(8,128)S(1)}, u32[]{:S(2)}, u32[]{:S(2)}) %collective-permute-start.12) | collective-permute-done | bytes 565280 | tf_op jit(solution)/shard_map/ppermute | solution.py:90
  94.8 2.9 %collective-permute-start.13 = (f32[64,128]{1,0:T(8,128)S(1)}, f32[64,128]{1,0:T(8,128)S(1)}, u32[]{:S(2)}, u32[]{:S(2)}) collective-permute-start(f32[64,128]{1,0:T(8,128)S(1)} %slice.28.p0_ref), channel_id=1, source_target_pairs={{0,4},{2,6},{4,0},{6,2},{8,12},{10,14},{12,8},{14,10},{16,20},{18,... | collective-permute-start | bytes 98312 | tf_op jit(solution)/shard_map/ppermute | solution.py:86
  99.5 1.3 pad_add_fusion
  100.8 2.5 %shard_map.52 = f32[4096,256]{1,0:T(8,128)} custom-call(f32[640,256]{1,0:T(8,128)S(1)} %collective-permute-done.11.x_ref, f32[64,128]{1,0:T(8,128)S(1)} %slice.28.p0_ref, f32[64,128]{1,0:T(8,128)S(1)} %collective-permute-done.13.p1_ref, f32[64,128]{1,0:T(8,128)S(1)} %collective-permute-done.14.p2_ref, ...), custom_call_target="tpu_custom_call", output_to_operand_aliasing={{}: (5, {})} | custom-call | flops 125829120 | bytes 983040 | tf_op jit(solution)/shard_map/pallas_call | solution.py:294
  104.2 35.4 %collective-permute-done.16 = f32[1792,128]{1,0:T(8,128)S(1)} collective-permute-done((f32[1792,128]{1,0:T(8,128)S(1)}, f32[1792,128]{1,0:T(8,128)S(1)}, u32[]{:S(2)}, u32[]{:S(2)}) %collective-permute-start.16) | collective-permute-done | bytes 917536 | tf_op jit(solution)/shard_map/ppermute | solution.py:90
  139.5 1.0 constant_dynamic-update-slice_fusion.1
  (34 shorter events, 8.0 us)
Async XLA Ops:
  0.6 37.8 %copy-start = (s32[2]{0:T(128)S(1)}, s32[2]{0:T(128)}, u32[]{:S(2)}) copy-start(s32[2]{0:T(128)} %ids_ref.1) | copy-start | bytes 28
  4.9 1.3 collective-permute-start
  6.3 7.7 %collective-permute-start.3 = (f32[136,128]{1,0:T(8,128)S(1)}, f32[136,128]{1,0:T(8,128)S(1)}, u32[]{:S(2)}, u32[]{:S(2)}) collective-permute-start(f32[136,128]{1,0:T(8,128)S(1)} %dynamic-slice_add_fusion), channel_id=1, source_target_pairs={{0,192},{2,194},{4,196},{6,198},{8,200},{10,202},{12,204},{14,206}... | collective-permute-start | bytes 208904 | tf_op jit(solution)/shard_map/ppermute | solution.py:86
  11.0 5.2 %collective-permute-start.2 = (f32[136,128]{1,0:T(8,128)S(1)}, f32[136,128]{1,0:T(8,128)S(1)}, u32[]{:S(2)}, u32[]{:S(2)}) collective-permute-start(f32[136,128]{1,0:T(8,128)S(1)} %dynamic-slice_add_fusion), channel_id=1, source_target_pairs={{0,64},{2,66},{4,68},{6,70},{8,72},{10,74},{12,76},{14,78},{16,80}... | collective-permute-start | bytes 208904 | tf_op jit(solution)/shard_map/ppermute | solution.py:86
  11.0 6.0 %collective-permute-start.1 = (f32[136,128]{1,0:T(8,128)S(1)}, f32[136,128]{1,0:T(8,128)S(1)}, u32[]{:S(2)}, u32[]{:S(2)}) collective-permute-start(f32[136,128]{1,0:T(8,128)S(1)} %dynamic-slice_add_fusion), channel_id=1, source_target_pairs={{0,128},{2,130},{4,132},{6,134},{8,136},{10,138},{12,140},{14,142}... | collective-permute-start | bytes 208904 | tf_op jit(solution)/shard_map/ppermute | solution.py:86
  17.0 10.6 %collective-permute-start.6 = (f32[136,128]{1,0:T(8,128)S(1)}, f32[136,128]{1,0:T(8,128)S(1)}, u32[]{:S(2)}, u32[]{:S(2)}) collective-permute-start(f32[136,128]{1,0:T(8,128)S(1)} %add_add_fusion.2), channel_id=1, source_target_pairs={{0,12},{2,14},{4,8},{6,10},{8,4},{10,6},{12,0},{14,2},{16,28},{18,... | collective-permute-start | bytes 208904 | tf_op jit(solution)/shard_map/ppermute | solution.py:86
  19.8 7.8 %collective-permute-start.5 = (f32[136,128]{1,0:T(8,128)S(1)}, f32[136,128]{1,0:T(8,128)S(1)}, u32[]{:S(2)}, u32[]{:S(2)}) collective-permute-start(f32[136,128]{1,0:T(8,128)S(1)} %add_add_fusion.2), channel_id=1, source_target_pairs={{0,4},{2,6},{4,0},{6,2},{8,12},{10,14},{12,8},{14,10},{16,20},{18,... | collective-permute-start | bytes 208904 | tf_op jit(solution)/shard_map/ppermute | solution.py:86
  20.1 7.6 %collective-permute-start.4 = (f32[136,128]{1,0:T(8,128)S(1)}, f32[136,128]{1,0:T(8,128)S(1)}, u32[]{:S(2)}, u32[]{:S(2)}) collective-permute-start(f32[136,128]{1,0:T(8,128)S(1)} %add_add_fusion.2), channel_id=1, source_target_pairs={{0,8},{2,10},{4,12},{6,14},{8,0},{10,2},{12,4},{14,6},{16,24},{18,... | collective-permute-start | bytes 208904 | tf_op jit(solution)/shard_map/ppermute | solution.py:86
  21.8 33.0 %collective-permute-start.11 = (f32[640,256]{1,0:T(8,128)S(1)}, f32[640,256]{1,0:T(8,128)S(1)}, u32[]{:S(2)}, u32[]{:S(2)}) collective-permute-start(f32[640,256]{1,0:T(8,128)S(1)} %slice.22), channel_id=1, source_target_pairs={{0,1},{1,0},{2,3},{3,2},{4,5},{5,4},{6,7},{7,6},{8,9},{9,8},{10,11... | collective-permute-start | bytes 1966088 | tf_op jit(solution)/shard_map/ppermute | solution.py:90
  27.7 4.4 %collective-permute-start.9 = (f32[136,128]{1,0:T(8,128)S(1)}, f32[136,128]{1,0:T(8,128)S(1)}, u32[]{:S(2)}, u32[]{:S(2)}) collective-permute-start(f32[136,128]{1,0:T(8,128)S(1)} %add_add_fusion.1), channel_id=1, source_target_pairs={{0,48},{2,50},{4,52},{6,54},{8,56},{10,58},{12,60},{14,62},{16,32}... | collective-permute-start | bytes 208904 | tf_op jit(solution)/shard_map/ppermute | solution.py:86
  29.3 4.3 %collective-permute-start.8 = (f32[136,128]{1,0:T(8,128)S(1)}, f32[136,128]{1,0:T(8,128)S(1)}, u32[]{:S(2)}, u32[]{:S(2)}) collective-permute-start(f32[136,128]{1,0:T(8,128)S(1)} %add_add_fusion.1), channel_id=1, source_target_pairs={{0,16},{2,18},{4,20},{6,22},{8,24},{10,26},{12,28},{14,30},{16,0},... | collective-permute-start | bytes 208904 | tf_op jit(solution)/shard_map/ppermute | solution.py:86
  31.2 5.8 %collective-permute-start.7 = (f32[136,128]{1,0:T(8,128)S(1)}, f32[136,128]{1,0:T(8,128)S(1)}, u32[]{:S(2)}, u32[]{:S(2)}) collective-permute-start(f32[136,128]{1,0:T(8,128)S(1)} %add_add_fusion.1), channel_id=1, source_target_pairs={{0,32},{2,34},{4,36},{6,38},{8,40},{10,42},{12,44},{14,46},{16,48}... | collective-permute-start | bytes 208904 | tf_op jit(solution)/shard_map/ppermute | solution.py:86
  37.1 1.3 collective-permute-start.10
  54.8 38.9 %collective-permute-start.12 = (f32[1104,128]{1,0:T(8,128)S(1)}, f32[1104,128]{1,0:T(8,128)S(1)}, u32[]{:S(2)}, u32[]{:S(2)}) collective-permute-start(f32[1104,128]{1,0:T(8,128)S(1)} %get-tuple-element.16), channel_id=1, source_target_pairs={{0,1},{1,0},{2,3},{3,2},{4,5},{5,4},{6,7},{7,6},{8,9},{9,8},{10,11... | collective-permute-start | bytes 1695752 | tf_op jit(solution)/shard_map/ppermute | solution.py:90
  60.8 79.7 %collective-permute-start.17 = (f32[640,128]{1,0:T(8,128)S(1)}, f32[640,128]{1,0:T(8,128)S(1)}, u32[]{:S(2)}, u32[]{:S(2)}) collective-permute-start(f32[640,128]{1,0:T(8,128)S(1)} %get-tuple-element.19), channel_id=1, source_target_pairs={{0,1},{1,0},{2,3},{3,2},{4,5},{5,4},{6,7},{7,6},{8,9},{9,8},{10,11... | collective-permute-start | bytes 983048 | tf_op jit(solution)/shard_map/ppermute | solution.py:90
  61.5 78.1 %collective-permute-start.16 = (f32[1792,128]{1,0:T(8,128)S(1)}, f32[1792,128]{1,0:T(8,128)S(1)}, u32[]{:S(2)}, u32[]{:S(2)}) collective-permute-start(f32[1792,128]{1,0:T(8,128)S(1)} %get-tuple-element.18), channel_id=1, source_target_pairs={{0,1},{1,0},{2,3},{3,2},{4,5},{5,4},{6,7},{7,6},{8,9},{9,8},{10,11... | collective-permute-start | bytes 2752520 | tf_op jit(solution)/shard_map/ppermute | solution.py:90
  93.7 7.1 %collective-permute-start.15 = (f32[64,128]{1,0:T(8,128)S(1)}, f32[64,128]{1,0:T(8,128)S(1)}, u32[]{:S(2)}, u32[]{:S(2)}) collective-permute-start(f32[64,128]{1,0:T(8,128)S(1)} %slice.28.p0_ref), channel_id=1, source_target_pairs={{0,12},{2,14},{4,8},{6,10},{8,4},{10,6},{12,0},{14,2},{16,28},{18,... | collective-permute-start | bytes 98312 | tf_op jit(solution)/shard_map/ppermute | solution.py:86
  94.2 6.6 %collective-permute-start.14 = (f32[64,128]{1,0:T(8,128)S(1)}, f32[64,128]{1,0:T(8,128)S(1)}, u32[]{:S(2)}, u32[]{:S(2)}) collective-permute-start(f32[64,128]{1,0:T(8,128)S(1)} %slice.28.p0_ref), channel_id=1, source_target_pairs={{0,8},{2,10},{4,12},{6,14},{8,0},{10,2},{12,4},{14,6},{16,24},{18,... | collective-permute-start | bytes 98312 | tf_op jit(solution)/shard_map/ppermute | solution.py:86
  94.8 6.0 %collective-permute-start.13 = (f32[64,128]{1,0:T(8,128)S(1)}, f32[64,128]{1,0:T(8,128)S(1)}, u32[]{:S(2)}, u32[]{:S(2)}) collective-permute-start(f32[64,128]{1,0:T(8,128)S(1)} %slice.28.p0_ref), channel_id=1, source_target_pairs={{0,4},{2,6},{4,0},{6,2},{8,12},{10,14},{12,8},{14,10},{16,20},{18,... | collective-permute-start | bytes 98312 | tf_op jit(solution)/shard_map/ppermute | solution.py:86

commit v3 on v2

--- a/solution.py
+++ b/solution.py
@@ -17,8 +17,8 @@
 ROWS = 4096
 RAW = 640
 CHUNKS = (1024, 1792, ROWS - RAW - 2816)
-EXTRA = 80
-STEP = 128
+EXTRA = 40
+STEP = 256
 PACKED = 272
 PARTS = 4
 
@@ -119,11 +119,11 @@
     return tang, cosv, tang * cosv
 
 def rounds_kernel(
-    ids_ref, mine_ref, other_ref, slab_ref, first_ref, second_ref, third_ref, stay_ref, diag_ref,
-    packed, vt, vb, wt, wb, leave, x_ref, sem,
+    ids_ref, mine_ref, other_ref, slab_ref, first_ref, leave_ref, stay_ref, diag_ref,
+    packed, vt, vb, wt, wb, x_ref, sem,
 ):
     rounds = ROUNDS
-    fetch = pltpu.make_async_copy(slab_ref.at[pl.ds(RAW, ROWS - RAW), :], x_ref, sem)
+    fetch = pltpu.make_async_copy(slab_ref.at[pl.ds(RAW, CHUNKS[0]), :], x_ref, sem)
     fetch.start()
     core, x = place()
     swap = (ids_ref[1] <= ids_ref[0]).astype(jnp.int32)
@@ -192,24 +192,19 @@
     low = (rot - high.astype(F32)).astype(BF16)
     stay_ref[:, 0:128] = high[:, 0:128]
     stay_ref[:, 128:256] = low[:, 0:128]
-    leave[:, 0:128] = high[:, 128:256]
-    leave[:, 128:256] = low[:, 128:256]
+    leave_ref[:, 0:128] = high[:, 128:256]
+    leave_ref[:, 128:256] = low[:, 128:256]
     diag = dot(d_top, p_top) + dot(d_bot, p_bot)
     diag_ref[...] = diag
     wt[...] = rot[:, 128:256]
-    first_ref[CHUNKS[0] : CHUNKS[0] + 64, :] = wt[pl.ds(pl.multiple_of(x * 64, 64), 64), :]
-    first_ref[CHUNKS[0] + 64 : CHUNKS[0] + 72, :] = diag[:, 128:256]
-    first_ref[CHUNKS[0] + 72 : CHUNKS[0] + 80, :] = jnp.full((8, half), jnp.maximum(ids_ref[0], ids_ref[1]).astype(F32))
+    piece = pl.ds(pl.multiple_of((2 * x + core) * 32, 32), 32)
+    first_ref[CHUNKS[0] : CHUNKS[0] + 32, :] = wt[piece, :]
+    label = jnp.full((8, half), jnp.maximum(ids_ref[0], ids_ref[1]).astype(F32))
+    upper = lax.broadcasted_iota(jnp.int32, (8, half), 0) < 4
+    first_ref[CHUNKS[0] + 32 : CHUNKS[0] + 40, :] = jnp.where(upper, diag[:, 128:256], label)
     fetch.wait()
-    for n, out_ref in enumerate((first_ref, second_ref, third_ref)):
-        base = sum(CHUNKS[:n])
-
-        def one_step(k, _, out_ref=out_ref, base=base):
-            start = pl.multiple_of(k * STEP, STEP)
-            out_ref[pl.ds(start, STEP), :] = rotation(x_ref[pl.ds(base + start, STEP), :], leave[...])
-            return 0
-
-        lax.fori_loop(0, CHUNKS[n] // STEP, one_step, 0, unroll=2)
+    for start in range(0, CHUNKS[0], STEP):
+        first_ref[start : start + STEP, :] = rotation(x_ref[start : start + STEP, :], leave_ref[...])
 
 
 def rotation(x, rot):
@@ -219,7 +214,7 @@
     return (both[:, 0:128] + both[:, 128:256]) + product(low, rot[:, 0:128])
 
 
-def rounds_and_leaving(parts, slab, block_ids):
+def rounds_and_first_chunk(parts, slab, block_ids):
     in_vmem = pl.BlockSpec(memory_space=pltpu.VMEM)
     return pl.pallas_call(
         rounds_kernel,
@@ -229,23 +224,21 @@
             in_vmem,
             pl.BlockSpec(memory_space=pl.ANY),
         ],
-        out_specs=(in_vmem,) * 5,
+        out_specs=(in_vmem,) * 4,
         out_shape=(
             jax.ShapeDtypeStruct((CHUNKS[0] + EXTRA, BLOCK), F32),
-            jax.ShapeDtypeStruct((CHUNKS[1], BLOCK), F32),
-            jax.ShapeDtypeStruct((CHUNKS[2], BLOCK), F32),
+            jax.ShapeDtypeStruct((WIDTH, WIDTH), BF16),
             jax.ShapeDtypeStruct((WIDTH, WIDTH), BF16),
             jax.ShapeDtypeStruct((8, WIDTH), F32),
         ),
         scratch_shapes=[pltpu.VMEM((PACKED, BLOCK), F32)]
         + [pltpu.VMEM((WIDTH, BLOCK), F32)] * 4
         + [
-            pltpu.VMEM((WIDTH, WIDTH), BF16),
-            pltpu.VMEM((ROWS - RAW, WIDTH), F32),
+            pltpu.VMEM((CHUNKS[0], WIDTH), F32),
             pltpu.SemaphoreType.DMA,
         ],
         compiler_params=pltpu.CompilerParams(vmem_limit_bytes=VMEM_LIMIT),
-        cost_estimate=pl.CostEstimate(flops=10**9, bytes_accessed=6 * 2**20, transcendentals=0),
+        cost_estimate=pl.CostEstimate(flops=0, bytes_accessed=0, transcendentals=0),
     )(block_ids, *parts, pltpu.with_memory_space_constraint(slab, pltpu.HBM))
 
 
@@ -255,14 +248,29 @@
     )
 
 
-def staying_kernel(x_ref, rot_ref, out_ref):
+def rotate_kernel(x_ref, rot_ref, out_ref):
     out_ref[...] = rotation(x_ref[...], rot_ref[...])
+
+
+def leaving(slab, rot, first, count, rows=128):
+    return pl.pallas_call(
+        rotate_kernel,
+        grid=(count // rows,),
+        in_specs=[
+            pl.BlockSpec((rows, WIDTH), lambda i: (i + first // rows, 0)),
+            pl.BlockSpec((WIDTH, WIDTH), lambda i: (0, 0)),
+        ],
+        out_specs=pl.BlockSpec((rows, BLOCK), lambda i: (i, 0)),
+        out_shape=jax.ShapeDtypeStruct((count, BLOCK), F32),
+        compiler_params=pltpu.CompilerParams(vmem_limit_bytes=VMEM_LIMIT),
+        cost_estimate=cost(count),
+    )(pltpu.with_memory_space_constraint(slab, pltpu.HBM), rot)
 
 
 def staying(slab, rot, rows=512):
     count = slab.shape[0]
     return pl.pallas_call(
-        staying_kernel,
+        rotate_kernel,
         grid=(count // rows,),
         in_specs=[
             pl.BlockSpec((rows, WIDTH), lambda i: (i, 0)),
@@ -279,8 +287,9 @@
     @pl.when(pl.program_id(0) == 0)
     def _():
         for d, piece in enumerate((p0_ref, p1_ref, p2_ref, p3_ref)):
-            start = (place()[1] ^ d) * 64
-            full[pl.ds(pl.multiple_of(start, 64), 64), :] = piece[...]
+            for h in range(2):
+                start = (2 * (place()[1] ^ d) + (place()[0] ^ h)) * 32
+                full[pl.ds(pl.multiple_of(start, 32), 32), :] = piece[32 * h : 32 * h + 32, :]
         high = full[...].astype(BF16)
         rot[:, 0:128] = high
         rot[:, 128:256] = (full[...] - high.astype(F32)).astype(BF16)
@@ -314,19 +323,22 @@
 def per_device(slab, block_ids):
     core, _ = place()
     parts, raw = summed_over_rows(local_gram(slab), core, slab[:RAW])
-    *leaving, rot_stay, diag = rounds_and_leaving(parts, slab, block_ids)
-    leaving[0], raw = lax.optimization_barrier((leaving[0], raw))
-    arrived = [passed_along(chunk) for chunk in leaving]
+    first, rot_leave, rot_stay, diag = rounds_and_first_chunk(parts, slab, block_ids)
+    first, raw = lax.optimization_barrier((first, raw))
+    arrived = [passed_along(first)]
     extra = arrived[0][CHUNKS[0] :]
+    starts = [RAW + sum(CHUNKS[:n]) for n in range(len(CHUNKS))]
+    for start, count in zip(starts[1:], CHUNKS[1:]):
+        arrived.append(passed_along(leaving(slab, rot_leave, start, count)))
     new_slab = staying(slab, rot_stay)
-    new_slab = rotated_raw(raw, with_three_others(extra[:64], 1), new_slab)
-    for n, chunk in enumerate(arrived):
-        start = (RAW + sum(CHUNKS[:n]), BLOCK)
-        new_slab = lax.dynamic_update_slice(new_slab, chunk[: CHUNKS[n]], start)
+    both = jnp.concatenate([extra[:32], exchanged(extra[:32], 1)])
+    new_slab = rotated_raw(raw, with_three_others(both, 1), new_slab)
+    for start, count, chunk in zip(starts, CHUNKS, arrived):
+        new_slab = lax.dynamic_update_slice(new_slab, chunk[:count], (start, BLOCK))
     total_rows = slab.shape[0] * lax.axis_size("row")
-    squares = jnp.concatenate([diag[0, :BLOCK], extra[64]])
+    squares = jnp.concatenate([diag[0, :BLOCK], extra[32]])
     col_norms = jnp.sqrt(jnp.maximum(squares, 0.0) / total_rows)
-    new_ids = jnp.stack([jnp.min(block_ids), extra[72, 0].astype(jnp.int32)])
+    new_ids = jnp.stack([jnp.min(block_ids), extra[36, 0].astype(jnp.int32)])
     return (new_slab, col_norms, new_ids)
 
 

time: 142 us -> 140 us (0.986)
  the two profiles are of different devices: /device:TPU:8 before, /device:TPU:56 now
where the time goes in v3:
time: 140 us
  starting transfers between devices  49.4 us (35%)
  waiting for transfers between devices  42.6 us (30%)
  Pallas kernels  39.4 us (28%)
  local copies, waits for them, and re-layouts  4.22 us (3%)
  other arithmetic  2.64 us (2%)
  between operations  1.42 us (1%)
    ppermute x15, starting transfers between devices, exchanged(): return lax.ppermute(array, 'row', [(i, i ^ mask) for i in range(128)])  31 us
    ppermute x4, waiting for transfers between devices, passed_along(): return lax.ppermute(array, 'pair', [(0, 1), (1, 0)])  29.6 us
    ppermute x4, starting transfers between devices, passed_along(): return lax.ppermute(array, 'pair', [(0, 1), (1, 0)])  18.4 us
    pallas_call x1, Pallas kernels, rounds_and_first_chunk(): pl.pallas_call(rounds_kernel, in_specs=[pl.BlockSpec(memory_space=pltpu.S...  14.2 us
    ppermute x15, waiting for transfers between devices, exchanged(): return lax.ppermute(array, 'row', [(i, i ^ mask) for i in range(128)])  13 us
    pallas_call x2, Pallas kernels, leaving(): pl.pallas_call(rotate_kernel, grid=(count // rows,), in_specs=[pl.BlockSp...  11.3 us
    pallas_call x1, Pallas kernels, staying(): pl.pallas_call(rotate_kernel, grid=(count // rows,), in_specs=[pl.BlockSp...  7.17 us
    pallas_call x1, Pallas kernels, local_gram(): pl.pallas_call(gram_kernel, in_specs=[pl.BlockSpec(memory_space=pl.ANY)],...  4.26 us
  transfers between devices with their start and end apart: 19, of which 11 were waited for; matrix products, arithmetic and copies ran while one was open for 4% of the time, Pallas kernels for 25%

profile of v3, /device:TPU:56, one launch (start us, length us, event | category | flops | bytes accessed | tf_op | source)
XLA Modules:
  0.0 139.6 jit_solution(1738753410215476106)
XLA Ops:
  0.6 4.3 %shard_map.49 = f32[272,128]{1,0:T(8,128)S(1)} custom-call(f32[4096,256]{1,0:T(8,128)} %x_ref.5), custom_call_target="tpu_custom_call" | custom-call | tf_op jit(solution)/shard_map/pallas_call | solution.py:65
  5.0 1.2 collective-permute-done
  6.3 3.4 %collective-permute-start.1 = (f32[136,128]{1,0:T(8,128)S(1)}, f32[136,128]{1,0:T(8,128)S(1)}, u32[]{:S(2)}, u32[]{:S(2)}) collective-permute-start(f32[136,128]{1,0:T(8,128)S(1)} %dynamic-slice_add_fusion), channel_id=1, source_target_pairs={{0,128},{2,130},{4,132},{6,134},{8,136},{10,138},{12,140},{14,142}... | collective-permute-start | bytes 208904 | tf_op jit(solution)/shard_map/ppermute | solution.py:86
  11.5 1.8 %collective-permute-done.1 = f32[136,128]{1,0:T(8,128)S(1)} collective-permute-done((f32[136,128]{1,0:T(8,128)S(1)}, f32[136,128]{1,0:T(8,128)S(1)}, u32[]{:S(2)}, u32[]{:S(2)}) %collective-permute-start.1) | collective-permute-done | bytes 69664 | tf_op jit(solution)/shard_map/ppermute | solution.py:86
  15.5 3.1 %collective-permute-start.4 = (f32[136,128]{1,0:T(8,128)S(1)}, f32[136,128]{1,0:T(8,128)S(1)}, u32[]{:S(2)}, u32[]{:S(2)}) collective-permute-start(f32[136,128]{1,0:T(8,128)S(1)} %add_add_fusion.2), channel_id=1, source_target_pairs={{0,8},{2,10},{4,12},{6,14},{8,0},{10,2},{12,4},{14,6},{16,24},{18,... | collective-permute-start | bytes 208904 | tf_op jit(solution)/shard_map/ppermute | solution.py:86
  19.7 6.4 %collective-permute-start.11 = (f32[640,256]{1,0:T(8,128)S(1)}, f32[640,256]{1,0:T(8,128)S(1)}, u32[]{:S(2)}, u32[]{:S(2)}) collective-permute-start(f32[640,256]{1,0:T(8,128)S(1)} %slice.23), channel_id=1, source_target_pairs={{0,1},{1,0},{2,3},{3,2},{4,5},{5,4},{6,7},{7,6},{8,9},{9,8},{10,11... | collective-permute-start | bytes 1966088 | tf_op jit(solution)/shard_map/ppermute | solution.py:90
  26.2 1.3 collective-permute-start.7
  27.5 2.9 %collective-permute-start.9 = (f32[136,128]{1,0:T(8,128)S(1)}, f32[136,128]{1,0:T(8,128)S(1)}, u32[]{:S(2)}, u32[]{:S(2)}) collective-permute-start(f32[136,128]{1,0:T(8,128)S(1)} %add_add_fusion.1), channel_id=1, source_target_pairs={{0,48},{2,50},{4,52},{6,54},{8,56},{10,58},{12,60},{14,62},{16,32}... | collective-permute-start | bytes 208904 | tf_op jit(solution)/shard_map/ppermute | solution.py:86
  30.3 1.7 %collective-permute-done.7 = f32[136,128]{1,0:T(8,128)S(1)} collective-permute-done((f32[136,128]{1,0:T(8,128)S(1)}, f32[136,128]{1,0:T(8,128)S(1)}, u32[]{:S(2)}, u32[]{:S(2)}) %collective-permute-start.7) | collective-permute-done | bytes 69664 | tf_op jit(solution)/shard_map/ppermute | solution.py:86
  33.1 1.2 collective-permute-done.10.other_ref
  34.4 14.2 %shard_map.50 = (f32[1064,128]{1,0:T(8,128)S(1)}, bf16[256,256]{1,0:T(8,128)(2,1)S(1)}, bf16[256,256]{1,0:T(8,128)(2,1)S(1)}, f32[8,256]{1,0:T(8,128)S(1)}) custom-call(s32[2]{0:T(128)S(1)} %copy-done, f32[136,128]{1,0:T(8,128)S(1)} %add_add_fusion.mine_ref, f32[136,128]{1,0:T(8,128)S(1)} %collective-permute-done.10.other_ref, f32[4096,256]{1,0:T(8,128)} %x_ref.5), custom_call_target="tpu_custom_call" | custom-call | tf_op jit(solution)/shard_map/pallas_call | solution.py:219
  48.5 5.6 %collective-permute-done.11.x_ref = f32[640,256]{1,0:T(8,128)S(1)} collective-permute-done((f32[640,256]{1,0:T(8,128)S(1)}, f32[640,256]{1,0:T(8,128)S(1)}, u32[]{:S(2)}, u32[]{:S(2)}) %collective-permute-start.11) | collective-permute-done | bytes 655392 | tf_op jit(solution)/shard_map/ppermute | solution.py:90
  54.1 5.7 %collective-permute-start.12 = (f32[1064,128]{1,0:T(8,128)S(1)}, f32[1064,128]{1,0:T(8,128)S(1)}, u32[]{:S(2)}, u32[]{:S(2)}) collective-permute-start(f32[1064,128]{1,0:T(8,128)S(1)} %get-tuple-element.15), channel_id=1, source_target_pairs={{0,1},{1,0},{2,3},{3,2},{4,5},{5,4},{6,7},{7,6},{8,9},{9,8},{10,11... | collective-permute-start | bytes 1634312 | tf_op jit(solution)/shard_map/ppermute | solution.py:90
  60.5 8.0 %shard_map.53 = f32[1792,128]{1,0:T(8,128)S(1)} custom-call(f32[4096,256]{1,0:T(8,128)} %x_ref.5, bf16[256,256]{1,0:T(8,128)(2,1)S(1)} %get-tuple-element.17.rot_ref), custom_call_target="tpu_custom_call" | custom-call | flops 352321536 | bytes 2752512 | tf_op jit(solution)/shard_map/pallas_call | solution.py:256
  69.0 3.3 %shard_map.54 = f32[640,128]{1,0:T(8,128)S(1)} custom-call(f32[4096,256]{1,0:T(8,128)} %x_ref.5, bf16[256,256]{1,0:T(8,128)(2,1)S(1)} %get-tuple-element.17.rot_ref), custom_call_target="tpu_custom_call" | custom-call | flops 125829120 | bytes 983040 | tf_op jit(solution)/shard_map/pallas_call | solution.py:256
  72.3 5.8 %collective-permute-start.18 = (f32[640,128]{1,0:T(8,128)S(1)}, f32[640,128]{1,0:T(8,128)S(1)}, u32[]{:S(2)}, u32[]{:S(2)}) collective-permute-start(f32[640,128]{1,0:T(8,128)S(1)} %shard_map.54), channel_id=1, source_target_pairs={{0,1},{1,0},{2,3},{3,2},{4,5},{5,4},{6,7},{7,6},{8,9},{9,8},{10,11... | collective-permute-start | bytes 983048 | tf_op jit(solution)/shard_map/ppermute | solution.py:90
  78.1 7.2 %shard_map.51._ = f32[4096,256]{1,0:T(8,128)} custom-call(f32[4096,256]{1,0:T(8,128)} %x_ref.5, bf16[256,256]{1,0:T(8,128)(2,1)S(1)} %get-tuple-element.16.rot_ref), custom_call_target="tpu_custom_call" | custom-call | flops 805306368 | bytes 6291456 | tf_op jit(solution)/shard_map/pallas_call | solution.py:272
  85.3 24.0 %collective-permute-done.12 = f32[1064,128]{1,0:T(8,128)S(1)} collective-permute-done((f32[1064,128]{1,0:T(8,128)S(1)}, f32[1064,128]{1,0:T(8,128)S(1)}, u32[]{:S(2)}, u32[]{:S(2)}) %collective-permute-start.12) | collective-permute-done | bytes 544800 | tf_op jit(solution)/shard_map/ppermute | solution.py:90
  111.1 1.2 collective-permute-start.14
  112.3 17.1 %collective-permute-start.15 = (f32[64,128]{1,0:T(8,128)S(1)}, f32[64,128]{1,0:T(8,128)S(1)}, u32[]{:S(2)}, u32[]{:S(2)}) collective-permute-start(f32[64,128]{1,0:T(8,128)S(1)} %pad_maximum_fusion.p0_ref), channel_id=1, source_target_pairs={{0,8},{2,10},{4,12},{6,14},{8,0},{10,2},{12,4},{14,6},{16,24},{18,... | collective-permute-start | bytes 98312 | tf_op jit(solution)/shard_map/ppermute | solution.py:86
  129.4 1.3 pad_add_fusion
  130.7 1.2 collective-permute-done.15.p2_ref
  131.9 2.7 %collective-permute-done.16.p3_ref = f32[64,128]{1,0:T(8,128)S(1)} collective-permute-done((f32[64,128]{1,0:T(8,128)S(1)}, f32[64,128]{1,0:T(8,128)S(1)}, u32[]{:S(2)}, u32[]{:S(2)}) %collective-permute-start.16) | collective-permute-done | bytes 32800 | tf_op jit(solution)/shard_map/ppermute | solution.py:86
  134.5 2.5 %shard_map.52 = f32[4096,256]{1,0:T(8,128)} custom-call(f32[640,256]{1,0:T(8,128)S(1)} %collective-permute-done.11.x_ref, f32[64,128]{1,0:T(8,128)S(1)} %pad_maximum_fusion.p0_ref, f32[64,128]{1,0:T(8,128)S(1)} %collective-permute-done.14.p1_ref, f32[64,128]{1,0:T(8,128)S(1)} %collective-permute-done.15.p2_ref, ...), custom_call_target="tpu_custom_call", output_to_operand_aliasing={{}: (5, {})} | custom-call | flops 125829120 | bytes 983040 | tf_op jit(solution)/shard_map/pallas_call | solution.py:303
  (39 shorter events, 11.3 us)
Async XLA Ops:
  0.6 33.7 %copy-start = (s32[2]{0:T(128)S(1)}, s32[2]{0:T(128)}, u32[]{:S(2)}) copy-start(s32[2]{0:T(128)} %ids_ref.1) | copy-start | bytes 28
  4.9 1.3 collective-permute-start
  6.3 6.9 %collective-permute-start.1 = (f32[136,128]{1,0:T(8,128)S(1)}, f32[136,128]{1,0:T(8,128)S(1)}, u32[]{:S(2)}, u32[]{:S(2)}) collective-permute-start(f32[136,128]{1,0:T(8,128)S(1)} %dynamic-slice_add_fusion), channel_id=1, source_target_pairs={{0,128},{2,130},{4,132},{6,134},{8,136},{10,138},{12,140},{14,142}... | collective-permute-start | bytes 208904 | tf_op jit(solution)/shard_map/ppermute | solution.py:86
  9.7 4.7 %collective-permute-start.2 = (f32[136,128]{1,0:T(8,128)S(1)}, f32[136,128]{1,0:T(8,128)S(1)}, u32[]{:S(2)}, u32[]{:S(2)}) collective-permute-start(f32[136,128]{1,0:T(8,128)S(1)} %dynamic-slice_add_fusion), channel_id=1, source_target_pairs={{0,64},{2,66},{4,68},{6,70},{8,72},{10,74},{12,76},{14,78},{16,80}... | collective-permute-start | bytes 208904 | tf_op jit(solution)/shard_map/ppermute | solution.py:86
  9.8 5.7 %collective-permute-start.3 = (f32[136,128]{1,0:T(8,128)S(1)}, f32[136,128]{1,0:T(8,128)S(1)}, u32[]{:S(2)}, u32[]{:S(2)}) collective-permute-start(f32[136,128]{1,0:T(8,128)S(1)} %dynamic-slice_add_fusion), channel_id=1, source_target_pairs={{0,192},{2,194},{4,196},{6,198},{8,200},{10,202},{12,204},{14,206}... | collective-permute-start | bytes 208904 | tf_op jit(solution)/shard_map/ppermute | solution.py:86
  15.5 10.7 %collective-permute-start.4 = (f32[136,128]{1,0:T(8,128)S(1)}, f32[136,128]{1,0:T(8,128)S(1)}, u32[]{:S(2)}, u32[]{:S(2)}) collective-permute-start(f32[136,128]{1,0:T(8,128)S(1)} %add_add_fusion.2), channel_id=1, source_target_pairs={{0,8},{2,10},{4,12},{6,14},{8,0},{10,2},{12,4},{14,6},{16,24},{18,... | collective-permute-start | bytes 208904 | tf_op jit(solution)/shard_map/ppermute | solution.py:86
  18.6 7.6 %collective-permute-start.5 = (f32[136,128]{1,0:T(8,128)S(1)}, f32[136,128]{1,0:T(8,128)S(1)}, u32[]{:S(2)}, u32[]{:S(2)}) collective-permute-start(f32[136,128]{1,0:T(8,128)S(1)} %add_add_fusion.2), channel_id=1, source_target_pairs={{0,4},{2,6},{4,0},{6,2},{8,12},{10,14},{12,8},{14,10},{16,20},{18,... | collective-permute-start | bytes 208904 | tf_op jit(solution)/shard_map/ppermute | solution.py:86
  19.2 7.0 %collective-permute-start.6 = (f32[136,128]{1,0:T(8,128)S(1)}, f32[136,128]{1,0:T(8,128)S(1)}, u32[]{:S(2)}, u32[]{:S(2)}) collective-permute-start(f32[136,128]{1,0:T(8,128)S(1)} %add_add_fusion.2), channel_id=1, source_target_pairs={{0,12},{2,14},{4,8},{6,10},{8,4},{10,6},{12,0},{14,2},{16,28},{18,... | collective-permute-start | bytes 208904 | tf_op jit(solution)/shard_map/ppermute | solution.py:86
  19.7 34.4 %collective-permute-start.11 = (f32[640,256]{1,0:T(8,128)S(1)}, f32[640,256]{1,0:T(8,128)S(1)}, u32[]{:S(2)}, u32[]{:S(2)}) collective-permute-start(f32[640,256]{1,0:T(8,128)S(1)} %slice.23), channel_id=1, source_target_pairs={{0,1},{1,0},{2,3},{3,2},{4,5},{5,4},{6,7},{7,6},{8,9},{9,8},{10,11... | collective-permute-start | bytes 1966088 | tf_op jit(solution)/shard_map/ppermute | solution.py:90
  26.2 5.9 %collective-permute-start.7 = (f32[136,128]{1,0:T(8,128)S(1)}, f32[136,128]{1,0:T(8,128)S(1)}, u32[]{:S(2)}, u32[]{:S(2)}) collective-permute-start(f32[136,128]{1,0:T(8,128)S(1)} %add_add_fusion.1), channel_id=1, source_target_pairs={{0,32},{2,34},{4,36},{6,38},{8,40},{10,42},{12,44},{14,46},{16,48}... | collective-permute-start | bytes 208904 | tf_op jit(solution)/shard_map/ppermute | solution.py:86
  27.5 4.6 %collective-permute-start.8 = (f32[136,128]{1,0:T(8,128)S(1)}, f32[136,128]{1,0:T(8,128)S(1)}, u32[]{:S(2)}, u32[]{:S(2)}) collective-permute-start(f32[136,128]{1,0:T(8,128)S(1)} %add_add_fusion.1), channel_id=1, source_target_pairs={{0,16},{2,18},{4,20},{6,22},{8,24},{10,26},{12,28},{14,30},{16,0},... | collective-permute-start | bytes 208904 | tf_op jit(solution)/shard_map/ppermute | solution.py:86
  27.5 5.5 %collective-permute-start.9 = (f32[136,128]{1,0:T(8,128)S(1)}, f32[136,128]{1,0:T(8,128)S(1)}, u32[]{:S(2)}, u32[]{:S(2)}) collective-permute-start(f32[136,128]{1,0:T(8,128)S(1)} %add_add_fusion.1), channel_id=1, source_target_pairs={{0,48},{2,50},{4,52},{6,54},{8,56},{10,58},{12,60},{14,62},{16,32}... | collective-permute-start | bytes 208904 | tf_op jit(solution)/shard_map/ppermute | solution.py:86
  33.0 1.3 collective-permute-start.10
  54.1 55.2 %collective-permute-start.12 = (f32[1064,128]{1,0:T(8,128)S(1)}, f32[1064,128]{1,0:T(8,128)S(1)}, u32[]{:S(2)}, u32[]{:S(2)}) collective-permute-start(f32[1064,128]{1,0:T(8,128)S(1)} %get-tuple-element.15), channel_id=1, source_target_pairs={{0,1},{1,0},{2,3},{3,2},{4,5},{5,4},{6,7},{7,6},{8,9},{9,8},{10,11... | collective-permute-start | bytes 1634312 | tf_op jit(solution)/shard_map/ppermute | solution.py:90
  68.5 69.3 %collective-permute-start.17 = (f32[1792,128]{1,0:T(8,128)S(1)}, f32[1792,128]{1,0:T(8,128)S(1)}, u32[]{:S(2)}, u32[]{:S(2)}) collective-permute-start(f32[1792,128]{1,0:T(8,128)S(1)} %shard_map.53), channel_id=1, source_target_pairs={{0,1},{1,0},{2,3},{3,2},{4,5},{5,4},{6,7},{7,6},{8,9},{9,8},{10,11... | collective-permute-start | bytes 2752520 | tf_op jit(solution)/shard_map/ppermute | solution.py:90
  72.3 66.5 %collective-permute-start.18 = (f32[640,128]{1,0:T(8,128)S(1)}, f32[640,128]{1,0:T(8,128)S(1)}, u32[]{:S(2)}, u32[]{:S(2)}) collective-permute-start(f32[640,128]{1,0:T(8,128)S(1)} %shard_map.54), channel_id=1, source_target_pairs={{0,1},{1,0},{2,3},{3,2},{4,5},{5,4},{6,7},{7,6},{8,9},{9,8},{10,11... | collective-permute-start | bytes 983048 | tf_op jit(solution)/shard_map/ppermute | solution.py:90
  109.3 1.8 %collective-permute-start.13 = (f32[32,128]{1,0:T(8,128)S(1)}, f32[32,128]{1,0:T(8,128)S(1)}, u32[]{:S(2)}, u32[]{:S(2)}) collective-permute-start(f32[32,128]{1,0:T(8,128)S(1)} %slice.29), channel_id=1, source_target_pairs={{0,2},{2,0},{4,6},{6,4},{8,10},{10,8},{12,14},{14,12},{16,18},{18,... | collective-permute-start | bytes 49160 | tf_op jit(solution)/shard_map/ppermute | solution.py:86
  111.1 19.6 %collective-permute-start.14 = (f32[64,128]{1,0:T(8,128)S(1)}, f32[64,128]{1,0:T(8,128)S(1)}, u32[]{:S(2)}, u32[]{:S(2)}) collective-permute-start(f32[64,128]{1,0:T(8,128)S(1)} %pad_maximum_fusion.p0_ref), channel_id=1, source_target_pairs={{0,4},{2,6},{4,0},{6,2},{8,12},{10,14},{12,8},{14,10},{16,20},{18,... | collective-permute-start | bytes 98312 | tf_op jit(solution)/shard_map/ppermute | solution.py:86
  112.3 19.6 %collective-permute-start.15 = (f32[64,128]{1,0:T(8,128)S(1)}, f32[64,128]{1,0:T(8,128)S(1)}, u32[]{:S(2)}, u32[]{:S(2)}) collective-permute-start(f32[64,128]{1,0:T(8,128)S(1)} %pad_maximum_fusion.p0_ref), channel_id=1, source_target_pairs={{0,8},{2,10},{4,12},{6,14},{8,0},{10,2},{12,4},{14,6},{16,24},{18,... | collective-permute-start | bytes 98312 | tf_op jit(solution)/shard_map/ppermute | solution.py:86
  129.4 5.1 %collective-permute-start.16 = (f32[64,128]{1,0:T(8,128)S(1)}, f32[64,128]{1,0:T(8,128)S(1)}, u32[]{:S(2)}, u32[]{:S(2)}) collective-permute-start(f32[64,128]{1,0:T(8,128)S(1)} %pad_maximum_fusion.p0_ref), channel_id=1, source_target_pairs={{0,12},{2,14},{4,8},{6,10},{8,4},{10,6},{12,0},{14,2},{16,28},{18,... | collective-permute-start | bytes 98312 | tf_op jit(solution)/shard_map/ppermute | solution.py:86

commit v4 on v3

--- a/solution.py
+++ b/solution.py
@@ -2,6 +2,7 @@
 
 import jax
 import jax.numpy as jnp
+import numpy as np
 from jax import lax
 from jax.experimental import pallas as pl
 from jax.experimental.pallas import tpu as pltpu
@@ -15,10 +16,10 @@
 HIGHEST = lax.Precision.HIGHEST
 VMEM_LIMIT = 32 * 1024 * 1024
 ROWS = 4096
-RAW = 640
-CHUNKS = (1024, 1792, ROWS - RAW - 2816)
+RAW = 512
+CHUNKS = (1536 - RAW, 1792, 768)
 EXTRA = 40
-STEP = 256
+STEP = CHUNKS[0] // 4
 PACKED = 272
 PARTS = 4
 
@@ -110,29 +111,61 @@
     return (total, exchanged(total, 1)), raw_arrived
 
 
-def angles(g, d_top, d_bot):
+def meetings(step):
+    ring = WIDTH - 1
+    return [(step, ring)] + [((step + k) % ring, (step - k) % ring) for k in range(1, BLOCK)]
+
+
+def round_tables():
+    top, bottom = np.arange(BLOCK), WIDTH - 1 - np.arange(BLOCK)
+    table = np.zeros((ROUNDS, 8, BLOCK), np.int32)
+    table[:, 0] = np.arange(BLOCK)
+    for step in range(ROUNDS):
+        first = {i for i, _ in meetings(step)}
+        table[step, 2] = [t in first for t in top]
+        if step == ROUNDS - 1:
+            break
+        now, later = np.zeros(WIDTH, int), np.zeros(WIDTH, int)
+        for pairs, partner in ((meetings(step), now), (meetings(step + 1), later)):
+            for i, j in pairs:
+                partner[i], partner[j] = j, i
+        side = np.full(WIDTH, -1)
+        for member in range(WIDTH):
+            while side[member] < 0:
+                side[member], side[now[member]] = 0, 1
+                member = later[now[member]]
+        swap = side[top] == 1
+        table[step, 1] = swap
+        top, bottom = np.where(swap, bottom, top), np.where(swap, top, bottom)
+        lane = np.zeros(WIDTH, int)
+        lane[bottom] = np.arange(BLOCK)
+        table[step, 0] = lane[later[top]]
+        bottom = later[top]
+    last = np.concatenate([top, bottom]).astype(np.int32)
+    return table, np.repeat(last[:, None], BLOCK, axis=1)
+
+
+def angles(g, d_top, d_bot, top_first):
     diff = d_bot - d_top
-    sgn = jnp.where(diff >= 0, 1.0, -1.0)
+    double = jnp.where((diff > 0) | ((diff == 0) & top_first), 2.0 * g, -2.0 * g)
     den = jnp.abs(diff) + jnp.sqrt(diff * diff + 4.0 * g * g)
-    tang = jnp.where(den > 0, 2.0 * g * sgn / jnp.where(den > 0, den, 1.0), 0.0)
-    cosv = 1.0 / jnp.sqrt(1.0 + tang * tang)
+    tang = jnp.where(den > 0, double / jnp.where(den > 0, den, 1.0), 0.0)
+    cosv = lax.rsqrt(1.0 + tang * tang)
     return tang, cosv, tang * cosv
 
+
 def rounds_kernel(
-    ids_ref, mine_ref, other_ref, slab_ref, first_ref, leave_ref, stay_ref, diag_ref,
-    packed, vt, vb, wt, wb, x_ref, sem,
+    ids_ref, table_ref, last_ref, mine_ref, other_ref, slab_ref, first_ref, leave_ref, stay_ref, diag_ref,
+    packed, vt, vb, wt, wb, start_ref, x_ref, sem,
 ):
-    rounds = ROUNDS
     fetch = pltpu.make_async_copy(slab_ref.at[pl.ds(RAW, CHUNKS[0]), :], x_ref, sem)
     fetch.start()
     core, x = place()
-    swap = (ids_ref[1] <= ids_ref[0]).astype(jnp.int32)
+    swap_blocks = (ids_ref[1] <= ids_ref[0]).astype(jnp.int32)
     for h, part in enumerate((mine_ref, other_ref)):
         start = pl.multiple_of((core ^ h) * (PACKED // 2), 8)
         packed[pl.ds(start, PACKED // 2), :] = part[...]
-    half = 128
-    lane = lax.broadcasted_iota(jnp.int32, (8, half), 1)
-    first, last = lane == 0, lane == half - 1
+    half = BLOCK
     row = lax.broadcasted_iota(jnp.int32, (2 * half, half), 0)
     col = lax.broadcasted_iota(jnp.int32, (2 * half, half), 1)
     vt[...] = (row == col).astype(F32)
@@ -152,49 +185,57 @@
     anti = row[:half] == half - 1 - col[:half]
     d_bot = jnp.sum(jnp.where(anti, wb[128:256, :], 0.0), axis=0, keepdims=True)
     g = (jnp.sum(jnp.where(eye, wb[0:128, :], 0.0), axis=0, keepdims=True))
-    d_top, d_bot, g = (jnp.broadcast_to(v, (8, half)) for v in (d_top, d_bot, g))
-
-    def shifted(top, bot):
-        new_top = jnp.where(last, bot, pltpu.roll(top, half - 1, 1))
-        new_bot = jnp.where(first, bot, pltpu.roll(jnp.where(first, top, bot), 1, 1))
-        return new_top, new_bot
-
-    def one_round(_, state):
+    for n, v in enumerate((g, d_top, d_bot)):
+        start_ref[n] = jnp.broadcast_to(v, (8, half))
+
+    def one_round(step, state):
         g, d_top, d_bot = state
-        t, c, s = angles(g, d_top, d_bot)
-        d_top, d_bot = shifted(d_top - t * g, d_bot + t * g)
+        source, swap, top_first = (
+            jnp.broadcast_to(table_ref[step, n : n + 1, :], (8, half)) for n in range(3)
+        )
+        swap = swap > 0
+
+        def moved(bottom):
+            return jnp.take_along_axis(bottom, source, axis=1, mode="promise_in_bounds")
+
+        t, c, s = angles(g, d_top, d_bot, top_first > 0)
+        a, b = d_top - t * g, d_bot + t * g
+        d_top, d_bot = jnp.where(swap, b, a), moved(jnp.where(swap, a, b))
+        top_a, top_b = jnp.where(swap, s, c), jnp.where(swap, c, -s)
+        bot_a, bot_b = jnp.where(swap, c, s), jnp.where(swap, -s, c)
         acc = [jnp.zeros((8, half), F32) for _ in range(4)]
         for k in range(32):
             sl = pl.ds(8 * k, 8)
             a, b = vt[sl, :], vb[sl, :]
-            nvt, nvb = shifted(c * a - s * b, s * a + c * b)
-            vt[sl, :] = nvt
-            vb[sl, :] = nvb
+            new_vt = top_a * a + top_b * b
+            vt[sl, :] = new_vt
+            vb[sl, :] = moved(bot_a * a + bot_b * b)
             a, b = wt[sl, :], wb[sl, :]
-            nwt, nwb = shifted(c * a - s * b, s * a + c * b)
-            wt[sl, :] = nwt
-            wb[sl, :] = nwb
-            acc[k % 4] = acc[k % 4] + nvt * nwb
+            wt[sl, :] = top_a * a + top_b * b
+            new_wb = moved(bot_a * a + bot_b * b)
+            wb[sl, :] = new_wb
+            acc[k % 4] = acc[k % 4] + new_vt * new_wb
         g = jnp.sum((acc[0] + acc[1]) + (acc[2] + acc[3]), axis=0, keepdims=True)
         return jnp.broadcast_to(g, (8, half)), d_top, d_bot
 
-    g, d_top, d_bot = lax.fori_loop(0, rounds, one_round, (g, d_top, d_bot))
-    r = lax.broadcasted_iota(jnp.int32, (half, 2 * half), 0)
-    j = lax.broadcasted_iota(jnp.int32, (half, 2 * half), 1)
-    idx = jnp.where(swap > 0, jnp.where(j >= half, j - half, j + half), j)
-    p_top = (r + rounds == idx).astype(F32)
-    back = rounds - idx
-    back = jnp.where(idx == 2 * half - 1, 0, jnp.where(back <= 0, back + 255, back))
-    p_bot = ((r == back) & ((idx < rounds) | (idx >= rounds + half))).astype(F32)
+    g, d_top, d_bot = lax.fori_loop(0, ROUNDS, one_round, tuple(start_ref[n] for n in range(3)))
     dot = functools.partial(jnp.dot, precision=HIGHEST, preferred_element_type=F32)
-    rot = dot(vt[...], p_top) + dot(vb[...], p_bot)
+    lane = lax.broadcasted_iota(jnp.int32, (half, half), 1)
+    halves, diags = [], []
+    for n in range(2):
+        column = lane + half * (n ^ swap_blocks)
+        p_top = (last_ref[0:half, :] == column).astype(F32)
+        p_bot = (last_ref[half : 2 * half, :] == column).astype(F32)
+        halves.append(dot(vt[...], p_top) + dot(vb[...], p_bot))
+        diags.append(dot(d_top, p_top) + dot(d_bot, p_bot))
+    rot = jnp.concatenate(halves, axis=1)
     high = rot.astype(BF16)
     low = (rot - high.astype(F32)).astype(BF16)
     stay_ref[:, 0:128] = high[:, 0:128]
     stay_ref[:, 128:256] = low[:, 0:128]
     leave_ref[:, 0:128] = high[:, 128:256]
     leave_ref[:, 128:256] = low[:, 128:256]
-    diag = dot(d_top, p_top) + dot(d_bot, p_bot)
+    diag = jnp.concatenate(diags, axis=1)
     diag_ref[...] = diag
     wt[...] = rot[:, 128:256]
     piece = pl.ds(pl.multiple_of((2 * x + core) * 32, 32), 32)
@@ -222,6 +263,8 @@
             pl.BlockSpec(memory_space=pltpu.SMEM),
             in_vmem,
             in_vmem,
+            in_vmem,
+            in_vmem,
             pl.BlockSpec(memory_space=pl.ANY),
         ],
         out_specs=(in_vmem,) * 4,
@@ -234,12 +277,13 @@
         scratch_shapes=[pltpu.VMEM((PACKED, BLOCK), F32)]
         + [pltpu.VMEM((WIDTH, BLOCK), F32)] * 4
         + [
+            pltpu.VMEM((3, 8, BLOCK), F32),
             pltpu.VMEM((CHUNKS[0], WIDTH), F32),
             pltpu.SemaphoreType.DMA,
         ],
         compiler_params=pltpu.CompilerParams(vmem_limit_bytes=VMEM_LIMIT),
         cost_estimate=pl.CostEstimate(flops=0, bytes_accessed=0, transcendentals=0),
-    )(block_ids, *parts, pltpu.with_memory_space_constraint(slab, pltpu.HBM))
+    )(block_ids, *(jnp.asarray(t) for t in round_tables()), *parts, pltpu.with_memory_space_constraint(slab, pltpu.HBM))
 
 
 def cost(count):
@@ -252,7 +296,7 @@
     out_ref[...] = rotation(x_ref[...], rot_ref[...])
 
 
-def leaving(slab, rot, first, count, rows=128):
+def leaving(slab, rot, first, count, rows=256):
     return pl.pallas_call(
         rotate_kernel,
         grid=(count // rows,),
@@ -297,7 +341,7 @@
     out_ref[...] = rotation(x_ref[...], rot[...])
 
 
-def rotated_raw(raw, pieces, result, rows=128):
+def rotated_raw(raw, pieces, result, rows=RAW // 4):
     count = raw.shape[0]
     piece = pl.BlockSpec((64, BLOCK), lambda i: (0, 0))
     return pl.pallas_call(

time: 140 us -> 135 us (0.964)
  waiting for transfers between devices: 42.6 us -> 59.4 us
  starting transfers between devices: 49.4 us -> 35.8 us
  Pallas kernels: 39.4 us -> 30.6 us
    ppermute x4, waiting for transfers between devices: 29.6 us -> 47.1 us  [passed_along(): return lax.ppermute(array, 'pair', [(0, 1), (1, 0)])]
    ppermute x15, starting transfers between devices: 31 us -> 17.4 us  [exchanged(): return lax.ppermute(array, 'row', [(i, i ^ mask) for i in range(128)])]
    pallas_call x2, Pallas kernels: 11.3 us -> 7.12 us  [leaving(): pl.pallas_call(rotate_kernel, grid=(count // rows,), in_specs=[pl.BlockSp...]
    pallas_call x1, Pallas kernels: 14.2 us -> 10.1 us  [rounds_and_first_chunk(): pl.pallas_call(rounds_kernel, in_specs=[pl.BlockSpec(memory_space=pltpu.S...]
  transfers between devices with their start and end apart: 19 -> 19, of which waited for: 11 -> 13; matrix products, arithmetic and copies ran while one was open for 4% -> 4% of each run, Pallas kernels for 25% -> 20%
where the time goes in v4:
time: 135 us; the launch traced here: 134 us
  waiting for transfers between devices  59.4 us (44%)
  starting transfers between devices  35.8 us (27%)
  Pallas kernels  30.6 us (23%)
  local copies, waits for them, and re-layouts  4.21 us (3%)
  other arithmetic  2.51 us (2%)
  between operations  1.44 us (1%)
    ppermute x4, waiting for transfers between devices, passed_along(): return lax.ppermute(array, 'pair', [(0, 1), (1, 0)])  47.1 us
    ppermute x4, starting transfers between devices, passed_along(): return lax.ppermute(array, 'pair', [(0, 1), (1, 0)])  18.4 us
    ppermute x15, starting transfers between devices, exchanged(): return lax.ppermute(array, 'row', [(i, i ^ mask) for i in range(128)])  17.4 us
    ppermute x15, waiting for transfers between devices, exchanged(): return lax.ppermute(array, 'row', [(i, i ^ mask) for i in range(128)])  12.3 us
    pallas_call x1, Pallas kernels, rounds_and_first_chunk(): pl.pallas_call(rounds_kernel, in_specs=[pl.BlockSpec(memory_space=pltpu.S...  10.1 us
    pallas_call x1, Pallas kernels, staying(): pl.pallas_call(rotate_kernel, grid=(count // rows,), in_specs=[pl.BlockSp...  7.2 us
    pallas_call x2, Pallas kernels, leaving(): pl.pallas_call(rotate_kernel, grid=(count // rows,), in_specs=[pl.BlockSp...  7.12 us
    pallas_call x1, Pallas kernels, local_gram(): pl.pallas_call(gram_kernel, in_specs=[pl.BlockSpec(memory_space=pl.ANY)],...  4.32 us
  transfers between devices with their start and end apart: 19, of which 13 were waited for; matrix products, arithmetic and copies ran while one was open for 4% of the time, Pallas kernels for 20%

profile of v4, /device:TPU:56, one launch (start us, length us, event | category | flops | bytes accessed | tf_op | source)
XLA Modules:
  0.0 133.9 jit_solution(17097749520015353020)
XLA Ops:
  0.7 4.3 %shard_map.67 = f32[272,128]{1,0:T(8,128)S(1)} custom-call(f32[4096,256]{1,0:T(8,128)} %x_ref.5), custom_call_target="tpu_custom_call" | custom-call | tf_op jit(solution)/shard_map/pallas_call | solution.py:66
  5.1 1.2 collective-permute-done
  6.4 3.4 %collective-permute-start.1 = (f32[136,128]{1,0:T(8,128)S(1)}, f32[136,128]{1,0:T(8,128)S(1)}, u32[]{:S(2)}, u32[]{:S(2)}) collective-permute-start(f32[136,128]{1,0:T(8,128)S(1)} %dynamic-slice_add_fusion), channel_id=1, source_target_pairs={{0,128},{2,130},{4,132},{6,134},{8,136},{10,138},{12,140},{14,142}... | collective-permute-start | bytes 208904 | tf_op jit(solution)/shard_map/ppermute | solution.py:87
  11.5 1.8 %collective-permute-done.1 = f32[136,128]{1,0:T(8,128)S(1)} collective-permute-done((f32[136,128]{1,0:T(8,128)S(1)}, f32[136,128]{1,0:T(8,128)S(1)}, u32[]{:S(2)}, u32[]{:S(2)}) %collective-permute-start.1) | collective-permute-done | bytes 69664 | tf_op jit(solution)/shard_map/ppermute | solution.py:87
  15.5 3.1 %collective-permute-start.4 = (f32[136,128]{1,0:T(8,128)S(1)}, f32[136,128]{1,0:T(8,128)S(1)}, u32[]{:S(2)}, u32[]{:S(2)}) collective-permute-start(f32[136,128]{1,0:T(8,128)S(1)} %add_add_fusion.2), channel_id=1, source_target_pairs={{0,8},{2,10},{4,12},{6,14},{8,0},{10,2},{12,4},{14,6},{16,24},{18,... | collective-permute-start | bytes 208904 | tf_op jit(solution)/shard_map/ppermute | solution.py:87
  19.8 6.4 %collective-permute-start.11 = (f32[512,256]{1,0:T(8,128)S(1)}, f32[512,256]{1,0:T(8,128)S(1)}, u32[]{:S(2)}, u32[]{:S(2)}) collective-permute-start(f32[512,256]{1,0:T(8,128)S(1)} %slice.23), channel_id=1, source_target_pairs={{0,1},{1,0},{2,3},{3,2},{4,5},{5,4},{6,7},{7,6},{8,9},{9,8},{10,11... | collective-permute-start | bytes 1572872 | tf_op jit(solution)/shard_map/ppermute | solution.py:91
  26.2 1.3 collective-permute-start.7
  27.6 2.9 %collective-permute-start.9 = (f32[136,128]{1,0:T(8,128)S(1)}, f32[136,128]{1,0:T(8,128)S(1)}, u32[]{:S(2)}, u32[]{:S(2)}) collective-permute-start(f32[136,128]{1,0:T(8,128)S(1)} %add_add_fusion.1), channel_id=1, source_target_pairs={{0,48},{2,50},{4,52},{6,54},{8,56},{10,58},{12,60},{14,62},{16,32}... | collective-permute-start | bytes 208904 | tf_op jit(solution)/shard_map/ppermute | solution.py:87
  30.4 1.7 %collective-permute-done.7 = f32[136,128]{1,0:T(8,128)S(1)} collective-permute-done((f32[136,128]{1,0:T(8,128)S(1)}, f32[136,128]{1,0:T(8,128)S(1)}, u32[]{:S(2)}, u32[]{:S(2)}) %collective-permute-start.7) | collective-permute-done | bytes 69664 | tf_op jit(solution)/shard_map/ppermute | solution.py:87
  33.2 1.2 collective-permute-done.10.other_ref
  34.5 10.1 %shard_map.68 = (f32[1064,128]{1,0:T(8,128)S(1)}, bf16[256,256]{1,0:T(8,128)(2,1)S(1)}, bf16[256,256]{1,0:T(8,128)(2,1)S(1)}, f32[8,256]{1,0:T(8,128)S(1)}) custom-call(s32[2]{0:T(128)S(1)} %copy-done.2, s32[48,8,128]{2,1,0:T(8,128)S(1)} %copy-done, s32[256,128]{1,0:T(8,128)S(1)} %copy-done.1, f32[136,128]{1,0:T(8,128)S(1)} %add_add_fusion.mine_ref, ...), custom_call_target="tpu_custom_call" | custom-call | tf_op jit(solution)/shard_map/pallas_call | solution.py:260
  44.5 4.1 %collective-permute-done.11.x_ref = f32[512,256]{1,0:T(8,128)S(1)} collective-permute-done((f32[512,256]{1,0:T(8,128)S(1)}, f32[512,256]{1,0:T(8,128)S(1)}, u32[]{:S(2)}, u32[]{:S(2)}) %collective-permute-start.11) | collective-permute-done | bytes 524320 | tf_op jit(solution)/shard_map/ppermute | solution.py:91
  48.6 5.7 %collective-permute-start.12 = (f32[1064,128]{1,0:T(8,128)S(1)}, f32[1064,128]{1,0:T(8,128)S(1)}, u32[]{:S(2)}, u32[]{:S(2)}) collective-permute-start(f32[1064,128]{1,0:T(8,128)S(1)} %get-tuple-element.15), channel_id=1, source_target_pairs={{0,1},{1,0},{2,3},{3,2},{4,5},{5,4},{6,7},{7,6},{8,9},{9,8},{10,11... | collective-permute-start | bytes 1634312 | tf_op jit(solution)/shard_map/ppermute | solution.py:91
  54.9 4.7 %shard_map.71 = f32[1792,128]{1,0:T(8,128)S(1)} custom-call(f32[4096,256]{1,0:T(8,128)} %x_ref.5, bf16[256,256]{1,0:T(8,128)(2,1)S(1)} %get-tuple-element.17.rot_ref), custom_call_target="tpu_custom_call" | custom-call | flops 352321536 | bytes 2752512 | tf_op jit(solution)/shard_map/pallas_call | solution.py:300
  60.2 2.4 %shard_map.72 = f32[768,128]{1,0:T(8,128)S(1)} custom-call(f32[4096,256]{1,0:T(8,128)} %x_ref.5, bf16[256,256]{1,0:T(8,128)(2,1)S(1)} %get-tuple-element.17.rot_ref), custom_call_target="tpu_custom_call" | custom-call | flops 150994944 | bytes 1179648 | tf_op jit(solution)/shard_map/pallas_call | solution.py:300
  62.6 5.8 %collective-permute-start.18 = (f32[768,128]{1,0:T(8,128)S(1)}, f32[768,128]{1,0:T(8,128)S(1)}, u32[]{:S(2)}, u32[]{:S(2)}) collective-permute-start(f32[768,128]{1,0:T(8,128)S(1)} %shard_map.72), channel_id=1, source_target_pairs={{0,1},{1,0},{2,3},{3,2},{4,5},{5,4},{6,7},{7,6},{8,9},{9,8},{10,11... | collective-permute-start | bytes 1179656 | tf_op jit(solution)/shard_map/ppermute | solution.py:91
  68.4 7.2 %shard_map.69._ = f32[4096,256]{1,0:T(8,128)} custom-call(f32[4096,256]{1,0:T(8,128)} %x_ref.5, bf16[256,256]{1,0:T(8,128)(2,1)S(1)} %get-tuple-element.16.rot_ref), custom_call_target="tpu_custom_call" | custom-call | flops 805306368 | bytes 6291456 | tf_op jit(solution)/shard_map/pallas_call | solution.py:316
  75.6 29.6 %collective-permute-done.12 = f32[1064,128]{1,0:T(8,128)S(1)} collective-permute-done((f32[1064,128]{1,0:T(8,128)S(1)}, f32[1064,128]{1,0:T(8,128)S(1)}, u32[]{:S(2)}, u32[]{:S(2)}) %collective-permute-start.12) | collective-permute-done | bytes 544800 | tf_op jit(solution)/shard_map/ppermute | solution.py:91
  106.9 1.2 collective-permute-start.14
  108.2 2.7 %collective-permute-start.15 = (f32[64,128]{1,0:T(8,128)S(1)}, f32[64,128]{1,0:T(8,128)S(1)}, u32[]{:S(2)}, u32[]{:S(2)}) collective-permute-start(f32[64,128]{1,0:T(8,128)S(1)} %pad_maximum_fusion.p0_ref), channel_id=1, source_target_pairs={{0,8},{2,10},{4,12},{6,14},{8,0},{10,2},{12,4},{14,6},{16,24},{18,... | collective-permute-start | bytes 98312 | tf_op jit(solution)/shard_map/ppermute | solution.py:87
  113.6 2.4 %collective-permute-done.16.p3_ref = f32[64,128]{1,0:T(8,128)S(1)} collective-permute-done((f32[64,128]{1,0:T(8,128)S(1)}, f32[64,128]{1,0:T(8,128)S(1)}, u32[]{:S(2)}, u32[]{:S(2)}) %collective-permute-start.16) | collective-permute-done | bytes 32800 | tf_op jit(solution)/shard_map/ppermute | solution.py:87
  116.0 1.9 %shard_map.70 = f32[4096,256]{1,0:T(8,128)} custom-call(f32[512,256]{1,0:T(8,128)S(1)} %collective-permute-done.11.x_ref, f32[64,128]{1,0:T(8,128)S(1)} %pad_maximum_fusion.p0_ref, f32[64,128]{1,0:T(8,128)S(1)} %collective-permute-done.14.p1_ref, f32[64,128]{1,0:T(8,128)S(1)} %collective-permute-done.15.p2_ref, ...), custom_call_target="tpu_custom_call", output_to_operand_aliasing={{}: (5, {})} | custom-call | flops 100663296 | bytes 786432 | tf_op jit(solution)/shard_map/pallas_call | solution.py:347
  118.7 6.1 %collective-permute-done.17 = f32[1792,128]{1,0:T(8,128)S(1)} collective-permute-done((f32[1792,128]{1,0:T(8,128)S(1)}, f32[1792,128]{1,0:T(8,128)S(1)}, u32[]{:S(2)}, u32[]{:S(2)}) %collective-permute-start.17) | collective-permute-done | bytes 917536 | tf_op jit(solution)/shard_map/ppermute | solution.py:91
  125.8 7.3 %collective-permute-done.18 = f32[768,128]{1,0:T(8,128)S(1)} collective-permute-done((f32[768,128]{1,0:T(8,128)S(1)}, f32[768,128]{1,0:T(8,128)S(1)}, u32[]{:S(2)}, u32[]{:S(2)}) %collective-permute-start.18) | collective-permute-done | bytes 393248 | tf_op jit(solution)/shard_map/ppermute | solution.py:91
  (43 shorter events, 13.9 us)
Async XLA Ops:
  0.6 33.8 %copy-start = (s32[48,8,128]{2,1,0:T(8,128)S(1)}, s32[48,8,128]{2,1,0:T(8,128)}, u32[]{:S(2)}) copy-start(s32[48,8,128]{2,1,0:T(8,128)} %constant.33.clone.table_ref) | copy-start | bytes 589828
  0.6 33.8 %copy-start.1 = (s32[256,128]{1,0:T(8,128)S(1)}, s32[256,128]{1,0:T(8,128)}, u32[]{:S(2)}) copy-start(s32[256,128]{1,0:T(8,128)} %constant.34.clone.last_ref) | copy-start | bytes 393220
  0.7 33.8 %copy-start.2 = (s32[2]{0:T(128)S(1)}, s32[2]{0:T(128)}, u32[]{:S(2)}) copy-start(s32[2]{0:T(128)} %ids_ref.1) | copy-start | bytes 28
  5.0 1.3 %collective-permute-start = (f32[136,128]{1,0:T(8,128)S(1)}, f32[136,128]{1,0:T(8,128)S(1)}, u32[]{:S(2)}, u32[]{:S(2)}) collective-permute-start(f32[136,128]{1,0:T(8,128)S(1)} %constant_dynamic-slice_fusion), channel_id=1, source_target_pairs={{0,2},{2,0},{4,6},{6,4},{8,10},{10,8},{12,14},{14,12},{16,18},{18,... | collective-permute-start | bytes 208904 | tf_op jit(solution)/shard_map/ppermute | solution.py:87
  6.4 6.9 %collective-permute-start.1 = (f32[136,128]{1,0:T(8,128)S(1)}, f32[136,128]{1,0:T(8,128)S(1)}, u32[]{:S(2)}, u32[]{:S(2)}) collective-permute-start(f32[136,128]{1,0:T(8,128)S(1)} %dynamic-slice_add_fusion), channel_id=1, source_target_pairs={{0,128},{2,130},{4,132},{6,134},{8,136},{10,138},{12,140},{14,142}... | collective-permute-start | bytes 208904 | tf_op jit(solution)/shard_map/ppermute | solution.py:87
  9.7 4.7 %collective-permute-start.2 = (f32[136,128]{1,0:T(8,128)S(1)}, f32[136,128]{1,0:T(8,128)S(1)}, u32[]{:S(2)}, u32[]{:S(2)}) collective-permute-start(f32[136,128]{1,0:T(8,128)S(1)} %dynamic-slice_add_fusion), channel_id=1, source_target_pairs={{0,64},{2,66},{4,68},{6,70},{8,72},{10,74},{12,76},{14,78},{16,80}... | collective-permute-start | bytes 208904 | tf_op jit(solution)/shard_map/ppermute | solution.py:87
  9.9 5.7 %collective-permute-start.3 = (f32[136,128]{1,0:T(8,128)S(1)}, f32[136,128]{1,0:T(8,128)S(1)}, u32[]{:S(2)}, u32[]{:S(2)}) collective-permute-start(f32[136,128]{1,0:T(8,128)S(1)} %dynamic-slice_add_fusion), channel_id=1, source_target_pairs={{0,192},{2,194},{4,196},{6,198},{8,200},{10,202},{12,204},{14,206}... | collective-permute-start | bytes 208904 | tf_op jit(solution)/shard_map/ppermute | solution.py:87
  15.5 10.7 %collective-permute-start.4 = (f32[136,128]{1,0:T(8,128)S(1)}, f32[136,128]{1,0:T(8,128)S(1)}, u32[]{:S(2)}, u32[]{:S(2)}) collective-permute-start(f32[136,128]{1,0:T(8,128)S(1)} %add_add_fusion.2), channel_id=1, source_target_pairs={{0,8},{2,10},{4,12},{6,14},{8,0},{10,2},{12,4},{14,6},{16,24},{18,... | collective-permute-start | bytes 208904 | tf_op jit(solution)/shard_map/ppermute | solution.py:87
  18.7 7.6 %collective-permute-start.5 = (f32[136,128]{1,0:T(8,128)S(1)}, f32[136,128]{1,0:T(8,128)S(1)}, u32[]{:S(2)}, u32[]{:S(2)}) collective-permute-start(f32[136,128]{1,0:T(8,128)S(1)} %add_add_fusion.2), channel_id=1, source_target_pairs={{0,4},{2,6},{4,0},{6,2},{8,12},{10,14},{12,8},{14,10},{16,20},{18,... | collective-permute-start | bytes 208904 | tf_op jit(solution)/shard_map/ppermute | solution.py:87
  19.3 7.0 %collective-permute-start.6 = (f32[136,128]{1,0:T(8,128)S(1)}, f32[136,128]{1,0:T(8,128)S(1)}, u32[]{:S(2)}, u32[]{:S(2)}) collective-permute-start(f32[136,128]{1,0:T(8,128)S(1)} %add_add_fusion.2), channel_id=1, source_target_pairs={{0,12},{2,14},{4,8},{6,10},{8,4},{10,6},{12,0},{14,2},{16,28},{18,... | collective-permute-start | bytes 208904 | tf_op jit(solution)/shard_map/ppermute | solution.py:87
  19.8 28.8 %collective-permute-start.11 = (f32[512,256]{1,0:T(8,128)S(1)}, f32[512,256]{1,0:T(8,128)S(1)}, u32[]{:S(2)}, u32[]{:S(2)}) collective-permute-start(f32[512,256]{1,0:T(8,128)S(1)} %slice.23), channel_id=1, source_target_pairs={{0,1},{1,0},{2,3},{3,2},{4,5},{5,4},{6,7},{7,6},{8,9},{9,8},{10,11... | collective-permute-start | bytes 1572872 | tf_op jit(solution)/shard_map/ppermute | solution.py:91
  26.2 5.9 %collective-permute-start.7 = (f32[136,128]{1,0:T(8,128)S(1)}, f32[136,128]{1,0:T(8,128)S(1)}, u32[]{:S(2)}, u32[]{:S(2)}) collective-permute-start(f32[136,128]{1,0:T(8,128)S(1)} %add_add_fusion.1), channel_id=1, source_target_pairs={{0,32},{2,34},{4,36},{6,38},{8,40},{10,42},{12,44},{14,46},{16,48}... | collective-permute-start | bytes 208904 | tf_op jit(solution)/shard_map/ppermute | solution.py:87
  27.6 4.6 %collective-permute-start.8 = (f32[136,128]{1,0:T(8,128)S(1)}, f32[136,128]{1,0:T(8,128)S(1)}, u32[]{:S(2)}, u32[]{:S(2)}) collective-permute-start(f32[136,128]{1,0:T(8,128)S(1)} %add_add_fusion.1), channel_id=1, source_target_pairs={{0,16},{2,18},{4,20},{6,22},{8,24},{10,26},{12,28},{14,30},{16,0},... | collective-permute-start | bytes 208904 | tf_op jit(solution)/shard_map/ppermute | solution.py:87
  27.6 5.5 %collective-permute-start.9 = (f32[136,128]{1,0:T(8,128)S(1)}, f32[136,128]{1,0:T(8,128)S(1)}, u32[]{:S(2)}, u32[]{:S(2)}) collective-permute-start(f32[136,128]{1,0:T(8,128)S(1)} %add_add_fusion.1), channel_id=1, source_target_pairs={{0,48},{2,50},{4,52},{6,54},{8,56},{10,58},{12,60},{14,62},{16,32}... | collective-permute-start | bytes 208904 | tf_op jit(solution)/shard_map/ppermute | solution.py:87
  33.1 1.3 %collective-permute-start.10 = (f32[136,128]{1,0:T(8,128)S(1)}, f32[136,128]{1,0:T(8,128)S(1)}, u32[]{:S(2)}, u32[]{:S(2)}) collective-permute-start(f32[136,128]{1,0:T(8,128)S(1)} %add_add_fusion.mine_ref), channel_id=1, source_target_pairs={{0,2},{2,0},{4,6},{6,4},{8,10},{10,8},{12,14},{14,12},{16,18},{18,... | collective-permute-start | bytes 208904 | tf_op jit(solution)/shard_map/ppermute | solution.py:87
  48.6 56.6 %collective-permute-start.12 = (f32[1064,128]{1,0:T(8,128)S(1)}, f32[1064,128]{1,0:T(8,128)S(1)}, u32[]{:S(2)}, u32[]{:S(2)}) collective-permute-start(f32[1064,128]{1,0:T(8,128)S(1)} %get-tuple-element.15), channel_id=1, source_target_pairs={{0,1},{1,0},{2,3},{3,2},{4,5},{5,4},{6,7},{7,6},{8,9},{9,8},{10,11... | collective-permute-start | bytes 1634312 | tf_op jit(solution)/shard_map/ppermute | solution.py:91
  59.7 65.1 %collective-permute-start.17 = (f32[1792,128]{1,0:T(8,128)S(1)}, f32[1792,128]{1,0:T(8,128)S(1)}, u32[]{:S(2)}, u32[]{:S(2)}) collective-permute-start(f32[1792,128]{1,0:T(8,128)S(1)} %shard_map.71), channel_id=1, source_target_pairs={{0,1},{1,0},{2,3},{3,2},{4,5},{5,4},{6,7},{7,6},{8,9},{9,8},{10,11... | collective-permute-start | bytes 2752520 | tf_op jit(solution)/shard_map/ppermute | solution.py:91
  62.6 70.6 %collective-permute-start.18 = (f32[768,128]{1,0:T(8,128)S(1)}, f32[768,128]{1,0:T(8,128)S(1)}, u32[]{:S(2)}, u32[]{:S(2)}) collective-permute-start(f32[768,128]{1,0:T(8,128)S(1)} %shard_map.72), channel_id=1, source_target_pairs={{0,1},{1,0},{2,3},{3,2},{4,5},{5,4},{6,7},{7,6},{8,9},{9,8},{10,11... | collective-permute-start | bytes 1179656 | tf_op jit(solution)/shard_map/ppermute | solution.py:91
  105.2 1.8 %collective-permute-start.13 = (f32[32,128]{1,0:T(8,128)S(1)}, f32[32,128]{1,0:T(8,128)S(1)}, u32[]{:S(2)}, u32[]{:S(2)}) collective-permute-start(f32[32,128]{1,0:T(8,128)S(1)} %slice.29), channel_id=1, source_target_pairs={{0,2},{2,0},{4,6},{6,4},{8,10},{10,8},{12,14},{14,12},{16,18},{18,... | collective-permute-start | bytes 49160 | tf_op jit(solution)/shard_map/ppermute | solution.py:87
  106.9 6.0 %collective-permute-start.14 = (f32[64,128]{1,0:T(8,128)S(1)}, f32[64,128]{1,0:T(8,128)S(1)}, u32[]{:S(2)}, u32[]{:S(2)}) collective-permute-start(f32[64,128]{1,0:T(8,128)S(1)} %pad_maximum_fusion.p0_ref), channel_id=1, source_target_pairs={{0,4},{2,6},{4,0},{6,2},{8,12},{10,14},{12,8},{14,10},{16,20},{18,... | collective-permute-start | bytes 98312 | tf_op jit(solution)/shard_map/ppermute | solution.py:87
  108.2 5.4 %collective-permute-start.15 = (f32[64,128]{1,0:T(8,128)S(1)}, f32[64,128]{1,0:T(8,128)S(1)}, u32[]{:S(2)}, u32[]{:S(2)}) collective-permute-start(f32[64,128]{1,0:T(8,128)S(1)} %pad_maximum_fusion.p0_ref), channel_id=1, source_target_pairs={{0,8},{2,10},{4,12},{6,14},{8,0},{10,2},{12,4},{14,6},{16,24},{18,... | collective-permute-start | bytes 98312 | tf_op jit(solution)/shard_map/ppermute | solution.py:87
  110.9 5.1 %collective-permute-start.16 = (f32[64,128]{1,0:T(8,128)S(1)}, f32[64,128]{1,0:T(8,128)S(1)}, u32[]{:S(2)}, u32[]{:S(2)}) collective-permute-start(f32[64,128]{1,0:T(8,128)S(1)} %pad_maximum_fusion.p0_ref), channel_id=1, source_target_pairs={{0,12},{2,14},{4,8},{6,10},{8,4},{10,6},{12,0},{14,2},{16,28},{18,... | collective-permute-start | bytes 98312 | tf_op jit(solution)/shard_map/ppermute | solution.py:87

commit v5 on v4

--- a/solution.py
+++ b/solution.py
@@ -17,8 +17,8 @@
 VMEM_LIMIT = 32 * 1024 * 1024
 ROWS = 4096
 RAW = 512
-CHUNKS = (1536 - RAW, 1792, 768)
-EXTRA = 40
+CHUNKS = (1536 - RAW, 2304, 256)
+EXTRA = 16
 STEP = CHUNKS[0] // 4
 PACKED = 272
 PARTS = 4
@@ -80,7 +80,7 @@
 
 def place():
     me = lax.axis_index("row")
-    return me & 1, (me >> 1) & 3
+    return me & 1, (me >> 1) & 3, (me >> 3) & 3
 
 
 def exchanged(array, mask):
@@ -106,9 +106,10 @@
     yours = lax.dynamic_slice_in_dim(part, (1 - core) * half, half, 0)
     total = summed_over_four(mine + exchanged(yours, 1), 5)
     raw, total = lax.optimization_barrier((raw, total))
-    raw_arrived = passed_along(raw)
-    total = summed_over_four(summed_over_four(total, 1), 3)
-    return (total, exchanged(total, 1)), raw_arrived
+    raw = passed_along(raw)
+    total = summed_over_four(total, 1)
+    total = summed_over_four(total, 3)
+    return (total, exchanged(total, 1)), raw
 
 
 def meetings(step):
@@ -160,7 +161,7 @@
 ):
     fetch = pltpu.make_async_copy(slab_ref.at[pl.ds(RAW, CHUNKS[0]), :], x_ref, sem)
     fetch.start()
-    core, x = place()
+    core, x, y = place()
     swap_blocks = (ids_ref[1] <= ids_ref[0]).astype(jnp.int32)
     for h, part in enumerate((mine_ref, other_ref)):
         start = pl.multiple_of((core ^ h) * (PACKED // 2), 8)
@@ -238,11 +239,11 @@
     diag = jnp.concatenate(diags, axis=1)
     diag_ref[...] = diag
     wt[...] = rot[:, 128:256]
-    piece = pl.ds(pl.multiple_of((2 * x + core) * 32, 32), 32)
-    first_ref[CHUNKS[0] : CHUNKS[0] + 32, :] = wt[piece, :]
+    piece = pl.ds(pl.multiple_of(((4 * y + x) * 2 + core) * 8, 8), 8)
+    first_ref[CHUNKS[0] : CHUNKS[0] + 8, :] = wt[piece, :]
     label = jnp.full((8, half), jnp.maximum(ids_ref[0], ids_ref[1]).astype(F32))
     upper = lax.broadcasted_iota(jnp.int32, (8, half), 0) < 4
-    first_ref[CHUNKS[0] + 32 : CHUNKS[0] + 40, :] = jnp.where(upper, diag[:, 128:256], label)
+    first_ref[CHUNKS[0] + 8 : CHUNKS[0] + 16, :] = jnp.where(upper, diag[:, 128:256], label)
     fetch.wait()
     for start in range(0, CHUNKS[0], STEP):
         first_ref[start : start + STEP, :] = rotation(x_ref[start : start + STEP, :], leave_ref[...])
@@ -331,9 +332,10 @@
     @pl.when(pl.program_id(0) == 0)
     def _():
         for d, piece in enumerate((p0_ref, p1_ref, p2_ref, p3_ref)):
-            for h in range(2):
-                start = (2 * (place()[1] ^ d) + (place()[0] ^ h)) * 32
-                full[pl.ds(pl.multiple_of(start, 32), 32), :] = piece[32 * h : 32 * h + 32, :]
+            core, x, y = place()
+            for n in range(8):
+                start = ((4 * (y ^ d) + (x ^ (n >> 1))) * 2 + (core ^ (n & 1))) * 8
+                full[pl.ds(pl.multiple_of(start, 8), 8), :] = piece[8 * n : 8 * n + 8, :]
         high = full[...].astype(BF16)
         rot[:, 0:128] = high
         rot[:, 128:256] = (full[...] - high.astype(F32)).astype(BF16)
@@ -365,7 +367,7 @@
 
 
 def per_device(slab, block_ids):
-    core, _ = place()
+    core, _, _ = place()
     parts, raw = summed_over_rows(local_gram(slab), core, slab[:RAW])
     first, rot_leave, rot_stay, diag = rounds_and_first_chunk(parts, slab, block_ids)
     first, raw = lax.optimization_barrier((first, raw))
@@ -375,14 +377,15 @@
     for start, count in zip(starts[1:], CHUNKS[1:]):
         arrived.append(passed_along(leaving(slab, rot_leave, start, count)))
     new_slab = staying(slab, rot_stay)
-    both = jnp.concatenate([extra[:32], exchanged(extra[:32], 1)])
-    new_slab = rotated_raw(raw, with_three_others(both, 1), new_slab)
+    both = jnp.concatenate([extra[:8], exchanged(extra[:8], 1)])
+    eight = jnp.concatenate(with_three_others(both, 1))
+    new_slab = rotated_raw(raw, with_three_others(eight, 3), new_slab)
     for start, count, chunk in zip(starts, CHUNKS, arrived):
         new_slab = lax.dynamic_update_slice(new_slab, chunk[:count], (start, BLOCK))
     total_rows = slab.shape[0] * lax.axis_size("row")
-    squares = jnp.concatenate([diag[0, :BLOCK], extra[32]])
+    squares = jnp.concatenate([diag[0, :BLOCK], extra[8]])
     col_norms = jnp.sqrt(jnp.maximum(squares, 0.0) / total_rows)
-    new_ids = jnp.stack([jnp.min(block_ids), extra[36, 0].astype(jnp.int32)])
+    new_ids = jnp.stack([jnp.min(block_ids), extra[12, 0].astype(jnp.int32)])
     return (new_slab, col_norms, new_ids)
 
 

time: 135 us -> 135 us (level)
  waiting for transfers between devices: 59.4 us -> 53.9 us
  starting transfers between devices: 35.8 us -> 40.5 us
    ppermute x4, waiting for transfers between devices: 47.1 us -> 38.9 us  [passed_along(): return lax.ppermute(array, 'pair', [(0, 1), (1, 0)])]
    ppermute x15 -> x18, starting transfers between devices: 17.4 us -> 22.1 us  [exchanged(): return lax.ppermute(array, 'row', [(i, i ^ mask) for i in range(128)])]
    ppermute x15 -> x18, waiting for transfers between devices: 12.3 us -> 15 us  [exchanged(): return lax.ppermute(array, 'row', [(i, i ^ mask) for i in range(128)])]
  transfers between devices with their start and end apart: 19 -> 22, of which waited for: 13 -> 15; matrix products, arithmetic and copies ran while one was open for 4% -> 5% of each run, Pallas kernels for 20% -> 20%
where the time goes in v5:
time: 135 us; the launch traced here: 133 us
  waiting for transfers between devices  53.9 us (40%)
  starting transfers between devices  40.5 us (30%)
  Pallas kernels  30.6 us (23%)
  local copies, waits for them, and re-layouts  4.21 us (3%)
  other arithmetic  2.64 us (2%)
  between operations  1.44 us (1%)
    ppermute x4, waiting for transfers between devices, passed_along(): return lax.ppermute(array, 'pair', [(0, 1), (1, 0)])  38.9 us
    ppermute x18, starting transfers between devices, exchanged(): return lax.ppermute(array, 'row', [(i, i ^ mask) for i in range(128)])  22.1 us
    ppermute x4, starting transfers between devices, passed_along(): return lax.ppermute(array, 'pair', [(0, 1), (1, 0)])  18.4 us
    ppermute x18, waiting for transfers between devices, exchanged(): return lax.ppermute(array, 'row', [(i, i ^ mask) for i in range(128)])  15 us
    pallas_call x1, Pallas kernels, rounds_and_first_chunk(): pl.pallas_call(rounds_kernel, in_specs=[pl.BlockSpec(memory_space=pltpu.S...  10.1 us
    pallas_call x1, Pallas kernels, staying(): pl.pallas_call(rotate_kernel, grid=(count // rows,), in_specs=[pl.BlockSp...  7.18 us
    pallas_call x2, Pallas kernels, leaving(): pl.pallas_call(rotate_kernel, grid=(count // rows,), in_specs=[pl.BlockSp...  7.12 us
    pallas_call x1, Pallas kernels, local_gram(): pl.pallas_call(gram_kernel, in_specs=[pl.BlockSpec(memory_space=pl.ANY)],...  4.32 us
  transfers between devices with their start and end apart: 22, of which 15 were waited for; matrix products, arithmetic and copies ran while one was open for 5% of the time, Pallas kernels for 20%

profile of v5, /device:TPU:56, one launch (start us, length us, event | category | flops | bytes accessed | tf_op | source)
XLA Modules:
  0.0 133.3 jit_solution(5342739219814974470)
XLA Ops:
  0.7 4.3 %shard_map.67 = f32[272,128]{1,0:T(8,128)S(1)} custom-call(f32[4096,256]{1,0:T(8,128)} %x_ref.5), custom_call_target="tpu_custom_call" | custom-call | tf_op jit(solution)/shard_map/pallas_call | solution.py:66
  6.4 3.4 %collective-permute-start.1 = (f32[136,128]{1,0:T(8,128)S(1)}, f32[136,128]{1,0:T(8,128)S(1)}, u32[]{:S(2)}, u32[]{:S(2)}) collective-permute-start(f32[136,128]{1,0:T(8,128)S(1)} %dynamic-slice_add_fusion), channel_id=1, source_target_pairs={{0,128},{2,130},{4,132},{6,134},{8,136},{10,138},{12,140},{14,142}... | collective-permute-start | bytes 208904 | tf_op jit(solution)/shard_map/ppermute | solution.py:87
  11.5 1.8 %collective-permute-done.1 = f32[136,128]{1,0:T(8,128)S(1)} collective-permute-done((f32[136,128]{1,0:T(8,128)S(1)}, f32[136,128]{1,0:T(8,128)S(1)}, u32[]{:S(2)}, u32[]{:S(2)}) %collective-permute-start.1) | collective-permute-done | bytes 69664 | tf_op jit(solution)/shard_map/ppermute | solution.py:87
  15.5 3.1 %collective-permute-start.4 = (f32[136,128]{1,0:T(8,128)S(1)}, f32[136,128]{1,0:T(8,128)S(1)}, u32[]{:S(2)}, u32[]{:S(2)}) collective-permute-start(f32[136,128]{1,0:T(8,128)S(1)} %add_add_fusion.2), channel_id=1, source_target_pairs={{0,8},{2,10},{4,12},{6,14},{8,0},{10,2},{12,4},{14,6},{16,24},{18,... | collective-permute-start | bytes 208904 | tf_op jit(solution)/shard_map/ppermute | solution.py:87
  19.8 6.4 %collective-permute-start.11 = (f32[512,256]{1,0:T(8,128)S(1)}, f32[512,256]{1,0:T(8,128)S(1)}, u32[]{:S(2)}, u32[]{:S(2)}) collective-permute-start(f32[512,256]{1,0:T(8,128)S(1)} %slice.23), channel_id=1, source_target_pairs={{0,1},{1,0},{2,3},{3,2},{4,5},{5,4},{6,7},{7,6},{8,9},{9,8},{10,11... | collective-permute-start | bytes 1572872 | tf_op jit(solution)/shard_map/ppermute | solution.py:91
  26.2 1.3 collective-permute-start.7
  27.6 2.9 %collective-permute-start.9 = (f32[136,128]{1,0:T(8,128)S(1)}, f32[136,128]{1,0:T(8,128)S(1)}, u32[]{:S(2)}, u32[]{:S(2)}) collective-permute-start(f32[136,128]{1,0:T(8,128)S(1)} %add_add_fusion.1), channel_id=1, source_target_pairs={{0,48},{2,50},{4,52},{6,54},{8,56},{10,58},{12,60},{14,62},{16,32}... | collective-permute-start | bytes 208904 | tf_op jit(solution)/shard_map/ppermute | solution.py:87
  30.4 1.7 %collective-permute-done.7 = f32[136,128]{1,0:T(8,128)S(1)} collective-permute-done((f32[136,128]{1,0:T(8,128)S(1)}, f32[136,128]{1,0:T(8,128)S(1)}, u32[]{:S(2)}, u32[]{:S(2)}) %collective-permute-start.7) | collective-permute-done | bytes 69664 | tf_op jit(solution)/shard_map/ppermute | solution.py:87
  34.5 10.1 %shard_map.68 = (f32[1040,128]{1,0:T(8,128)S(1)}, bf16[256,256]{1,0:T(8,128)(2,1)S(1)}, bf16[256,256]{1,0:T(8,128)(2,1)S(1)}, f32[8,256]{1,0:T(8,128)S(1)}) custom-call(s32[2]{0:T(128)S(1)} %copy-done.2, s32[48,8,128]{2,1,0:T(8,128)S(1)} %copy-done, s32[256,128]{1,0:T(8,128)S(1)} %copy-done.1, f32[136,128]{1,0:T(8,128)S(1)} %add_add_fusion.mine_ref, ...), custom_call_target="tpu_custom_call" | custom-call | tf_op jit(solution)/shard_map/pallas_call | solution.py:261
  44.5 4.1 %collective-permute-done.11.x_ref = f32[512,256]{1,0:T(8,128)S(1)} collective-permute-done((f32[512,256]{1,0:T(8,128)S(1)}, f32[512,256]{1,0:T(8,128)S(1)}, u32[]{:S(2)}, u32[]{:S(2)}) %collective-permute-start.11) | collective-permute-done | bytes 524320 | tf_op jit(solution)/shard_map/ppermute | solution.py:91
  48.6 5.7 %collective-permute-start.12 = (f32[1040,128]{1,0:T(8,128)S(1)}, f32[1040,128]{1,0:T(8,128)S(1)}, u32[]{:S(2)}, u32[]{:S(2)}) collective-permute-start(f32[1040,128]{1,0:T(8,128)S(1)} %get-tuple-element.15), channel_id=1, source_target_pairs={{0,1},{1,0},{2,3},{3,2},{4,5},{5,4},{6,7},{7,6},{8,9},{9,8},{10,11... | collective-permute-start | bytes 1597448 | tf_op jit(solution)/shard_map/ppermute | solution.py:91
  55.0 5.9 %shard_map.71 = f32[2304,128]{1,0:T(8,128)S(1)} custom-call(f32[4096,256]{1,0:T(8,128)} %x_ref.5, bf16[256,256]{1,0:T(8,128)(2,1)S(1)} %get-tuple-element.17.rot_ref), custom_call_target="tpu_custom_call" | custom-call | flops 452984832 | bytes 3538944 | tf_op jit(solution)/shard_map/pallas_call | solution.py:301
  62.6 5.8 %collective-permute-start.21 = (f32[256,128]{1,0:T(8,128)S(1)}, f32[256,128]{1,0:T(8,128)S(1)}, u32[]{:S(2)}, u32[]{:S(2)}) collective-permute-start(f32[256,128]{1,0:T(8,128)S(1)} %shard_map.72), channel_id=1, source_target_pairs={{0,1},{1,0},{2,3},{3,2},{4,5},{5,4},{6,7},{7,6},{8,9},{9,8},{10,11... | collective-permute-start | bytes 393224 | tf_op jit(solution)/shard_map/ppermute | solution.py:91
  68.4 7.2 %shard_map.69._ = f32[4096,256]{1,0:T(8,128)} custom-call(f32[4096,256]{1,0:T(8,128)} %x_ref.5, bf16[256,256]{1,0:T(8,128)(2,1)S(1)} %get-tuple-element.16.rot_ref), custom_call_target="tpu_custom_call" | custom-call | flops 805306368 | bytes 6291456 | tf_op jit(solution)/shard_map/pallas_call | solution.py:317
  75.6 29.0 %collective-permute-done.12 = f32[1040,128]{1,0:T(8,128)S(1)} collective-permute-done((f32[1040,128]{1,0:T(8,128)S(1)}, f32[1040,128]{1,0:T(8,128)S(1)}, u32[]{:S(2)}, u32[]{:S(2)}) %collective-permute-start.12) | collective-permute-done | bytes 532512 | tf_op jit(solution)/shard_map/ppermute | solution.py:91
  107.6 2.7 %collective-permute-start.15 = (f32[16,128]{1,0:T(8,128)S(1)}, f32[16,128]{1,0:T(8,128)S(1)}, u32[]{:S(2)}, u32[]{:S(2)}) collective-permute-start(f32[16,128]{1,0:T(8,128)S(1)} %pad_maximum_fusion), channel_id=1, source_target_pairs={{0,8},{2,10},{4,12},{6,14},{8,0},{10,2},{12,4},{14,6},{16,24},{18,... | collective-permute-start | bytes 24584 | tf_op jit(solution)/shard_map/ppermute | solution.py:87
  111.2 1.6 %collective-permute-done.15 = f32[16,128]{1,0:T(8,128)S(1)} collective-permute-done((f32[16,128]{1,0:T(8,128)S(1)}, f32[16,128]{1,0:T(8,128)S(1)}, u32[]{:S(2)}, u32[]{:S(2)}) %collective-permute-start.15) | collective-permute-done | bytes 8224 | tf_op jit(solution)/shard_map/ppermute | solution.py:87
  112.8 2.4 %collective-permute-done.16 = f32[16,128]{1,0:T(8,128)S(1)} collective-permute-done((f32[16,128]{1,0:T(8,128)S(1)}, f32[16,128]{1,0:T(8,128)S(1)}, u32[]{:S(2)}, u32[]{:S(2)}) %collective-permute-start.16) | collective-permute-done | bytes 8224 | tf_op jit(solution)/shard_map/ppermute | solution.py:87
  116.0 1.9 %collective-permute-start.18 = (f32[64,128]{1,0:T(8,128)S(1)}, f32[64,128]{1,0:T(8,128)S(1)}, u32[]{:S(2)}, u32[]{:S(2)}) collective-permute-start(f32[64,128]{1,0:T(8,128)S(1)} %constant_dynamic-update-slice_fusion.p0_ref), channel_id=1, source_target_pairs={{0,32},{2,34},{4,36},{6,38},{8,40},{10,42},{12,44},{14,46},{16,48}... | collective-permute-start | bytes 98312 | tf_op jit(solution)/shard_map/ppermute | solution.py:87
  117.9 2.0 %collective-permute-start.19 = (f32[64,128]{1,0:T(8,128)S(1)}, f32[64,128]{1,0:T(8,128)S(1)}, u32[]{:S(2)}, u32[]{:S(2)}) collective-permute-start(f32[64,128]{1,0:T(8,128)S(1)} %constant_dynamic-update-slice_fusion.p0_ref), channel_id=1, source_target_pairs={{0,48},{2,50},{4,52},{6,54},{8,56},{10,58},{12,60},{14,62},{16,32}... | collective-permute-start | bytes 98312 | tf_op jit(solution)/shard_map/ppermute | solution.py:87
  121.4 1.6 %collective-permute-done.19.p3_ref = f32[64,128]{1,0:T(8,128)S(1)} collective-permute-done((f32[64,128]{1,0:T(8,128)S(1)}, f32[64,128]{1,0:T(8,128)S(1)}, u32[]{:S(2)}, u32[]{:S(2)}) %collective-permute-start.19) | collective-permute-done | bytes 32800 | tf_op jit(solution)/shard_map/ppermute | solution.py:87
  123.0 1.9 %shard_map.70 = f32[4096,256]{1,0:T(8,128)} custom-call(f32[512,256]{1,0:T(8,128)S(1)} %collective-permute-done.11.x_ref, f32[64,128]{1,0:T(8,128)S(1)} %constant_dynamic-update-slice_fusion.p0_ref, f32[64,128]{1,0:T(8,128)S(1)} %collective-permute-done.17.p1_ref, f32[64,128]{1,0:T(8,128)S(1)} %collective-permute-done.18.p2_ref, ...), custom_call_target="tpu_custom_call", output_to_operand_aliasing={{}: (5, {})} | custom-call | flops 100663296 | bytes 786432 | tf_op jit(solution)/shard_map/pallas_call | solution.py:349
  125.7 4.2 %collective-permute-done.20 = f32[2304,128]{1,0:T(8,128)S(1)} collective-permute-done((f32[2304,128]{1,0:T(8,128)S(1)}, f32[2304,128]{1,0:T(8,128)S(1)}, u32[]{:S(2)}, u32[]{:S(2)}) %collective-permute-start.20) | collective-permute-done | bytes 1179680 | tf_op jit(solution)/shard_map/ppermute | solution.py:91
  131.0 1.6 %collective-permute-done.21 = f32[256,128]{1,0:T(8,128)S(1)} collective-permute-done((f32[256,128]{1,0:T(8,128)S(1)}, f32[256,128]{1,0:T(8,128)S(1)}, u32[]{:S(2)}, u32[]{:S(2)}) %collective-permute-start.21) | collective-permute-done | bytes 131104 | tf_op jit(solution)/shard_map/ppermute | solution.py:91
  (53 shorter events, 19.2 us)
Async XLA Ops:
  0.6 33.8 %copy-start = (s32[48,8,128]{2,1,0:T(8,128)S(1)}, s32[48,8,128]{2,1,0:T(8,128)}, u32[]{:S(2)}) copy-start(s32[48,8,128]{2,1,0:T(8,128)} %constant.33.clone.table_ref) | copy-start | bytes 589828
  0.6 33.8 %copy-start.1 = (s32[256,128]{1,0:T(8,128)S(1)}, s32[256,128]{1,0:T(8,128)}, u32[]{:S(2)}) copy-start(s32[256,128]{1,0:T(8,128)} %constant.34.clone.last_ref) | copy-start | bytes 393220
  5.0 1.3 %collective-permute-start = (f32[136,128]{1,0:T(8,128)S(1)}, f32[136,128]{1,0:T(8,128)S(1)}, u32[]{:S(2)}, u32[]{:S(2)}) collective-permute-start(f32[136,128]{1,0:T(8,128)S(1)} %constant_dynamic-slice_fusion), channel_id=1, source_target_pairs={{0,2},{2,0},{4,6},{6,4},{8,10},{10,8},{12,14},{14,12},{16,18},{18,... | collective-permute-start | bytes 208904 | tf_op jit(solution)/shard_map/ppermute | solution.py:87
  6.4 6.9 %collective-permute-start.1 = (f32[136,128]{1,0:T(8,128)S(1)}, f32[136,128]{1,0:T(8,128)S(1)}, u32[]{:S(2)}, u32[]{:S(2)}) collective-permute-start(f32[136,128]{1,0:T(8,128)S(1)} %dynamic-slice_add_fusion), channel_id=1, source_target_pairs={{0,128},{2,130},{4,132},{6,134},{8,136},{10,138},{12,140},{14,142}... | collective-permute-start | bytes 208904 | tf_op jit(solution)/shard_map/ppermute | solution.py:87
  9.7 4.7 %collective-permute-start.2 = (f32[136,128]{1,0:T(8,128)S(1)}, f32[136,128]{1,0:T(8,128)S(1)}, u32[]{:S(2)}, u32[]{:S(2)}) collective-permute-start(f32[136,128]{1,0:T(8,128)S(1)} %dynamic-slice_add_fusion), channel_id=1, source_target_pairs={{0,64},{2,66},{4,68},{6,70},{8,72},{10,74},{12,76},{14,78},{16,80}... | collective-permute-start | bytes 208904 | tf_op jit(solution)/shard_map/ppermute | solution.py:87
  9.9 5.7 %collective-permute-start.3 = (f32[136,128]{1,0:T(8,128)S(1)}, f32[136,128]{1,0:T(8,128)S(1)}, u32[]{:S(2)}, u32[]{:S(2)}) collective-permute-start(f32[136,128]{1,0:T(8,128)S(1)} %dynamic-slice_add_fusion), channel_id=1, source_target_pairs={{0,192},{2,194},{4,196},{6,198},{8,200},{10,202},{12,204},{14,206}... | collective-permute-start | bytes 208904 | tf_op jit(solution)/shard_map/ppermute | solution.py:87
  15.5 10.7 %collective-permute-start.4 = (f32[136,128]{1,0:T(8,128)S(1)}, f32[136,128]{1,0:T(8,128)S(1)}, u32[]{:S(2)}, u32[]{:S(2)}) collective-permute-start(f32[136,128]{1,0:T(8,128)S(1)} %add_add_fusion.2), channel_id=1, source_target_pairs={{0,8},{2,10},{4,12},{6,14},{8,0},{10,2},{12,4},{14,6},{16,24},{18,... | collective-permute-start | bytes 208904 | tf_op jit(solution)/shard_map/ppermute | solution.py:87
  18.7 7.6 %collective-permute-start.5 = (f32[136,128]{1,0:T(8,128)S(1)}, f32[136,128]{1,0:T(8,128)S(1)}, u32[]{:S(2)}, u32[]{:S(2)}) collective-permute-start(f32[136,128]{1,0:T(8,128)S(1)} %add_add_fusion.2), channel_id=1, source_target_pairs={{0,4},{2,6},{4,0},{6,2},{8,12},{10,14},{12,8},{14,10},{16,20},{18,... | collective-permute-start | bytes 208904 | tf_op jit(solution)/shard_map/ppermute | solution.py:87
  19.3 7.0 %collective-permute-start.6 = (f32[136,128]{1,0:T(8,128)S(1)}, f32[136,128]{1,0:T(8,128)S(1)}, u32[]{:S(2)}, u32[]{:S(2)}) collective-permute-start(f32[136,128]{1,0:T(8,128)S(1)} %add_add_fusion.2), channel_id=1, source_target_pairs={{0,12},{2,14},{4,8},{6,10},{8,4},{10,6},{12,0},{14,2},{16,28},{18,... | collective-permute-start | bytes 208904 | tf_op jit(solution)/shard_map/ppermute | solution.py:87
  19.8 28.8 %collective-permute-start.11 = (f32[512,256]{1,0:T(8,128)S(1)}, f32[512,256]{1,0:T(8,128)S(1)}, u32[]{:S(2)}, u32[]{:S(2)}) collective-permute-start(f32[512,256]{1,0:T(8,128)S(1)} %slice.23), channel_id=1, source_target_pairs={{0,1},{1,0},{2,3},{3,2},{4,5},{5,4},{6,7},{7,6},{8,9},{9,8},{10,11... | collective-permute-start | bytes 1572872 | tf_op jit(solution)/shard_map/ppermute | solution.py:91
  26.2 5.9 %collective-permute-start.7 = (f32[136,128]{1,0:T(8,128)S(1)}, f32[136,128]{1,0:T(8,128)S(1)}, u32[]{:S(2)}, u32[]{:S(2)}) collective-permute-start(f32[136,128]{1,0:T(8,128)S(1)} %add_add_fusion.1), channel_id=1, source_target_pairs={{0,32},{2,34},{4,36},{6,38},{8,40},{10,42},{12,44},{14,46},{16,48}... | collective-permute-start | bytes 208904 | tf_op jit(solution)/shard_map/ppermute | solution.py:87
  27.6 4.6 %collective-permute-start.8 = (f32[136,128]{1,0:T(8,128)S(1)}, f32[136,128]{1,0:T(8,128)S(1)}, u32[]{:S(2)}, u32[]{:S(2)}) collective-permute-start(f32[136,128]{1,0:T(8,128)S(1)} %add_add_fusion.1), channel_id=1, source_target_pairs={{0,16},{2,18},{4,20},{6,22},{8,24},{10,26},{12,28},{14,30},{16,0},... | collective-permute-start | bytes 208904 | tf_op jit(solution)/shard_map/ppermute | solution.py:87
  27.6 5.5 %collective-permute-start.9 = (f32[136,128]{1,0:T(8,128)S(1)}, f32[136,128]{1,0:T(8,128)S(1)}, u32[]{:S(2)}, u32[]{:S(2)}) collective-permute-start(f32[136,128]{1,0:T(8,128)S(1)} %add_add_fusion.1), channel_id=1, source_target_pairs={{0,48},{2,50},{4,52},{6,54},{8,56},{10,58},{12,60},{14,62},{16,32}... | collective-permute-start | bytes 208904 | tf_op jit(solution)/shard_map/ppermute | solution.py:87
  33.1 1.3 %collective-permute-start.10 = (f32[136,128]{1,0:T(8,128)S(1)}, f32[136,128]{1,0:T(8,128)S(1)}, u32[]{:S(2)}, u32[]{:S(2)}) collective-permute-start(f32[136,128]{1,0:T(8,128)S(1)} %add_add_fusion.mine_ref), channel_id=1, source_target_pairs={{0,2},{2,0},{4,6},{6,4},{8,10},{10,8},{12,14},{14,12},{16,18},{18,... | collective-permute-start | bytes 208904 | tf_op jit(solution)/shard_map/ppermute | solution.py:87
  48.6 56.0 %collective-permute-start.12 = (f32[1040,128]{1,0:T(8,128)S(1)}, f32[1040,128]{1,0:T(8,128)S(1)}, u32[]{:S(2)}, u32[]{:S(2)}) collective-permute-start(f32[1040,128]{1,0:T(8,128)S(1)} %get-tuple-element.15), channel_id=1, source_target_pairs={{0,1},{1,0},{2,3},{3,2},{4,5},{5,4},{6,7},{7,6},{8,9},{9,8},{10,11... | collective-permute-start | bytes 1597448 | tf_op jit(solution)/shard_map/ppermute | solution.py:91
  61.0 69.0 %collective-permute-start.20 = (f32[2304,128]{1,0:T(8,128)S(1)}, f32[2304,128]{1,0:T(8,128)S(1)}, u32[]{:S(2)}, u32[]{:S(2)}) collective-permute-start(f32[2304,128]{1,0:T(8,128)S(1)} %shard_map.71), channel_id=1, source_target_pairs={{0,1},{1,0},{2,3},{3,2},{4,5},{5,4},{6,7},{7,6},{8,9},{9,8},{10,11... | collective-permute-start | bytes 3538952 | tf_op jit(solution)/shard_map/ppermute | solution.py:91
  62.6 70.0 %collective-permute-start.21 = (f32[256,128]{1,0:T(8,128)S(1)}, f32[256,128]{1,0:T(8,128)S(1)}, u32[]{:S(2)}, u32[]{:S(2)}) collective-permute-start(f32[256,128]{1,0:T(8,128)S(1)} %shard_map.72), channel_id=1, source_target_pairs={{0,1},{1,0},{2,3},{3,2},{4,5},{5,4},{6,7},{7,6},{8,9},{9,8},{10,11... | collective-permute-start | bytes 393224 | tf_op jit(solution)/shard_map/ppermute | solution.py:91
  104.6 1.8 %collective-permute-start.13 = (f32[8,128]{1,0:T(8,128)S(1)}, f32[8,128]{1,0:T(8,128)S(1)}, u32[]{:S(2)}, u32[]{:S(2)}) collective-permute-start(f32[8,128]{1,0:T(8,128)S(1)} %get-tuple-element.19), channel_id=1, source_target_pairs={{0,2},{2,0},{4,6},{6,4},{8,10},{10,8},{12,14},{14,12},{16,18},{18,... | collective-permute-start | bytes 12296 | tf_op jit(solution)/shard_map/ppermute | solution.py:87
  106.4 4.8 %collective-permute-start.14 = (f32[16,128]{1,0:T(8,128)S(1)}, f32[16,128]{1,0:T(8,128)S(1)}, u32[]{:S(2)}, u32[]{:S(2)}) collective-permute-start(f32[16,128]{1,0:T(8,128)S(1)} %pad_maximum_fusion), channel_id=1, source_target_pairs={{0,4},{2,6},{4,0},{6,2},{8,12},{10,14},{12,8},{14,10},{16,20},{18,... | collective-permute-start | bytes 24584 | tf_op jit(solution)/shard_map/ppermute | solution.py:87
  107.6 5.2 %collective-permute-start.15 = (f32[16,128]{1,0:T(8,128)S(1)}, f32[16,128]{1,0:T(8,128)S(1)}, u32[]{:S(2)}, u32[]{:S(2)}) collective-permute-start(f32[16,128]{1,0:T(8,128)S(1)} %pad_maximum_fusion), channel_id=1, source_target_pairs={{0,8},{2,10},{4,12},{6,14},{8,0},{10,2},{12,4},{14,6},{16,24},{18,... | collective-permute-start | bytes 24584 | tf_op jit(solution)/shard_map/ppermute | solution.py:87
  110.4 4.9 %collective-permute-start.16 = (f32[16,128]{1,0:T(8,128)S(1)}, f32[16,128]{1,0:T(8,128)S(1)}, u32[]{:S(2)}, u32[]{:S(2)}) collective-permute-start(f32[16,128]{1,0:T(8,128)S(1)} %pad_maximum_fusion), channel_id=1, source_target_pairs={{0,12},{2,14},{4,8},{6,10},{8,4},{10,6},{12,0},{14,2},{16,28},{18,... | collective-permute-start | bytes 24584 | tf_op jit(solution)/shard_map/ppermute | solution.py:87
  115.2 6.0 %collective-permute-start.17 = (f32[64,128]{1,0:T(8,128)S(1)}, f32[64,128]{1,0:T(8,128)S(1)}, u32[]{:S(2)}, u32[]{:S(2)}) collective-permute-start(f32[64,128]{1,0:T(8,128)S(1)} %constant_dynamic-update-slice_fusion.p0_ref), channel_id=1, source_target_pairs={{0,16},{2,18},{4,20},{6,22},{8,24},{10,26},{12,28},{14,30},{16,0},... | collective-permute-start | bytes 98312 | tf_op jit(solution)/shard_map/ppermute | solution.py:87
  116.0 5.4 %collective-permute-start.18 = (f32[64,128]{1,0:T(8,128)S(1)}, f32[64,128]{1,0:T(8,128)S(1)}, u32[]{:S(2)}, u32[]{:S(2)}) collective-permute-start(f32[64,128]{1,0:T(8,128)S(1)} %constant_dynamic-update-slice_fusion.p0_ref), channel_id=1, source_target_pairs={{0,32},{2,34},{4,36},{6,38},{8,40},{10,42},{12,44},{14,46},{16,48}... | collective-permute-start | bytes 98312 | tf_op jit(solution)/shard_map/ppermute | solution.py:87
  117.9 5.1 %collective-permute-start.19 = (f32[64,128]{1,0:T(8,128)S(1)}, f32[64,128]{1,0:T(8,128)S(1)}, u32[]{:S(2)}, u32[]{:S(2)}) collective-permute-start(f32[64,128]{1,0:T(8,128)S(1)} %constant_dynamic-update-slice_fusion.p0_ref), channel_id=1, source_target_pairs={{0,48},{2,50},{4,52},{6,54},{8,56},{10,58},{12,60},{14,62},{16,32}... | collective-permute-start | bytes 98312 | tf_op jit(solution)/shard_map/ppermute | solution.py:87
  (1 other events, 33.8 us)

commit v6 on v5

--- a/solution.py
+++ b/solution.py
@@ -19,7 +19,8 @@
 RAW = 512
 CHUNKS = (1536 - RAW, 2304, 256)
 EXTRA = 16
-STEP = CHUNKS[0] // 4
+PIECES = 4
+STEP = CHUNKS[0] // PIECES
 PACKED = 272
 PARTS = 4
 
@@ -107,8 +108,8 @@
     total = summed_over_four(mine + exchanged(yours, 1), 5)
     raw, total = lax.optimization_barrier((raw, total))
     raw = passed_along(raw)
+    total = summed_over_four(total, 3)
     total = summed_over_four(total, 1)
-    total = summed_over_four(total, 3)
     return (total, exchanged(total, 1)), raw
 
 
@@ -176,11 +177,20 @@
     above, below = row[:half] < col[:half], row[:half] > col[:half]
     a = jnp.where(below, mirrored, both)
     c = jnp.where(below, both, jnp.where(above, mirrored, packed[256:257, :]))
+    both, b = packed[0:128, :], packed[128:256, :]
+    mirrored = both.T
+    above, below = row[:half] < col[:half], row[:half] > col[:half]
+    a = jnp.where(below, mirrored, both)
+    c = jnp.where(below, both, jnp.where(above, mirrored, packed[256:257, :]))
     rev = (row[:half] == half - 1 - col[:half]).astype(F32)
     wt[0:128, :] = a
     wt[128:256, :] = b.T
-    wb[0:128, :] = jnp.dot(b, rev, precision=HIGHEST, preferred_element_type=F32)
-    wb[128:256, :] = jnp.dot(c, rev, precision=HIGHEST, preferred_element_type=F32)
+    turned = half - 1 - lax.broadcasted_iota(jnp.int32, (8, half), 1)
+    for n, part in enumerate((b, c)):
+        for k in range(0, half, 8):
+            wb[half * n + k : half * n + k + 8, :] = jnp.take_along_axis(
+                part[k : k + 8, :], turned, axis=1, mode="promise_in_bounds"
+            )
     eye = row[:half] == col[:half]
     d_top = jnp.sum(jnp.where(eye, wt[0:128, :], 0.0), axis=0, keepdims=True)
     anti = row[:half] == half - 1 - col[:half]
@@ -222,23 +232,22 @@
     g, d_top, d_bot = lax.fori_loop(0, ROUNDS, one_round, tuple(start_ref[n] for n in range(3)))
     dot = functools.partial(jnp.dot, precision=HIGHEST, preferred_element_type=F32)
     lane = lax.broadcasted_iota(jnp.int32, (half, half), 1)
-    halves, diags = [], []
-    for n in range(2):
+    parts = []
+    for ref in (vt, vb):
+        high = ref[...].astype(BF16)
+        parts.append((high, (ref[...] - high.astype(F32)).astype(BF16)))
+    diags = []
+    for n, out_ref in enumerate((stay_ref, leave_ref)):
         column = lane + half * (n ^ swap_blocks)
         p_top = (last_ref[0:half, :] == column).astype(F32)
         p_bot = (last_ref[half : 2 * half, :] == column).astype(F32)
-        halves.append(dot(vt[...], p_top) + dot(vb[...], p_bot))
+        for m in range(2):
+            part = product(parts[0][m], p_top.astype(BF16)) + product(parts[1][m], p_bot.astype(BF16))
+            out_ref[:, half * m : half * m + half] = part.astype(BF16)
         diags.append(dot(d_top, p_top) + dot(d_bot, p_bot))
-    rot = jnp.concatenate(halves, axis=1)
-    high = rot.astype(BF16)
-    low = (rot - high.astype(F32)).astype(BF16)
-    stay_ref[:, 0:128] = high[:, 0:128]
-    stay_ref[:, 128:256] = low[:, 0:128]
-    leave_ref[:, 0:128] = high[:, 128:256]
-    leave_ref[:, 128:256] = low[:, 128:256]
     diag = jnp.concatenate(diags, axis=1)
     diag_ref[...] = diag
-    wt[...] = rot[:, 128:256]
+    wt[...] = leave_ref[:, 0:128].astype(F32) + leave_ref[:, 128:256].astype(F32)
     piece = pl.ds(pl.multiple_of(((4 * y + x) * 2 + core) * 8, 8), 8)
     first_ref[CHUNKS[0] : CHUNKS[0] + 8, :] = wt[piece, :]
     label = jnp.full((8, half), jnp.maximum(ids_ref[0], ids_ref[1]).astype(F32))
@@ -343,7 +352,7 @@
     out_ref[...] = rotation(x_ref[...], rot[...])
 
 
-def rotated_raw(raw, pieces, result, rows=RAW // 4):
+def rotated_raw(raw, pieces, result, rows=RAW // PIECES):
     count = raw.shape[0]
     piece = pl.BlockSpec((64, BLOCK), lambda i: (0, 0))
     return pl.pallas_call(

time: 135 us -> 134 us (level)
    ppermute x18, waiting for transfers between devices: 15 us -> 16.7 us  [exchanged(): return lax.ppermute(array, 'row', [(i, i ^ mask) for i in range(128)])]
  transfers between devices with their start and end apart: 22 -> 22, of which waited for: 15 -> 16; matrix products, arithmetic and copies ran while one was open for 5% -> 5% of each run, Pallas kernels for 20% -> 19%
where the time goes in v6:
time: 134 us; the launch traced here: 133 us
  waiting for transfers between devices  54.4 us (41%)
  starting transfers between devices  40.4 us (30%)
  Pallas kernels  30.3 us (23%)
  local copies, waits for them, and re-layouts  4.21 us (3%)
  other arithmetic  2.64 us (2%)
  between operations  1.44 us (1%)
    ppermute x4, waiting for transfers between devices, passed_along(): return lax.ppermute(array, 'pair', [(0, 1), (1, 0)])  37.6 us
    ppermute x18, starting transfers between devices, exchanged(): return lax.ppermute(array, 'row', [(i, i ^ mask) for i in range(128)])  22.1 us
    ppermute x4, starting transfers between devices, passed_along(): return lax.ppermute(array, 'pair', [(0, 1), (1, 0)])  18.3 us
    ppermute x18, waiting for transfers between devices, exchanged(): return lax.ppermute(array, 'row', [(i, i ^ mask) for i in range(128)])  16.7 us
    pallas_call x1, Pallas kernels, rounds_and_first_chunk(): pl.pallas_call(rounds_kernel, in_specs=[pl.BlockSpec(memory_space=pltpu.S...  9.78 us
    pallas_call x1, Pallas kernels, staying(): pl.pallas_call(rotate_kernel, grid=(count // rows,), in_specs=[pl.BlockSp...  7.19 us
    pallas_call x2, Pallas kernels, leaving(): pl.pallas_call(rotate_kernel, grid=(count // rows,), in_specs=[pl.BlockSp...  7.12 us
    pallas_call x1, Pallas kernels, local_gram(): pl.pallas_call(gram_kernel, in_specs=[pl.BlockSpec(memory_space=pl.ANY)],...  4.32 us
  transfers between devices with their start and end apart: 22, of which 16 were waited for; matrix products, arithmetic and copies ran while one was open for 5% of the time, Pallas kernels for 19%

profile of v6, /device:TPU:56, one launch (start us, length us, event | category | flops | bytes accessed | tf_op | source)
XLA Modules:
  0.0 133.4 jit_solution(5103869758093247031)
XLA Ops:
  0.7 4.3 %shard_map.67 = f32[272,128]{1,0:T(8,128)S(1)} custom-call(f32[4096,256]{1,0:T(8,128)} %x_ref.5), custom_call_target="tpu_custom_call" | custom-call | tf_op jit(solution)/shard_map/pallas_call | solution.py:67
  6.4 3.4 %collective-permute-start.1 = (f32[136,128]{1,0:T(8,128)S(1)}, f32[136,128]{1,0:T(8,128)S(1)}, u32[]{:S(2)}, u32[]{:S(2)}) collective-permute-start(f32[136,128]{1,0:T(8,128)S(1)} %dynamic-slice_add_fusion), channel_id=1, source_target_pairs={{0,128},{2,130},{4,132},{6,134},{8,136},{10,138},{12,140},{14,142}... | collective-permute-start | bytes 208904 | tf_op jit(solution)/shard_map/ppermute | solution.py:88
  11.5 1.8 %collective-permute-done.1 = f32[136,128]{1,0:T(8,128)S(1)} collective-permute-done((f32[136,128]{1,0:T(8,128)S(1)}, f32[136,128]{1,0:T(8,128)S(1)}, u32[]{:S(2)}, u32[]{:S(2)}) %collective-permute-start.1) | collective-permute-done | bytes 69664 | tf_op jit(solution)/shard_map/ppermute | solution.py:88
  16.9 2.8 %collective-permute-start.6 = (f32[136,128]{1,0:T(8,128)S(1)}, f32[136,128]{1,0:T(8,128)S(1)}, u32[]{:S(2)}, u32[]{:S(2)}) collective-permute-start(f32[136,128]{1,0:T(8,128)S(1)} %add_add_fusion.2), channel_id=1, source_target_pairs={{0,48},{2,50},{4,52},{6,54},{8,56},{10,58},{12,60},{14,62},{16,32}... | collective-permute-start | bytes 208904 | tf_op jit(solution)/shard_map/ppermute | solution.py:88
  19.7 6.4 %collective-permute-start.11 = (f32[512,256]{1,0:T(8,128)S(1)}, f32[512,256]{1,0:T(8,128)S(1)}, u32[]{:S(2)}, u32[]{:S(2)}) collective-permute-start(f32[512,256]{1,0:T(8,128)S(1)} %slice.23), channel_id=1, source_target_pairs={{0,1},{1,0},{2,3},{3,2},{4,5},{5,4},{6,7},{7,6},{8,9},{9,8},{10,11... | collective-permute-start | bytes 1572872 | tf_op jit(solution)/shard_map/ppermute | solution.py:92
  26.2 3.1 %collective-permute-start.7 = (f32[136,128]{1,0:T(8,128)S(1)}, f32[136,128]{1,0:T(8,128)S(1)}, u32[]{:S(2)}, u32[]{:S(2)}) collective-permute-start(f32[136,128]{1,0:T(8,128)S(1)} %add_add_fusion.1), channel_id=1, source_target_pairs={{0,8},{2,10},{4,12},{6,14},{8,0},{10,2},{12,4},{14,6},{16,24},{18,... | collective-permute-start | bytes 208904 | tf_op jit(solution)/shard_map/ppermute | solution.py:88
  30.4 1.8 %collective-permute-done.7 = f32[136,128]{1,0:T(8,128)S(1)} collective-permute-done((f32[136,128]{1,0:T(8,128)S(1)}, f32[136,128]{1,0:T(8,128)S(1)}, u32[]{:S(2)}, u32[]{:S(2)}) %collective-permute-start.7) | collective-permute-done | bytes 69664 | tf_op jit(solution)/shard_map/ppermute | solution.py:88
  32.2 1.4 %collective-permute-done.8 = f32[136,128]{1,0:T(8,128)S(1)} collective-permute-done((f32[136,128]{1,0:T(8,128)S(1)}, f32[136,128]{1,0:T(8,128)S(1)}, u32[]{:S(2)}, u32[]{:S(2)}) %collective-permute-start.8) | collective-permute-done | bytes 69664 | tf_op jit(solution)/shard_map/ppermute | solution.py:88
  33.6 1.8 %collective-permute-done.9 = f32[136,128]{1,0:T(8,128)S(1)} collective-permute-done((f32[136,128]{1,0:T(8,128)S(1)}, f32[136,128]{1,0:T(8,128)S(1)}, u32[]{:S(2)}, u32[]{:S(2)}) %collective-permute-start.9) | collective-permute-done | bytes 69664 | tf_op jit(solution)/shard_map/ppermute | solution.py:88
  36.8 9.8 %shard_map.68 = (f32[1040,128]{1,0:T(8,128)S(1)}, bf16[256,256]{1,0:T(8,128)(2,1)S(1)}, bf16[256,256]{1,0:T(8,128)(2,1)S(1)}, f32[8,256]{1,0:T(8,128)S(1)}) custom-call(s32[2]{0:T(128)S(1)} %copy-done.2, s32[48,8,128]{2,1,0:T(8,128)S(1)} %copy-done, s32[256,128]{1,0:T(8,128)S(1)} %copy-done.1, f32[136,128]{1,0:T(8,128)S(1)} %add_add_fusion.mine_ref, ...), custom_call_target="tpu_custom_call" | custom-call | tf_op jit(solution)/shard_map/pallas_call | solution.py:270
  46.6 1.7 %collective-permute-done.11.x_ref = f32[512,256]{1,0:T(8,128)S(1)} collective-permute-done((f32[512,256]{1,0:T(8,128)S(1)}, f32[512,256]{1,0:T(8,128)S(1)}, u32[]{:S(2)}, u32[]{:S(2)}) %collective-permute-start.11) | collective-permute-done | bytes 524320 | tf_op jit(solution)/shard_map/ppermute | solution.py:92
  48.2 5.6 %collective-permute-start.12 = (f32[1040,128]{1,0:T(8,128)S(1)}, f32[1040,128]{1,0:T(8,128)S(1)}, u32[]{:S(2)}, u32[]{:S(2)}) collective-permute-start(f32[1040,128]{1,0:T(8,128)S(1)} %get-tuple-element.15), channel_id=1, source_target_pairs={{0,1},{1,0},{2,3},{3,2},{4,5},{5,4},{6,7},{7,6},{8,9},{9,8},{10,11... | collective-permute-start | bytes 1597448 | tf_op jit(solution)/shard_map/ppermute | solution.py:92
  54.5 5.9 %shard_map.71 = f32[2304,128]{1,0:T(8,128)S(1)} custom-call(f32[4096,256]{1,0:T(8,128)} %x_ref.5, bf16[256,256]{1,0:T(8,128)(2,1)S(1)} %get-tuple-element.17.rot_ref), custom_call_target="tpu_custom_call" | custom-call | flops 452984832 | bytes 3538944 | tf_op jit(solution)/shard_map/pallas_call | solution.py:310
  62.1 5.9 %collective-permute-start.21 = (f32[256,128]{1,0:T(8,128)S(1)}, f32[256,128]{1,0:T(8,128)S(1)}, u32[]{:S(2)}, u32[]{:S(2)}) collective-permute-start(f32[256,128]{1,0:T(8,128)S(1)} %shard_map.72), channel_id=1, source_target_pairs={{0,1},{1,0},{2,3},{3,2},{4,5},{5,4},{6,7},{7,6},{8,9},{9,8},{10,11... | collective-permute-start | bytes 393224 | tf_op jit(solution)/shard_map/ppermute | solution.py:92
  68.0 7.2 %shard_map.69._ = f32[4096,256]{1,0:T(8,128)} custom-call(f32[4096,256]{1,0:T(8,128)} %x_ref.5, bf16[256,256]{1,0:T(8,128)(2,1)S(1)} %get-tuple-element.16.rot_ref), custom_call_target="tpu_custom_call" | custom-call | flops 805306368 | bytes 6291456 | tf_op jit(solution)/shard_map/pallas_call | solution.py:326
  75.2 29.6 %collective-permute-done.12 = f32[1040,128]{1,0:T(8,128)S(1)} collective-permute-done((f32[1040,128]{1,0:T(8,128)S(1)}, f32[1040,128]{1,0:T(8,128)S(1)}, u32[]{:S(2)}, u32[]{:S(2)}) %collective-permute-start.12) | collective-permute-done | bytes 532512 | tf_op jit(solution)/shard_map/ppermute | solution.py:92
  107.6 2.7 %collective-permute-start.15 = (f32[16,128]{1,0:T(8,128)S(1)}, f32[16,128]{1,0:T(8,128)S(1)}, u32[]{:S(2)}, u32[]{:S(2)}) collective-permute-start(f32[16,128]{1,0:T(8,128)S(1)} %pad_maximum_fusion), channel_id=1, source_target_pairs={{0,8},{2,10},{4,12},{6,14},{8,0},{10,2},{12,4},{14,6},{16,24},{18,... | collective-permute-start | bytes 24584 | tf_op jit(solution)/shard_map/ppermute | solution.py:88
  111.3 1.5 %collective-permute-done.15 = f32[16,128]{1,0:T(8,128)S(1)} collective-permute-done((f32[16,128]{1,0:T(8,128)S(1)}, f32[16,128]{1,0:T(8,128)S(1)}, u32[]{:S(2)}, u32[]{:S(2)}) %collective-permute-start.15) | collective-permute-done | bytes 8224 | tf_op jit(solution)/shard_map/ppermute | solution.py:88
  112.8 2.4 %collective-permute-done.16 = f32[16,128]{1,0:T(8,128)S(1)} collective-permute-done((f32[16,128]{1,0:T(8,128)S(1)}, f32[16,128]{1,0:T(8,128)S(1)}, u32[]{:S(2)}, u32[]{:S(2)}) %collective-permute-start.16) | collective-permute-done | bytes 8224 | tf_op jit(solution)/shard_map/ppermute | solution.py:88
  116.0 1.4 %collective-permute-start.18 = (f32[64,128]{1,0:T(8,128)S(1)}, f32[64,128]{1,0:T(8,128)S(1)}, u32[]{:S(2)}, u32[]{:S(2)}) collective-permute-start(f32[64,128]{1,0:T(8,128)S(1)} %constant_dynamic-update-slice_fusion.p0_ref), channel_id=1, source_target_pairs={{0,32},{2,34},{4,36},{6,38},{8,40},{10,42},{12,44},{14,46},{16,48}... | collective-permute-start | bytes 98312 | tf_op jit(solution)/shard_map/ppermute | solution.py:88
  117.4 2.6 %collective-permute-start.19 = (f32[64,128]{1,0:T(8,128)S(1)}, f32[64,128]{1,0:T(8,128)S(1)}, u32[]{:S(2)}, u32[]{:S(2)}) collective-permute-start(f32[64,128]{1,0:T(8,128)S(1)} %constant_dynamic-update-slice_fusion.p0_ref), channel_id=1, source_target_pairs={{0,48},{2,50},{4,52},{6,54},{8,56},{10,58},{12,60},{14,62},{16,32}... | collective-permute-start | bytes 98312 | tf_op jit(solution)/shard_map/ppermute | solution.py:88
  122.5 1.9 %shard_map.70 = f32[4096,256]{1,0:T(8,128)} custom-call(f32[512,256]{1,0:T(8,128)S(1)} %collective-permute-done.11.x_ref, f32[64,128]{1,0:T(8,128)S(1)} %constant_dynamic-update-slice_fusion.p0_ref, f32[64,128]{1,0:T(8,128)S(1)} %collective-permute-done.17.p1_ref, f32[64,128]{1,0:T(8,128)S(1)} %collective-permute-done.18.p2_ref, ...), custom_call_target="tpu_custom_call", output_to_operand_aliasing={{}: (5, {})} | custom-call | flops 100663296 | bytes 786432 | tf_op jit(solution)/shard_map/pallas_call | solution.py:358
  125.2 4.8 %collective-permute-done.20 = f32[2304,128]{1,0:T(8,128)S(1)} collective-permute-done((f32[2304,128]{1,0:T(8,128)S(1)}, f32[2304,128]{1,0:T(8,128)S(1)}, u32[]{:S(2)}, u32[]{:S(2)}) %collective-permute-start.20) | collective-permute-done | bytes 1179680 | tf_op jit(solution)/shard_map/ppermute | solution.py:92
  131.1 1.6 %collective-permute-done.21 = f32[256,128]{1,0:T(8,128)S(1)} collective-permute-done((f32[256,128]{1,0:T(8,128)S(1)}, f32[256,128]{1,0:T(8,128)S(1)}, u32[]{:S(2)}, u32[]{:S(2)}) %collective-permute-start.21) | collective-permute-done | bytes 131104 | tf_op jit(solution)/shard_map/ppermute | solution.py:92
  (53 shorter events, 20.6 us)
Async XLA Ops:
  0.6 36.1 %copy-start = (s32[48,8,128]{2,1,0:T(8,128)S(1)}, s32[48,8,128]{2,1,0:T(8,128)}, u32[]{:S(2)}) copy-start(s32[48,8,128]{2,1,0:T(8,128)} %constant.33.clone.table_ref) | copy-start | bytes 589828
  0.6 36.1 %copy-start.1 = (s32[256,128]{1,0:T(8,128)S(1)}, s32[256,128]{1,0:T(8,128)}, u32[]{:S(2)}) copy-start(s32[256,128]{1,0:T(8,128)} %constant.34.clone.last_ref) | copy-start | bytes 393220
  5.0 1.3 %collective-permute-start = (f32[136,128]{1,0:T(8,128)S(1)}, f32[136,128]{1,0:T(8,128)S(1)}, u32[]{:S(2)}, u32[]{:S(2)}) collective-permute-start(f32[136,128]{1,0:T(8,128)S(1)} %constant_dynamic-slice_fusion), channel_id=1, source_target_pairs={{0,2},{2,0},{4,6},{6,4},{8,10},{10,8},{12,14},{14,12},{16,18},{18,... | collective-permute-start | bytes 208904 | tf_op jit(solution)/shard_map/ppermute | solution.py:88
  6.4 6.9 %collective-permute-start.1 = (f32[136,128]{1,0:T(8,128)S(1)}, f32[136,128]{1,0:T(8,128)S(1)}, u32[]{:S(2)}, u32[]{:S(2)}) collective-permute-start(f32[136,128]{1,0:T(8,128)S(1)} %dynamic-slice_add_fusion), channel_id=1, source_target_pairs={{0,128},{2,130},{4,132},{6,134},{8,136},{10,138},{12,140},{14,142}... | collective-permute-start | bytes 208904 | tf_op jit(solution)/shard_map/ppermute | solution.py:88
  9.7 4.7 %collective-permute-start.2 = (f32[136,128]{1,0:T(8,128)S(1)}, f32[136,128]{1,0:T(8,128)S(1)}, u32[]{:S(2)}, u32[]{:S(2)}) collective-permute-start(f32[136,128]{1,0:T(8,128)S(1)} %dynamic-slice_add_fusion), channel_id=1, source_target_pairs={{0,64},{2,66},{4,68},{6,70},{8,72},{10,74},{12,76},{14,78},{16,80}... | collective-permute-start | bytes 208904 | tf_op jit(solution)/shard_map/ppermute | solution.py:88
  9.9 5.7 %collective-permute-start.3 = (f32[136,128]{1,0:T(8,128)S(1)}, f32[136,128]{1,0:T(8,128)S(1)}, u32[]{:S(2)}, u32[]{:S(2)}) collective-permute-start(f32[136,128]{1,0:T(8,128)S(1)} %dynamic-slice_add_fusion), channel_id=1, source_target_pairs={{0,192},{2,194},{4,196},{6,198},{8,200},{10,202},{12,204},{14,206}... | collective-permute-start | bytes 208904 | tf_op jit(solution)/shard_map/ppermute | solution.py:88
  15.5 10.6 %collective-permute-start.4 = (f32[136,128]{1,0:T(8,128)S(1)}, f32[136,128]{1,0:T(8,128)S(1)}, u32[]{:S(2)}, u32[]{:S(2)}) collective-permute-start(f32[136,128]{1,0:T(8,128)S(1)} %add_add_fusion.2), channel_id=1, source_target_pairs={{0,32},{2,34},{4,36},{6,38},{8,40},{10,42},{12,44},{14,46},{16,48}... | collective-permute-start | bytes 208904 | tf_op jit(solution)/shard_map/ppermute | solution.py:88
  16.9 9.3 %collective-permute-start.5 = (f32[136,128]{1,0:T(8,128)S(1)}, f32[136,128]{1,0:T(8,128)S(1)}, u32[]{:S(2)}, u32[]{:S(2)}) collective-permute-start(f32[136,128]{1,0:T(8,128)S(1)} %add_add_fusion.2), channel_id=1, source_target_pairs={{0,16},{2,18},{4,20},{6,22},{8,24},{10,26},{12,28},{14,30},{16,0},... | collective-permute-start | bytes 208904 | tf_op jit(solution)/shard_map/ppermute | solution.py:88
  16.9 9.2 %collective-permute-start.6 = (f32[136,128]{1,0:T(8,128)S(1)}, f32[136,128]{1,0:T(8,128)S(1)}, u32[]{:S(2)}, u32[]{:S(2)}) collective-permute-start(f32[136,128]{1,0:T(8,128)S(1)} %add_add_fusion.2), channel_id=1, source_target_pairs={{0,48},{2,50},{4,52},{6,54},{8,56},{10,58},{12,60},{14,62},{16,32}... | collective-permute-start | bytes 208904 | tf_op jit(solution)/shard_map/ppermute | solution.py:88
  19.7 28.5 %collective-permute-start.11 = (f32[512,256]{1,0:T(8,128)S(1)}, f32[512,256]{1,0:T(8,128)S(1)}, u32[]{:S(2)}, u32[]{:S(2)}) collective-permute-start(f32[512,256]{1,0:T(8,128)S(1)} %slice.23), channel_id=1, source_target_pairs={{0,1},{1,0},{2,3},{3,2},{4,5},{5,4},{6,7},{7,6},{8,9},{9,8},{10,11... | collective-permute-start | bytes 1572872 | tf_op jit(solution)/shard_map/ppermute | solution.py:92
  26.2 6.0 %collective-permute-start.7 = (f32[136,128]{1,0:T(8,128)S(1)}, f32[136,128]{1,0:T(8,128)S(1)}, u32[]{:S(2)}, u32[]{:S(2)}) collective-permute-start(f32[136,128]{1,0:T(8,128)S(1)} %add_add_fusion.1), channel_id=1, source_target_pairs={{0,8},{2,10},{4,12},{6,14},{8,0},{10,2},{12,4},{14,6},{16,24},{18,... | collective-permute-start | bytes 208904 | tf_op jit(solution)/shard_map/ppermute | solution.py:88
  29.3 4.3 %collective-permute-start.8 = (f32[136,128]{1,0:T(8,128)S(1)}, f32[136,128]{1,0:T(8,128)S(1)}, u32[]{:S(2)}, u32[]{:S(2)}) collective-permute-start(f32[136,128]{1,0:T(8,128)S(1)} %add_add_fusion.1), channel_id=1, source_target_pairs={{0,4},{2,6},{4,0},{6,2},{8,12},{10,14},{12,8},{14,10},{16,20},{18,... | collective-permute-start | bytes 208904 | tf_op jit(solution)/shard_map/ppermute | solution.py:88
  29.9 5.5 %collective-permute-start.9 = (f32[136,128]{1,0:T(8,128)S(1)}, f32[136,128]{1,0:T(8,128)S(1)}, u32[]{:S(2)}, u32[]{:S(2)}) collective-permute-start(f32[136,128]{1,0:T(8,128)S(1)} %add_add_fusion.1), channel_id=1, source_target_pairs={{0,12},{2,14},{4,8},{6,10},{8,4},{10,6},{12,0},{14,2},{16,28},{18,... | collective-permute-start | bytes 208904 | tf_op jit(solution)/shard_map/ppermute | solution.py:88
  35.4 1.3 %collective-permute-start.10 = (f32[136,128]{1,0:T(8,128)S(1)}, f32[136,128]{1,0:T(8,128)S(1)}, u32[]{:S(2)}, u32[]{:S(2)}) collective-permute-start(f32[136,128]{1,0:T(8,128)S(1)} %add_add_fusion.mine_ref), channel_id=1, source_target_pairs={{0,2},{2,0},{4,6},{6,4},{8,10},{10,8},{12,14},{14,12},{16,18},{18,... | collective-permute-start | bytes 208904 | tf_op jit(solution)/shard_map/ppermute | solution.py:88
  48.2 56.5 %collective-permute-start.12 = (f32[1040,128]{1,0:T(8,128)S(1)}, f32[1040,128]{1,0:T(8,128)S(1)}, u32[]{:S(2)}, u32[]{:S(2)}) collective-permute-start(f32[1040,128]{1,0:T(8,128)S(1)} %get-tuple-element.15), channel_id=1, source_target_pairs={{0,1},{1,0},{2,3},{3,2},{4,5},{5,4},{6,7},{7,6},{8,9},{9,8},{10,11... | collective-permute-start | bytes 1597448 | tf_op jit(solution)/shard_map/ppermute | solution.py:92
  60.5 69.5 %collective-permute-start.20 = (f32[2304,128]{1,0:T(8,128)S(1)}, f32[2304,128]{1,0:T(8,128)S(1)}, u32[]{:S(2)}, u32[]{:S(2)}) collective-permute-start(f32[2304,128]{1,0:T(8,128)S(1)} %shard_map.71), channel_id=1, source_target_pairs={{0,1},{1,0},{2,3},{3,2},{4,5},{5,4},{6,7},{7,6},{8,9},{9,8},{10,11... | collective-permute-start | bytes 3538952 | tf_op jit(solution)/shard_map/ppermute | solution.py:92
  62.1 70.6 %collective-permute-start.21 = (f32[256,128]{1,0:T(8,128)S(1)}, f32[256,128]{1,0:T(8,128)S(1)}, u32[]{:S(2)}, u32[]{:S(2)}) collective-permute-start(f32[256,128]{1,0:T(8,128)S(1)} %shard_map.72), channel_id=1, source_target_pairs={{0,1},{1,0},{2,3},{3,2},{4,5},{5,4},{6,7},{7,6},{8,9},{9,8},{10,11... | collective-permute-start | bytes 393224 | tf_op jit(solution)/shard_map/ppermute | solution.py:92
  104.7 1.8 %collective-permute-start.13 = (f32[8,128]{1,0:T(8,128)S(1)}, f32[8,128]{1,0:T(8,128)S(1)}, u32[]{:S(2)}, u32[]{:S(2)}) collective-permute-start(f32[8,128]{1,0:T(8,128)S(1)} %get-tuple-element.19), channel_id=1, source_target_pairs={{0,2},{2,0},{4,6},{6,4},{8,10},{10,8},{12,14},{14,12},{16,18},{18,... | collective-permute-start | bytes 12296 | tf_op jit(solution)/shard_map/ppermute | solution.py:88
  106.5 4.8 %collective-permute-start.14 = (f32[16,128]{1,0:T(8,128)S(1)}, f32[16,128]{1,0:T(8,128)S(1)}, u32[]{:S(2)}, u32[]{:S(2)}) collective-permute-start(f32[16,128]{1,0:T(8,128)S(1)} %pad_maximum_fusion), channel_id=1, source_target_pairs={{0,4},{2,6},{4,0},{6,2},{8,12},{10,14},{12,8},{14,10},{16,20},{18,... | collective-permute-start | bytes 24584 | tf_op jit(solution)/shard_map/ppermute | solution.py:88
  107.6 5.2 %collective-permute-start.15 = (f32[16,128]{1,0:T(8,128)S(1)}, f32[16,128]{1,0:T(8,128)S(1)}, u32[]{:S(2)}, u32[]{:S(2)}) collective-permute-start(f32[16,128]{1,0:T(8,128)S(1)} %pad_maximum_fusion), channel_id=1, source_target_pairs={{0,8},{2,10},{4,12},{6,14},{8,0},{10,2},{12,4},{14,6},{16,24},{18,... | collective-permute-start | bytes 24584 | tf_op jit(solution)/shard_map/ppermute | solution.py:88
  110.4 4.9 %collective-permute-start.16 = (f32[16,128]{1,0:T(8,128)S(1)}, f32[16,128]{1,0:T(8,128)S(1)}, u32[]{:S(2)}, u32[]{:S(2)}) collective-permute-start(f32[16,128]{1,0:T(8,128)S(1)} %pad_maximum_fusion), channel_id=1, source_target_pairs={{0,12},{2,14},{4,8},{6,10},{8,4},{10,6},{12,0},{14,2},{16,28},{18,... | collective-permute-start | bytes 24584 | tf_op jit(solution)/shard_map/ppermute | solution.py:88
  115.2 6.0 %collective-permute-start.17 = (f32[64,128]{1,0:T(8,128)S(1)}, f32[64,128]{1,0:T(8,128)S(1)}, u32[]{:S(2)}, u32[]{:S(2)}) collective-permute-start(f32[64,128]{1,0:T(8,128)S(1)} %constant_dynamic-update-slice_fusion.p0_ref), channel_id=1, source_target_pairs={{0,16},{2,18},{4,20},{6,22},{8,24},{10,26},{12,28},{14,30},{16,0},... | collective-permute-start | bytes 98312 | tf_op jit(solution)/shard_map/ppermute | solution.py:88
  116.0 5.4 %collective-permute-start.18 = (f32[64,128]{1,0:T(8,128)S(1)}, f32[64,128]{1,0:T(8,128)S(1)}, u32[]{:S(2)}, u32[]{:S(2)}) collective-permute-start(f32[64,128]{1,0:T(8,128)S(1)} %constant_dynamic-update-slice_fusion.p0_ref), channel_id=1, source_target_pairs={{0,32},{2,34},{4,36},{6,38},{8,40},{10,42},{12,44},{14,46},{16,48}... | collective-permute-start | bytes 98312 | tf_op jit(solution)/shard_map/ppermute | solution.py:88
  117.4 5.1 %collective-permute-start.19 = (f32[64,128]{1,0:T(8,128)S(1)}, f32[64,128]{1,0:T(8,128)S(1)}, u32[]{:S(2)}, u32[]{:S(2)}) collective-permute-start(f32[64,128]{1,0:T(8,128)S(1)} %constant_dynamic-update-slice_fusion.p0_ref), channel_id=1, source_target_pairs={{0,48},{2,50},{4,52},{6,54},{8,56},{10,58},{12,60},{14,62},{16,32}... | collective-permute-start | bytes 98312 | tf_op jit(solution)/shard_map/ppermute | solution.py:88
  (1 other events, 36.1 us)

commit v7 on v6

--- a/solution.py
+++ b/solution.py
@@ -22,7 +22,7 @@
 PIECES = 4
 STEP = CHUNKS[0] // PIECES
 PACKED = 272
-PARTS = 4
+PARTS = (512, 1024, 1280, 1280)
 
 
 def product(a, b):
@@ -34,8 +34,7 @@
 
 
 def gram_kernel(slab_ref, out_ref, x_ref, even, odd, sems):
-    rows = ROWS // PARTS
-    parts = [pl.ds(n * rows, rows) for n in range(PARTS)]
+    parts = [pl.ds(sum(PARTS[:n]), rows) for n, rows in enumerate(PARTS)]
     copies = [
         pltpu.make_async_copy(slab_ref.at[part, :], x_ref.at[part, :], sems.at[n])
         for n, part in enumerate(parts)
@@ -73,7 +72,7 @@
             pltpu.VMEM((ROWS, WIDTH), F32),
             pltpu.VMEM((WIDTH, WIDTH), F32),
             pltpu.VMEM((WIDTH, WIDTH), F32),
-            pltpu.SemaphoreType.DMA((PARTS,)),
+            pltpu.SemaphoreType.DMA((len(PARTS),)),
         ],
         compiler_params=pltpu.CompilerParams(vmem_limit_bytes=VMEM_LIMIT),
     )(pltpu.with_memory_space_constraint(slab, pltpu.HBM))

time: 134 us -> 134 us (level)
  transfers between devices with their start and end apart: 22 -> 22, of which waited for: 16 -> 16; matrix products, arithmetic and copies ran while one was open for 5% -> 5% of each run, Pallas kernels for 19% -> 20%
where the time goes in v7:
time: 134 us; the launch traced here: 133 us
  waiting for transfers between devices  54.4 us (41%)
  starting transfers between devices  40.4 us (30%)
  Pallas kernels  30.1 us (22%)
  local copies, waits for them, and re-layouts  4.21 us (3%)
  other arithmetic  2.64 us (2%)
  between operations  1.44 us (1%)
    ppermute x4, waiting for transfers between devices, passed_along(): return lax.ppermute(array, 'pair', [(0, 1), (1, 0)])  37.6 us
    ppermute x18, starting transfers between devices, exchanged(): return lax.ppermute(array, 'row', [(i, i ^ mask) for i in range(128)])  22.1 us
    ppermute x4, starting transfers between devices, passed_along(): return lax.ppermute(array, 'pair', [(0, 1), (1, 0)])  18.3 us
    ppermute x18, waiting for transfers between devices, exchanged(): return lax.ppermute(array, 'row', [(i, i ^ mask) for i in range(128)])  16.7 us
    pallas_call x1, Pallas kernels, rounds_and_first_chunk(): pl.pallas_call(rounds_kernel, in_specs=[pl.BlockSpec(memory_space=pltpu.S...  9.78 us
    pallas_call x1, Pallas kernels, staying(): pl.pallas_call(rotate_kernel, grid=(count // rows,), in_specs=[pl.BlockSp...  7.18 us
    pallas_call x2, Pallas kernels, leaving(): pl.pallas_call(rotate_kernel, grid=(count // rows,), in_specs=[pl.BlockSp...  7.12 us
    pallas_call x1, Pallas kernels, local_gram(): pl.pallas_call(gram_kernel, in_specs=[pl.BlockSpec(memory_space=pl.ANY)],...  4.14 us
  transfers between devices with their start and end apart: 22, of which 16 were waited for; matrix products, arithmetic and copies ran while one was open for 5% of the time, Pallas kernels for 20%

profile of v7, /device:TPU:56, one launch (start us, length us, event | category | flops | bytes accessed | tf_op | source)
XLA Modules:
  0.0 133.2 jit_solution(1874683473629511535)
XLA Ops:
  0.7 4.1 %shard_map.67 = f32[272,128]{1,0:T(8,128)S(1)} custom-call(f32[4096,256]{1,0:T(8,128)} %x_ref.5), custom_call_target="tpu_custom_call" | custom-call | tf_op jit(solution)/shard_map/pallas_call | solution.py:66
  6.2 3.4 %collective-permute-start.1 = (f32[136,128]{1,0:T(8,128)S(1)}, f32[136,128]{1,0:T(8,128)S(1)}, u32[]{:S(2)}, u32[]{:S(2)}) collective-permute-start(f32[136,128]{1,0:T(8,128)S(1)} %dynamic-slice_add_fusion), channel_id=1, source_target_pairs={{0,128},{2,130},{4,132},{6,134},{8,136},{10,138},{12,140},{14,142}... | collective-permute-start | bytes 208904 | tf_op jit(solution)/shard_map/ppermute | solution.py:87
  11.3 1.8 %collective-permute-done.1 = f32[136,128]{1,0:T(8,128)S(1)} collective-permute-done((f32[136,128]{1,0:T(8,128)S(1)}, f32[136,128]{1,0:T(8,128)S(1)}, u32[]{:S(2)}, u32[]{:S(2)}) %collective-permute-start.1) | collective-permute-done | bytes 69664 | tf_op jit(solution)/shard_map/ppermute | solution.py:87
  16.7 2.8 %collective-permute-start.6 = (f32[136,128]{1,0:T(8,128)S(1)}, f32[136,128]{1,0:T(8,128)S(1)}, u32[]{:S(2)}, u32[]{:S(2)}) collective-permute-start(f32[136,128]{1,0:T(8,128)S(1)} %add_add_fusion.2), channel_id=1, source_target_pairs={{0,48},{2,50},{4,52},{6,54},{8,56},{10,58},{12,60},{14,62},{16,32}... | collective-permute-start | bytes 208904 | tf_op jit(solution)/shard_map/ppermute | solution.py:87
  19.6 6.4 %collective-permute-start.11 = (f32[512,256]{1,0:T(8,128)S(1)}, f32[512,256]{1,0:T(8,128)S(1)}, u32[]{:S(2)}, u32[]{:S(2)}) collective-permute-start(f32[512,256]{1,0:T(8,128)S(1)} %slice.23), channel_id=1, source_target_pairs={{0,1},{1,0},{2,3},{3,2},{4,5},{5,4},{6,7},{7,6},{8,9},{9,8},{10,11... | collective-permute-start | bytes 1572872 | tf_op jit(solution)/shard_map/ppermute | solution.py:91
  26.0 3.1 %collective-permute-start.7 = (f32[136,128]{1,0:T(8,128)S(1)}, f32[136,128]{1,0:T(8,128)S(1)}, u32[]{:S(2)}, u32[]{:S(2)}) collective-permute-start(f32[136,128]{1,0:T(8,128)S(1)} %add_add_fusion.1), channel_id=1, source_target_pairs={{0,8},{2,10},{4,12},{6,14},{8,0},{10,2},{12,4},{14,6},{16,24},{18,... | collective-permute-start | bytes 208904 | tf_op jit(solution)/shard_map/ppermute | solution.py:87
  30.2 1.8 %collective-permute-done.7 = f32[136,128]{1,0:T(8,128)S(1)} collective-permute-done((f32[136,128]{1,0:T(8,128)S(1)}, f32[136,128]{1,0:T(8,128)S(1)}, u32[]{:S(2)}, u32[]{:S(2)}) %collective-permute-start.7) | collective-permute-done | bytes 69664 | tf_op jit(solution)/shard_map/ppermute | solution.py:87
  32.0 1.4 %collective-permute-done.8 = f32[136,128]{1,0:T(8,128)S(1)} collective-permute-done((f32[136,128]{1,0:T(8,128)S(1)}, f32[136,128]{1,0:T(8,128)S(1)}, u32[]{:S(2)}, u32[]{:S(2)}) %collective-permute-start.8) | collective-permute-done | bytes 69664 | tf_op jit(solution)/shard_map/ppermute | solution.py:87
  33.4 1.8 %collective-permute-done.9 = f32[136,128]{1,0:T(8,128)S(1)} collective-permute-done((f32[136,128]{1,0:T(8,128)S(1)}, f32[136,128]{1,0:T(8,128)S(1)}, u32[]{:S(2)}, u32[]{:S(2)}) %collective-permute-start.9) | collective-permute-done | bytes 69664 | tf_op jit(solution)/shard_map/ppermute | solution.py:87
  36.6 9.8 %shard_map.68 = (f32[1040,128]{1,0:T(8,128)S(1)}, bf16[256,256]{1,0:T(8,128)(2,1)S(1)}, bf16[256,256]{1,0:T(8,128)(2,1)S(1)}, f32[8,256]{1,0:T(8,128)S(1)}) custom-call(s32[2]{0:T(128)S(1)} %copy-done.2, s32[48,8,128]{2,1,0:T(8,128)S(1)} %copy-done, s32[256,128]{1,0:T(8,128)S(1)} %copy-done.1, f32[136,128]{1,0:T(8,128)S(1)} %add_add_fusion.mine_ref, ...), custom_call_target="tpu_custom_call" | custom-call | tf_op jit(solution)/shard_map/pallas_call | solution.py:269
  46.4 1.7 %collective-permute-done.11.x_ref = f32[512,256]{1,0:T(8,128)S(1)} collective-permute-done((f32[512,256]{1,0:T(8,128)S(1)}, f32[512,256]{1,0:T(8,128)S(1)}, u32[]{:S(2)}, u32[]{:S(2)}) %collective-permute-start.11) | collective-permute-done | bytes 524320 | tf_op jit(solution)/shard_map/ppermute | solution.py:91
  48.1 5.6 %collective-permute-start.12 = (f32[1040,128]{1,0:T(8,128)S(1)}, f32[1040,128]{1,0:T(8,128)S(1)}, u32[]{:S(2)}, u32[]{:S(2)}) collective-permute-start(f32[1040,128]{1,0:T(8,128)S(1)} %get-tuple-element.15), channel_id=1, source_target_pairs={{0,1},{1,0},{2,3},{3,2},{4,5},{5,4},{6,7},{7,6},{8,9},{9,8},{10,11... | collective-permute-start | bytes 1597448 | tf_op jit(solution)/shard_map/ppermute | solution.py:91
  54.4 5.9 %shard_map.71 = f32[2304,128]{1,0:T(8,128)S(1)} custom-call(f32[4096,256]{1,0:T(8,128)} %x_ref.5, bf16[256,256]{1,0:T(8,128)(2,1)S(1)} %get-tuple-element.17.rot_ref), custom_call_target="tpu_custom_call" | custom-call | flops 452984832 | bytes 3538944 | tf_op jit(solution)/shard_map/pallas_call | solution.py:309
  61.9 5.9 %collective-permute-start.21 = (f32[256,128]{1,0:T(8,128)S(1)}, f32[256,128]{1,0:T(8,128)S(1)}, u32[]{:S(2)}, u32[]{:S(2)}) collective-permute-start(f32[256,128]{1,0:T(8,128)S(1)} %shard_map.72), channel_id=1, source_target_pairs={{0,1},{1,0},{2,3},{3,2},{4,5},{5,4},{6,7},{7,6},{8,9},{9,8},{10,11... | collective-permute-start | bytes 393224 | tf_op jit(solution)/shard_map/ppermute | solution.py:91
  67.8 7.2 %shard_map.69._ = f32[4096,256]{1,0:T(8,128)} custom-call(f32[4096,256]{1,0:T(8,128)} %x_ref.5, bf16[256,256]{1,0:T(8,128)(2,1)S(1)} %get-tuple-element.16.rot_ref), custom_call_target="tpu_custom_call" | custom-call | flops 805306368 | bytes 6291456 | tf_op jit(solution)/shard_map/pallas_call | solution.py:325
  75.0 29.6 %collective-permute-done.12 = f32[1040,128]{1,0:T(8,128)S(1)} collective-permute-done((f32[1040,128]{1,0:T(8,128)S(1)}, f32[1040,128]{1,0:T(8,128)S(1)}, u32[]{:S(2)}, u32[]{:S(2)}) %collective-permute-start.12) | collective-permute-done | bytes 532512 | tf_op jit(solution)/shard_map/ppermute | solution.py:91
  107.4 2.7 %collective-permute-start.15 = (f32[16,128]{1,0:T(8,128)S(1)}, f32[16,128]{1,0:T(8,128)S(1)}, u32[]{:S(2)}, u32[]{:S(2)}) collective-permute-start(f32[16,128]{1,0:T(8,128)S(1)} %pad_maximum_fusion), channel_id=1, source_target_pairs={{0,8},{2,10},{4,12},{6,14},{8,0},{10,2},{12,4},{14,6},{16,24},{18,... | collective-permute-start | bytes 24584 | tf_op jit(solution)/shard_map/ppermute | solution.py:87
  111.1 1.5 %collective-permute-done.15 = f32[16,128]{1,0:T(8,128)S(1)} collective-permute-done((f32[16,128]{1,0:T(8,128)S(1)}, f32[16,128]{1,0:T(8,128)S(1)}, u32[]{:S(2)}, u32[]{:S(2)}) %collective-permute-start.15) | collective-permute-done | bytes 8224 | tf_op jit(solution)/shard_map/ppermute | solution.py:87
  112.6 2.4 %collective-permute-done.16 = f32[16,128]{1,0:T(8,128)S(1)} collective-permute-done((f32[16,128]{1,0:T(8,128)S(1)}, f32[16,128]{1,0:T(8,128)S(1)}, u32[]{:S(2)}, u32[]{:S(2)}) %collective-permute-start.16) | collective-permute-done | bytes 8224 | tf_op jit(solution)/shard_map/ppermute | solution.py:87
  115.8 1.4 %collective-permute-start.18 = (f32[64,128]{1,0:T(8,128)S(1)}, f32[64,128]{1,0:T(8,128)S(1)}, u32[]{:S(2)}, u32[]{:S(2)}) collective-permute-start(f32[64,128]{1,0:T(8,128)S(1)} %constant_dynamic-update-slice_fusion.p0_ref), channel_id=1, source_target_pairs={{0,32},{2,34},{4,36},{6,38},{8,40},{10,42},{12,44},{14,46},{16,48}... | collective-permute-start | bytes 98312 | tf_op jit(solution)/shard_map/ppermute | solution.py:87
  117.2 2.6 %collective-permute-start.19 = (f32[64,128]{1,0:T(8,128)S(1)}, f32[64,128]{1,0:T(8,128)S(1)}, u32[]{:S(2)}, u32[]{:S(2)}) collective-permute-start(f32[64,128]{1,0:T(8,128)S(1)} %constant_dynamic-update-slice_fusion.p0_ref), channel_id=1, source_target_pairs={{0,48},{2,50},{4,52},{6,54},{8,56},{10,58},{12,60},{14,62},{16,32}... | collective-permute-start | bytes 98312 | tf_op jit(solution)/shard_map/ppermute | solution.py:87
  122.3 1.9 %shard_map.70 = f32[4096,256]{1,0:T(8,128)} custom-call(f32[512,256]{1,0:T(8,128)S(1)} %collective-permute-done.11.x_ref, f32[64,128]{1,0:T(8,128)S(1)} %constant_dynamic-update-slice_fusion.p0_ref, f32[64,128]{1,0:T(8,128)S(1)} %collective-permute-done.17.p1_ref, f32[64,128]{1,0:T(8,128)S(1)} %collective-permute-done.18.p2_ref, ...), custom_call_target="tpu_custom_call", output_to_operand_aliasing={{}: (5, {})} | custom-call | flops 100663296 | bytes 786432 | tf_op jit(solution)/shard_map/pallas_call | solution.py:357
  125.0 4.8 %collective-permute-done.20 = f32[2304,128]{1,0:T(8,128)S(1)} collective-permute-done((f32[2304,128]{1,0:T(8,128)S(1)}, f32[2304,128]{1,0:T(8,128)S(1)}, u32[]{:S(2)}, u32[]{:S(2)}) %collective-permute-start.20) | collective-permute-done | bytes 1179680 | tf_op jit(solution)/shard_map/ppermute | solution.py:91
  130.9 1.6 %collective-permute-done.21 = f32[256,128]{1,0:T(8,128)S(1)} collective-permute-done((f32[256,128]{1,0:T(8,128)S(1)}, f32[256,128]{1,0:T(8,128)S(1)}, u32[]{:S(2)}, u32[]{:S(2)}) %collective-permute-start.21) | collective-permute-done | bytes 131104 | tf_op jit(solution)/shard_map/ppermute | solution.py:91
  (53 shorter events, 20.6 us)
Async XLA Ops:
  0.6 36.0 %copy-start = (s32[48,8,128]{2,1,0:T(8,128)S(1)}, s32[48,8,128]{2,1,0:T(8,128)}, u32[]{:S(2)}) copy-start(s32[48,8,128]{2,1,0:T(8,128)} %constant.33.clone.table_ref) | copy-start | bytes 589828
  0.6 35.9 %copy-start.1 = (s32[256,128]{1,0:T(8,128)S(1)}, s32[256,128]{1,0:T(8,128)}, u32[]{:S(2)}) copy-start(s32[256,128]{1,0:T(8,128)} %constant.34.clone.last_ref) | copy-start | bytes 393220
  4.8 1.3 %collective-permute-start = (f32[136,128]{1,0:T(8,128)S(1)}, f32[136,128]{1,0:T(8,128)S(1)}, u32[]{:S(2)}, u32[]{:S(2)}) collective-permute-start(f32[136,128]{1,0:T(8,128)S(1)} %constant_dynamic-slice_fusion), channel_id=1, source_target_pairs={{0,2},{2,0},{4,6},{6,4},{8,10},{10,8},{12,14},{14,12},{16,18},{18,... | collective-permute-start | bytes 208904 | tf_op jit(solution)/shard_map/ppermute | solution.py:87
  6.2 6.9 %collective-permute-start.1 = (f32[136,128]{1,0:T(8,128)S(1)}, f32[136,128]{1,0:T(8,128)S(1)}, u32[]{:S(2)}, u32[]{:S(2)}) collective-permute-start(f32[136,128]{1,0:T(8,128)S(1)} %dynamic-slice_add_fusion), channel_id=1, source_target_pairs={{0,128},{2,130},{4,132},{6,134},{8,136},{10,138},{12,140},{14,142}... | collective-permute-start | bytes 208904 | tf_op jit(solution)/shard_map/ppermute | solution.py:87
  9.6 4.7 %collective-permute-start.2 = (f32[136,128]{1,0:T(8,128)S(1)}, f32[136,128]{1,0:T(8,128)S(1)}, u32[]{:S(2)}, u32[]{:S(2)}) collective-permute-start(f32[136,128]{1,0:T(8,128)S(1)} %dynamic-slice_add_fusion), channel_id=1, source_target_pairs={{0,64},{2,66},{4,68},{6,70},{8,72},{10,74},{12,76},{14,78},{16,80}... | collective-permute-start | bytes 208904 | tf_op jit(solution)/shard_map/ppermute | solution.py:87
  9.7 5.7 %collective-permute-start.3 = (f32[136,128]{1,0:T(8,128)S(1)}, f32[136,128]{1,0:T(8,128)S(1)}, u32[]{:S(2)}, u32[]{:S(2)}) collective-permute-start(f32[136,128]{1,0:T(8,128)S(1)} %dynamic-slice_add_fusion), channel_id=1, source_target_pairs={{0,192},{2,194},{4,196},{6,198},{8,200},{10,202},{12,204},{14,206}... | collective-permute-start | bytes 208904 | tf_op jit(solution)/shard_map/ppermute | solution.py:87
  15.4 10.6 %collective-permute-start.4 = (f32[136,128]{1,0:T(8,128)S(1)}, f32[136,128]{1,0:T(8,128)S(1)}, u32[]{:S(2)}, u32[]{:S(2)}) collective-permute-start(f32[136,128]{1,0:T(8,128)S(1)} %add_add_fusion.2), channel_id=1, source_target_pairs={{0,32},{2,34},{4,36},{6,38},{8,40},{10,42},{12,44},{14,46},{16,48}... | collective-permute-start | bytes 208904 | tf_op jit(solution)/shard_map/ppermute | solution.py:87
  16.7 9.3 %collective-permute-start.5 = (f32[136,128]{1,0:T(8,128)S(1)}, f32[136,128]{1,0:T(8,128)S(1)}, u32[]{:S(2)}, u32[]{:S(2)}) collective-permute-start(f32[136,128]{1,0:T(8,128)S(1)} %add_add_fusion.2), channel_id=1, source_target_pairs={{0,16},{2,18},{4,20},{6,22},{8,24},{10,26},{12,28},{14,30},{16,0},... | collective-permute-start | bytes 208904 | tf_op jit(solution)/shard_map/ppermute | solution.py:87
  16.7 9.2 %collective-permute-start.6 = (f32[136,128]{1,0:T(8,128)S(1)}, f32[136,128]{1,0:T(8,128)S(1)}, u32[]{:S(2)}, u32[]{:S(2)}) collective-permute-start(f32[136,128]{1,0:T(8,128)S(1)} %add_add_fusion.2), channel_id=1, source_target_pairs={{0,48},{2,50},{4,52},{6,54},{8,56},{10,58},{12,60},{14,62},{16,32}... | collective-permute-start | bytes 208904 | tf_op jit(solution)/shard_map/ppermute | solution.py:87
  19.6 28.5 %collective-permute-start.11 = (f32[512,256]{1,0:T(8,128)S(1)}, f32[512,256]{1,0:T(8,128)S(1)}, u32[]{:S(2)}, u32[]{:S(2)}) collective-permute-start(f32[512,256]{1,0:T(8,128)S(1)} %slice.23), channel_id=1, source_target_pairs={{0,1},{1,0},{2,3},{3,2},{4,5},{5,4},{6,7},{7,6},{8,9},{9,8},{10,11... | collective-permute-start | bytes 1572872 | tf_op jit(solution)/shard_map/ppermute | solution.py:91
  26.0 6.0 %collective-permute-start.7 = (f32[136,128]{1,0:T(8,128)S(1)}, f32[136,128]{1,0:T(8,128)S(1)}, u32[]{:S(2)}, u32[]{:S(2)}) collective-permute-start(f32[136,128]{1,0:T(8,128)S(1)} %add_add_fusion.1), channel_id=1, source_target_pairs={{0,8},{2,10},{4,12},{6,14},{8,0},{10,2},{12,4},{14,6},{16,24},{18,... | collective-permute-start | bytes 208904 | tf_op jit(solution)/shard_map/ppermute | solution.py:87
  29.1 4.3 %collective-permute-start.8 = (f32[136,128]{1,0:T(8,128)S(1)}, f32[136,128]{1,0:T(8,128)S(1)}, u32[]{:S(2)}, u32[]{:S(2)}) collective-permute-start(f32[136,128]{1,0:T(8,128)S(1)} %add_add_fusion.1), channel_id=1, source_target_pairs={{0,4},{2,6},{4,0},{6,2},{8,12},{10,14},{12,8},{14,10},{16,20},{18,... | collective-permute-start | bytes 208904 | tf_op jit(solution)/shard_map/ppermute | solution.py:87
  29.7 5.5 %collective-permute-start.9 = (f32[136,128]{1,0:T(8,128)S(1)}, f32[136,128]{1,0:T(8,128)S(1)}, u32[]{:S(2)}, u32[]{:S(2)}) collective-permute-start(f32[136,128]{1,0:T(8,128)S(1)} %add_add_fusion.1), channel_id=1, source_target_pairs={{0,12},{2,14},{4,8},{6,10},{8,4},{10,6},{12,0},{14,2},{16,28},{18,... | collective-permute-start | bytes 208904 | tf_op jit(solution)/shard_map/ppermute | solution.py:87
  35.2 1.3 %collective-permute-start.10 = (f32[136,128]{1,0:T(8,128)S(1)}, f32[136,128]{1,0:T(8,128)S(1)}, u32[]{:S(2)}, u32[]{:S(2)}) collective-permute-start(f32[136,128]{1,0:T(8,128)S(1)} %add_add_fusion.mine_ref), channel_id=1, source_target_pairs={{0,2},{2,0},{4,6},{6,4},{8,10},{10,8},{12,14},{14,12},{16,18},{18,... | collective-permute-start | bytes 208904 | tf_op jit(solution)/shard_map/ppermute | solution.py:87
  48.1 56.5 %collective-permute-start.12 = (f32[1040,128]{1,0:T(8,128)S(1)}, f32[1040,128]{1,0:T(8,128)S(1)}, u32[]{:S(2)}, u32[]{:S(2)}) collective-permute-start(f32[1040,128]{1,0:T(8,128)S(1)} %get-tuple-element.15), channel_id=1, source_target_pairs={{0,1},{1,0},{2,3},{3,2},{4,5},{5,4},{6,7},{7,6},{8,9},{9,8},{10,11... | collective-permute-start | bytes 1597448 | tf_op jit(solution)/shard_map/ppermute | solution.py:91
  60.3 69.5 %collective-permute-start.20 = (f32[2304,128]{1,0:T(8,128)S(1)}, f32[2304,128]{1,0:T(8,128)S(1)}, u32[]{:S(2)}, u32[]{:S(2)}) collective-permute-start(f32[2304,128]{1,0:T(8,128)S(1)} %shard_map.71), channel_id=1, source_target_pairs={{0,1},{1,0},{2,3},{3,2},{4,5},{5,4},{6,7},{7,6},{8,9},{9,8},{10,11... | collective-permute-start | bytes 3538952 | tf_op jit(solution)/shard_map/ppermute | solution.py:91
  61.9 70.6 %collective-permute-start.21 = (f32[256,128]{1,0:T(8,128)S(1)}, f32[256,128]{1,0:T(8,128)S(1)}, u32[]{:S(2)}, u32[]{:S(2)}) collective-permute-start(f32[256,128]{1,0:T(8,128)S(1)} %shard_map.72), channel_id=1, source_target_pairs={{0,1},{1,0},{2,3},{3,2},{4,5},{5,4},{6,7},{7,6},{8,9},{9,8},{10,11... | collective-permute-start | bytes 393224 | tf_op jit(solution)/shard_map/ppermute | solution.py:91
  104.5 1.8 %collective-permute-start.13 = (f32[8,128]{1,0:T(8,128)S(1)}, f32[8,128]{1,0:T(8,128)S(1)}, u32[]{:S(2)}, u32[]{:S(2)}) collective-permute-start(f32[8,128]{1,0:T(8,128)S(1)} %get-tuple-element.19), channel_id=1, source_target_pairs={{0,2},{2,0},{4,6},{6,4},{8,10},{10,8},{12,14},{14,12},{16,18},{18,... | collective-permute-start | bytes 12296 | tf_op jit(solution)/shard_map/ppermute | solution.py:87
  106.3 4.8 %collective-permute-start.14 = (f32[16,128]{1,0:T(8,128)S(1)}, f32[16,128]{1,0:T(8,128)S(1)}, u32[]{:S(2)}, u32[]{:S(2)}) collective-permute-start(f32[16,128]{1,0:T(8,128)S(1)} %pad_maximum_fusion), channel_id=1, source_target_pairs={{0,4},{2,6},{4,0},{6,2},{8,12},{10,14},{12,8},{14,10},{16,20},{18,... | collective-permute-start | bytes 24584 | tf_op jit(solution)/shard_map/ppermute | solution.py:87
  107.4 5.2 %collective-permute-start.15 = (f32[16,128]{1,0:T(8,128)S(1)}, f32[16,128]{1,0:T(8,128)S(1)}, u32[]{:S(2)}, u32[]{:S(2)}) collective-permute-start(f32[16,128]{1,0:T(8,128)S(1)} %pad_maximum_fusion), channel_id=1, source_target_pairs={{0,8},{2,10},{4,12},{6,14},{8,0},{10,2},{12,4},{14,6},{16,24},{18,... | collective-permute-start | bytes 24584 | tf_op jit(solution)/shard_map/ppermute | solution.py:87
  110.2 4.9 %collective-permute-start.16 = (f32[16,128]{1,0:T(8,128)S(1)}, f32[16,128]{1,0:T(8,128)S(1)}, u32[]{:S(2)}, u32[]{:S(2)}) collective-permute-start(f32[16,128]{1,0:T(8,128)S(1)} %pad_maximum_fusion), channel_id=1, source_target_pairs={{0,12},{2,14},{4,8},{6,10},{8,4},{10,6},{12,0},{14,2},{16,28},{18,... | collective-permute-start | bytes 24584 | tf_op jit(solution)/shard_map/ppermute | solution.py:87
  115.0 6.0 %collective-permute-start.17 = (f32[64,128]{1,0:T(8,128)S(1)}, f32[64,128]{1,0:T(8,128)S(1)}, u32[]{:S(2)}, u32[]{:S(2)}) collective-permute-start(f32[64,128]{1,0:T(8,128)S(1)} %constant_dynamic-update-slice_fusion.p0_ref), channel_id=1, source_target_pairs={{0,16},{2,18},{4,20},{6,22},{8,24},{10,26},{12,28},{14,30},{16,0},... | collective-permute-start | bytes 98312 | tf_op jit(solution)/shard_map/ppermute | solution.py:87
  115.8 5.4 %collective-permute-start.18 = (f32[64,128]{1,0:T(8,128)S(1)}, f32[64,128]{1,0:T(8,128)S(1)}, u32[]{:S(2)}, u32[]{:S(2)}) collective-permute-start(f32[64,128]{1,0:T(8,128)S(1)} %constant_dynamic-update-slice_fusion.p0_ref), channel_id=1, source_target_pairs={{0,32},{2,34},{4,36},{6,38},{8,40},{10,42},{12,44},{14,46},{16,48}... | collective-permute-start | bytes 98312 | tf_op jit(solution)/shard_map/ppermute | solution.py:87
  117.2 5.1 %collective-permute-start.19 = (f32[64,128]{1,0:T(8,128)S(1)}, f32[64,128]{1,0:T(8,128)S(1)}, u32[]{:S(2)}, u32[]{:S(2)}) collective-permute-start(f32[64,128]{1,0:T(8,128)S(1)} %constant_dynamic-update-slice_fusion.p0_ref), channel_id=1, source_target_pairs={{0,48},{2,50},{4,52},{6,54},{8,56},{10,58},{12,60},{14,62},{16,32}... | collective-permute-start | bytes 98312 | tf_op jit(solution)/shard_map/ppermute | solution.py:87
  (1 other events, 35.9 us)
